TPU v7x, 512 devices: a whole 4x8x8 slice. The times are simulated.
512 devices in a mesh: shard: 64 (over x, y_lo, z), dp: 8 (over y_hi, core).
Axes of the slice: x: 4, y: 8 (y_hi: 4, y_lo: 2; y = y_hi * 2 + y_lo), z: 8, core: 2. Of those that a mesh axis runs over, the one named last changes fastest.
Arguments:
- tokens: bfloat16 [1024, 8192], P('dp', 'shard'), may hold values from -6 to 6
- frozen_up_weight: bfloat16 [8192, 32768], P('dp', 'shard'), may hold values from -0.0625 to 0.0625
- adapter_down_factor: bfloat16 [8192, 256], P('shard'), may hold values from -0.0625 to 0.0625
- adapter_up_factor: bfloat16 [256, 32768], P(None, 'shard'), may hold values from -0.375 to 0.375
- cotangent: bfloat16 [1024, 32768], P('dp', 'shard'), may hold values from -0.59765625 to 0.59765625
- previous_task_directions: bfloat16 [8192, 1024], P('shard'), may hold values from -0.0625 to 0.0625
Outputs:
- projection_output: bfloat16 [1024, 32768], P('dp', 'shard')
- token_input_gradient: bfloat16 [1024, 8192], P('dp', 'shard')
- grad_down: float32 [8192, 256], P('shard')
- grad_up: float32 [256, 32768], P(None, 'shard')
All inputs are finite; a program needn't handle non-finite values.
Results may differ from a plain program's by a relative error of at most 0.005.
Values may be sent and summed in bfloat16 or wider, within the bound.
No kernel may reach another device: no remote copies, remote signals or barrier semaphores. Data moves between devices by JAX's collectives and lax.ppermute only.
A program may use at most 64 MiB of HBM per device.

v0:
```python
import jax
import jax.numpy as jnp
from jax import lax
from jax.sharding import PartitionSpec as P


def inner_first(left, right):
    return lax.dot_general(
        left, right, (((0,), (0,)), ((), ())), preferred_element_type=jnp.float32
    )


def final_inner_product(left, right):
    return lax.dot_general(
        left, right, (((1,), (1,)), ((), ())), preferred_element_type=jnp.float32
    )


def split_parts(wide):
    high = wide.astype(jnp.bfloat16)
    rest = (wide - high.astype(jnp.float32)).astype(jnp.bfloat16)
    return (high, rest)


def basis_inner(basis, wide):
    high, rest = split_parts(wide)
    return inner_first(basis, high) + inner_first(basis, rest)


def basis_apply(basis, wide):
    high, rest = split_parts(wide)
    return jnp.dot(basis, high, preferred_element_type=jnp.float32) + jnp.dot(
        basis, rest, preferred_element_type=jnp.float32
    )


def local(
    tokens,
    frozen_up_weight,
    adapter_down_factor,
    adapter_up_factor,
    cotangent,
    previous_task_directions,
):
    adapter_contribution = jnp.dot(tokens, adapter_down_factor, preferred_element_type=jnp.float32)
    lowrank_activation = lax.psum(adapter_contribution, "shard").astype(jnp.bfloat16)
    gathered = lax.all_gather(tokens, "shard", axis=1, tiled=True)
    panel_full = lax.all_gather(frozen_up_weight, "dp", axis=0, tiled=True)
    frozen_contribution = jnp.dot(gathered, panel_full, preferred_element_type=jnp.float32)
    projection_output = (
        frozen_contribution
        + jnp.dot(lowrank_activation, adapter_up_factor, preferred_element_type=jnp.float32)
    ).astype(jnp.bfloat16)
    backward_lowrank = lax.psum(final_inner_product(cotangent, adapter_up_factor), "shard").astype(
        jnp.bfloat16
    )
    combined_output = lax.psum_scatter(
        final_inner_product(panel_full, cotangent), "shard", scatter_dimension=0, tiled=True
    )
    token_input_gradient = (
        combined_output.T + final_inner_product(backward_lowrank, adapter_down_factor)
    ).astype(jnp.bfloat16)
    up_part = inner_first(lowrank_activation, cotangent)
    raw_part = inner_first(tokens, backward_lowrank)
    raw_grad, grad_up = lax.psum((raw_part, up_part), "dp")
    coefficients = lax.psum(basis_inner(previous_task_directions, raw_grad), "shard")
    grad_down = raw_grad - basis_apply(previous_task_directions, coefficients)
    return (projection_output, token_input_gradient, grad_down, grad_up)


def solution(mesh):
    placed = (
        P("dp", "shard"),
        P("dp", "shard"),
        P("shard", None),
        P(None, "shard"),
        P("dp", "shard"),
        P("shard", None),
    )
    return jax.shard_map(
        local,
        mesh=mesh,
        in_specs=placed,
        out_specs=(P("dp", "shard"), P("dp", "shard"), P("shard", None), P(None, "shard")),
        check_vma=False,
    )
```

profile of v0, /device:TPU:48, one launch (start us, length us, event | category | flops | bytes accessed | tf_op | source)
XLA Modules:
  0.0 1672.9 jit_solution(10114838166033490243)
XLA Ops:
  7.2 1.0 fusion.17
  8.3 1.2 fusion.19
  9.5 314.1 %all-reduce.9 = (bf16[128,256]{1,0:T(8,128)(2,1)S(1)}, bf16[128,256]{1,0:T(8,128)(2,1)S(1)}) all-reduce(f32[128,256]{1,0:T(8,128)S(1)} %fusion.17, f32[128,256]{1,0:T(8,128)S(1)} %fusion.19), channel_id=1, replica_groups=mesh['shard'=64,'dp'=8] {'shard'}, use_global_device_ids=true, to_apply=%region_0.0 | all-reduce | flops 65536 | bytes 393216 | tf_op jit(solution)/shard_map/psum | solution.py:46
  323.7 1.6 convolution_bitcast_fusion
  325.3 1.9 fusion.20
  327.3 0.0 all-gather.5.cloned.1.call-start
  327.3 0.7 all-gather.5.cloned.1.call-update
  328.1 69.5 %all-reduce.8.cloned.1.call-done = (f32[128,256]{0,1:T(8,128)}, f32[256,512]{1,0:T(8,128)}) async-done(((f32[128,256]{0,1:T(8,128)}, f32[256,512]{1,0:T(8,128)}), (f32[128,256]{0,1:T(8,128)}, f32[256,512]{1,0:T(8,128)})) %all-reduce.8.cloned.1.call-update) | async-done | bytes 655376 | tf_op jit(solution)/shard_map/psum | solution.py:65
  397.6 1.2 fusion.9
  398.7 2.2 fusion
  401.1 0.5 all-gather.3.cloned.1.call-update
  401.6 88.8 %all-gather.5.cloned.1.call-done = bf16[8192,512]{1,0:T(8,128)(2,1)} async-done(((bf16[1024,512]{1,0:T(8,128)(2,1)}), bf16[8192,512]{1,0:T(8,128)(2,1)}) %all-gather.5.cloned.1.call-update) | async-done | bytes 8388624 | tf_op jit(solution)/shard_map/all_gather | solution.py:48
  490.5 7.7 fusion.18
  498.2 605.0 %all-reduce.6.cloned.1.call-done = f32[1024,256]{0,1:T(8,128)} async-done(((f32[1024,256]{0,1:T(8,128)}), f32[1024,256]{0,1:T(8,128)}) %all-reduce.6.cloned.1.call-update) | async-done | bytes 1048592 | tf_op jit(solution)/shard_map/psum | solution.py:66
  1103.2 1.5 fusion.6
  1104.7 1.8 fusion.3
  1106.6 0.8 copy.12
  1107.4 231.5 %all-gather.3.cloned.1.call-done = bf16[128,8192]{1,0:T(8,128)(2,1)} async-done(((bf16[128,128]{1,0:T(8,128)(2,1)}), bf16[128,8192]{1,0:T(8,128)(2,1)}) %all-gather.3.cloned.1.call-update) | async-done | bytes 2097168 | tf_op jit(solution)/shard_map/all_gather | solution.py:47
  1338.9 5.3 fusion.16
  1344.2 0.8 fusion.1
  1345.0 318.8 %reduce-scatter.2.cloned.1.call-done = f32[128,128]{1,0:T(8,128)} async-done(((f32[8192,128]{1,0:T(8,128)}), f32[128,128]{1,0:T(8,128)}) %reduce-scatter.2.cloned.1.call-update) | async-done | bytes 65552 | tf_op jit(solution)/shard_map/reduce_scatter | solution.py:57
  1663.8 1.0 fusion.4
  1664.8 0.7 copy.11
  1665.6 0.8 copy.21
  (19 shorter events, 0.2 us)
Async XLA Ops:
  7.2 390.4 %copy-start = (bf16[128,1024]{1,0:T(8,128)(2,1)S(1)}, bf16[128,1024]{1,0:T(8,128)(2,1)}, u32[]{:S(2)}) copy-start(bf16[128,1024]{1,0:T(8,128)(2,1)} %param.11) | copy-start | bytes 786436
  7.2 483.3 %copy-start.1 = (bf16[128,512]{1,0:T(8,128)(2,1)S(1)}, bf16[128,512]{1,0:T(8,128)(2,1)}, u32[]{:S(2)}) copy-start(bf16[128,512]{1,0:T(8,128)(2,1)} %param.10) | copy-start | bytes 393220
  7.2 390.4 %all-reduce.8.cloned.1.call-start = ((), (), s32[]{:S(2)}) async-start(), calls=%async_computation.5 | async-start | bytes 1310720 | tf_op jit(solution)/shard_map/psum | solution.py:65
  327.3 163.2 %all-gather.5.cloned.1.call-start = ((), (), s32[]{:S(2)}) async-start(), calls=%async_computation.2 | async-start | bytes 9437184 | tf_op jit(solution)/shard_map/all_gather | solution.py:48
  328.0 775.2 %all-reduce.6.cloned.1.call-start = ((), (), s32[]{:S(2)}) async-start(), calls=%async_computation.4 | async-start | bytes 2097152 | tf_op jit(solution)/shard_map/psum | solution.py:66
  401.0 937.9 %all-gather.3.cloned.1.call-start = ((), (), s32[]{:S(2)}) async-start(), calls=%async_computation.1 | async-start | bytes 2129920 | tf_op jit(solution)/shard_map/all_gather | solution.py:47
  401.6 703.1 %copy-start.2 = (f32[128,256]{0,1:T(8,128)S(1)}, f32[128,256]{0,1:T(8,128)}, u32[]{:S(2)}) copy-start(f32[128,256]{0,1:T(8,128)} %get-tuple-element.10) | copy-start | bytes 393220
  401.6 1262.2 %reduce-scatter.2.cloned.1.call-start = ((), (), s32[]{:S(2)}) async-start(), calls=%async_computation.3 | async-start | bytes 4259840 | tf_op jit(solution)/shard_map/reduce_scatter | solution.py:57
  1107.3 236.8 %copy-start.3 = (bf16[256,512]{1,0:T(8,128)(2,1)S(1)}, bf16[256,512]{1,0:T(8,128)(2,1)}, u32[]{:S(2)}) copy-start(bf16[256,512]{1,0:T(8,128)(2,1)} %param.9) | copy-start | bytes 786436
  1107.3 556.5 %copy-start.5 = (bf16[128,256]{1,0:T(8,128)(2,1)S(1)}, bf16[128,256]{1,0:T(8,128)(2,1)}, u32[]{:S(2)}) copy-start(bf16[128,256]{1,0:T(8,128)(2,1)} %param.8) | copy-start | bytes 196612
  1107.4 558.2 %copy-start.4 = (f32[256,512]{1,0:T(8,128)S(1)}, f32[256,512]{1,0:T(8,128)}, u32[]{:S(2)}) copy-start(f32[256,512]{1,0:T(8,128)} %get-tuple-element.15) | copy-start | bytes 1572868
Sparse Core Ops, SparseCore 0:
  327.4 70.1 all-reduce.7
  399.7 90.7 all-gather.4
  493.4 609.7 all-reduce.5
  1105.2 233.5 all-gather.2
  1341.8 322.0 reduce-scatter.1
where the time goes:
time: 1670 us
  waiting for transfers between devices  1310 us (78%)
  blocking collectives  314 us (19%)
  matrix products  27.4 us (2%)
    psum x1, waiting for transfers between devices, local(): lax.psum(basis_inner(previous_task_directions, raw_grad), 'shard')  605 us
    reduce_scatter x1, waiting for transfers between devices, local(): lax.psum_scatter(final_inner_product(panel_full, cotangent), 'shard', sca...  319 us
    psum x1, blocking collectives, local(): lax.psum(adapter_contribution, 'shard').astype(jnp.bfloat16)  314 us
    all_gather x1, waiting for transfers between devices, local(): gathered = lax.all_gather(tokens, 'shard', axis=1, tiled=True)  232 us
    all_gather x1, waiting for transfers between devices, local(): panel_full = lax.all_gather(frozen_up_weight, 'dp', axis=0, tiled=True)  88.8 us
    psum x1, waiting for transfers between devices, local(): raw_grad, grad_up = lax.psum((raw_part, up_part), 'dp')  69.5 us
  transfers between devices with their start and end apart: 5, of which 5 were waited for; matrix products, arithmetic and copies ran while one was open for 1% of the time, Pallas kernels for 0%

commit v1 on v0

v1 whole, which is shorter than its diff:
```python
import jax
import jax.numpy as jnp
from jax import lax
from jax.sharding import PartitionSpec as P

F32 = jnp.float32
BF16 = jnp.bfloat16


def dot(left, right, contract):
    return lax.dot_general(left, right, ((contract[0], contract[1]), ((), ())), preferred_element_type=F32)


def exchange(pieces, axis):
    return lax.all_to_all(pieces, axis, split_axis=0, concat_axis=0, tiled=True)


def to_all(block, count):
    return jnp.broadcast_to(block[None], (count, *block.shape))


def local(tokens, weight, down, up, cotangent, directions):
    shards = lax.axis_size("shard")
    groups = lax.axis_size("dp")
    batch, block = tokens.shape
    rank = down.shape[1]
    past = directions.shape[1]

    weight_full = lax.all_gather(weight, "dp", axis=0, tiled=True)

    share = jnp.concatenate(
        [
            dot(down, tokens, ((0,), (1,))),
            dot(directions, tokens, ((0,), (1,))),
            dot(up, cotangent, ((1,), (1,))),
        ],
        axis=0,
    ).astype(BF16)
    rows = share.shape[0] // shards
    first = exchange(
        jnp.concatenate([to_all(tokens, shards), share.reshape(shards, rows, batch)], axis=1), "shard"
    )
    tokens_full = first[:, :batch]
    summed = jnp.sum(first[:, batch:].astype(F32), axis=0).astype(BF16)

    partial_gradient = dot(weight_full, cotangent, ((1,), (1,))).astype(BF16)
    second = exchange(
        jnp.concatenate(
            [partial_gradient.reshape(shards, block, batch), to_all(summed, shards)], axis=1
        ),
        "shard",
    )
    gradient = jnp.sum(second[:, :block].astype(F32), axis=0)
    whole = second[:, block:].reshape(shards * rows, batch)
    low, along, back_low = whole[:rank], whole[rank : rank + past], whole[rank + past :]

    frozen = dot(tokens_full.transpose(1, 0, 2).reshape(batch, shards * block), weight_full, ((1,), (0,)))
    projection_output = (frozen + dot(low, up, ((0,), (0,)))).astype(BF16)
    token_input_gradient = (gradient + dot(down, back_low, ((1,), (0,)))).T.astype(BF16)

    up_part = dot(cotangent, low, ((0,), (1,)))
    kept = tokens.astype(F32).T - dot(directions, along, ((1,), (0,)))
    kept_high = kept.astype(BF16)
    kept_rest = (kept - kept_high.astype(F32)).astype(BF16)
    down_part = dot(kept_high, back_low, ((1,), (1,))) + dot(kept_rest, back_low, ((1,), (1,)))
    up_rows, down_rows = up_part.shape[0] // groups, block // groups
    third = exchange(
        jnp.concatenate(
            [up_part.reshape(groups, up_rows, rank), down_part.reshape(groups, down_rows, rank)], axis=1
        ).astype(BF16),
        "dp",
    )
    mine = jnp.sum(third.astype(F32), axis=0).astype(BF16)
    fourth = exchange(to_all(mine, groups), "dp").astype(F32)
    grad_up = fourth[:, :up_rows].reshape(groups * up_rows, rank).T
    grad_down = fourth[:, up_rows:].reshape(block, rank)
    return projection_output, token_input_gradient, grad_down, grad_up


def solution(mesh):
    placed = (
        P("dp", "shard"),
        P("dp", "shard"),
        P("shard", None),
        P(None, "shard"),
        P("dp", "shard"),
        P("shard", None),
    )
    return jax.shard_map(
        local,
        mesh=mesh,
        in_specs=placed,
        out_specs=(P("dp", "shard"), P("dp", "shard"), P("shard", None), P(None, "shard")),
        check_vma=False,
    )
```

time: 1670 us -> 251 us (0.15)
  the two profiles are of different devices: /device:TPU:48 before, /device:TPU:1 now
where the time goes in v1:
time: 251 us; the launch traced here: 250 us
  blocking collectives  92.9 us (37%)
  waiting for transfers between devices  89.8 us (36%)
  starting transfers between devices  23.5 us (9%)
  matrix products  16.2 us (6%)
  between operations  14.2 us (6%)
  local copies, waits for them, and re-layouts  9.1 us (4%)
  other arithmetic  4.77 us (2%)
    all_to_all x1, blocking collectives, exchange(): return lax.all_to_all(pieces, axis, split_axis=0, concat_axis=0, tiled=True)  92.9 us
    all_to_all x3, waiting for transfers between devices, exchange(): return lax.all_to_all(pieces, axis, split_axis=0, concat_axis=0, tiled=True)  66.3 us
    all_to_all x3, starting transfers between devices, exchange(): return lax.all_to_all(pieces, axis, split_axis=0, concat_axis=0, tiled=True)  23.5 us
    all_gather x1, waiting for transfers between devices, local(): weight_full = lax.all_gather(weight, 'dp', axis=0, tiled=True)  22.8 us
    dot_general x11, matrix products, dot(): lax.dot_general(left, right, ((contract[0], contract[1]), ((), ())), pref...  16.2 us
  transfers between devices with their start and end apart: 4, of which 4 were waited for; matrix products, arithmetic and copies ran while one was open for 7% of the time, Pallas kernels for 0%

profile of v1, /device:TPU:1, one launch (start us, length us, event | category | flops | bytes accessed | tf_op | source)
XLA Modules:
  0.0 250.4 jit_solution(7670436475327465896)
XLA Ops:
  7.2 0.7 all-gather.2.cloned.1.call-update
  7.9 1.0 convolution_convert_fusion.4
  9.0 1.2 convolution_convert_fusion.3
  10.2 1.0 convolution_convert_fusion.2
  12.0 92.9 %all_to_all.20 = bf16[64,152,128]{2,1,0:T(8,128)(2,1)S(1)} all-to-all(bf16[64,152,128]{2,1,0:T(8,128)(2,1)S(1)} %pad_maximum_fusion), channel_id=1, replica_groups=mesh['shard'=64,'dp'=8] {'shard'}, dimensions={0} | all-to-all | bytes 4980736 | tf_op jit(solution)/shard_map/all_to_all | solution.py:15
  104.9 22.8 %all-gather.2.cloned.1.call-done = bf16[8192,512]{1,0:T(8,128)(2,1)} async-done(((bf16[1024,512]{1,0:T(8,128)(2,1)}), bf16[8192,512]{1,0:T(8,128)(2,1)}) %all-gather.2.cloned.1.call-update) | async-done | bytes 8388624 | tf_op jit(solution)/shard_map/all_gather | solution.py:29
  127.7 5.7 %convolution_convert_fusion = bf16[8192,128]{1,0:T(8,128)(2,1)S(1)} fusion(bf16[8192,512]{1,0:T(8,128)(2,1)} %all-gather.2.cloned.1.call-done, bf16[128,512]{1,0:T(8,128)(2,1)S(1)} %copy-done.1), kind=kOutput, calls=%fused_computation | convolution fusion | flops 1074790400 | bytes 10616832 | tf_op jit(solution)/shard_map/dot_general | solution.py:11
  133.5 1.7 pad_maximum_fusion.1
  135.3 10.2 %all-to-all-start.1 = ((bf16[64,152,128]{2,1,0:T(8,128)(2,1)}), bf16[64,152,128]{2,1,0:T(8,128)(2,1)}, u32[]{:S(2)}, u32[]{:S(2)}) async-start(bf16[64,152,128]{2,1,0:T(8,128)(2,1)} %pad_maximum_fusion.1), calls=%async_computation.1 | async-start | bytes 4980736 | tf_op jit(solution)/shard_map/all_to_all | solution.py:15
  145.5 1.6 slice.36
  147.1 3.2 %copy.23 = bf16[64,128,128]{1,2,0:T(8,128)(2,1)S(1)} copy(bf16[64,128,128]{2,1,0:T(8,128)(2,1)} %slice.36) | data formatting | bytes 4194304
  150.3 51.9 %all-to-all-done.1 = bf16[64,152,128]{2,1,0:T(8,128)(2,1)} async-done(((bf16[64,152,128]{2,1,0:T(8,128)(2,1)}), bf16[64,152,128]{2,1,0:T(8,128)(2,1)}, u32[]{:S(2)}, u32[]{:S(2)}) %all-to-all-start.1) | async-done | bytes 2490400 | tf_op jit(solution)/shard_map/all_to_all | solution.py:15
  202.1 1.0 slice.38
  204.2 0.7 pad_maximum_fusion.3
  205.0 6.7 %all-to-all-start.2 = ((bf16[8,80,256]{2,1,0:T(8,128)(2,1)}), bf16[8,80,256]{2,1,0:T(8,128)(2,1)S(1)}, u32[]{:S(2)}, u32[]{:S(2)}) async-start(bf16[8,80,256]{2,1,0:T(8,128)(2,1)} %pad_maximum_fusion.3), calls=%async_computation.2 | async-start | bytes 655360 | tf_op jit(solution)/shard_map/all_to_all | solution.py:15
  211.7 4.7 %fusion.14 = f32[128,512]{1,0:T(8,128)S(1)} fusion(bf16[128,8192]{0,1:T(8,128)(2,1)S(1)} %bitcast.32, bf16[8192,512]{1,0:T(8,128)(2,1)} %all-gather.2.cloned.1.call-done), kind=kOutput, calls=%fused_computation.30 | convolution fusion | flops 1073741824 | bytes 10747904 | tf_op jit(solution)/shard_map/dot_general | solution.py:11
  216.4 6.1 %all-to-all-done.2 = bf16[8,80,256]{2,1,0:T(8,128)(2,1)S(1)} async-done(((bf16[8,80,256]{2,1,0:T(8,128)(2,1)}), bf16[8,80,256]{2,1,0:T(8,128)(2,1)S(1)}, u32[]{:S(2)}, u32[]{:S(2)}) %all-to-all-start.2) | async-done | bytes 327712 | tf_op jit(solution)/shard_map/all_to_all | solution.py:15
  222.6 0.7 broadcast_in_dim.8
  223.3 6.6 %all-to-all-start.3 = ((bf16[8,80,256]{2,1,0:T(8,128)(2,1)}), bf16[8,80,256]{2,1,0:T(8,128)(2,1)S(1)}, u32[]{:S(2)}, u32[]{:S(2)}) async-start(bf16[8,80,256]{2,1,0:T(8,128)(2,1)} %broadcast_in_dim.8), calls=%async_computation.3 | async-start | bytes 655360 | tf_op jit(solution)/shard_map/all_to_all | solution.py:15
  229.9 1.9 convert_reduce_fusion
  231.9 0.8 fusion.4
  232.7 0.9 fusion.1
  233.6 8.3 %all-to-all-done.3 = bf16[8,80,256]{2,1,0:T(8,128)(2,1)S(1)} async-done(((bf16[8,80,256]{2,1,0:T(8,128)(2,1)}), bf16[8,80,256]{2,1,0:T(8,128)(2,1)S(1)}, u32[]{:S(2)}, u32[]{:S(2)}) %all-to-all-start.3) | async-done | bytes 327712 | tf_op jit(solution)/shard_map/all_to_all | solution.py:15
  241.9 1.0 copy.21
  (25 shorter events, 2.8 us)
Async XLA Ops:
  7.2 3.0 %copy-start = (bf16[128,1024]{1,0:T(8,128)(2,1)S(1)}, bf16[128,1024]{1,0:T(8,128)(2,1)}, u32[]{:S(2)}) copy-start(bf16[128,1024]{1,0:T(8,128)(2,1)} %param.11) | copy-start | bytes 786436
  7.2 4.1 %copy-start.3 = (bf16[128,128]{1,0:T(8,128)(2,1)S(1)}, bf16[128,128]{1,0:T(8,128)(2,1)}, u32[]{:S(2)}) copy-start(bf16[128,128]{1,0:T(8,128)(2,1)} %param.6) | copy-start | bytes 98308
  7.2 120.5 %all-gather.2.cloned.1.call-start = ((), (), s32[]{:S(2)}) async-start(), calls=%async_computation.4 | async-start | bytes 9437184 | tf_op jit(solution)/shard_map/all_gather | solution.py:29
  12.0 115.8 %copy-start.1 = (bf16[128,512]{1,0:T(8,128)(2,1)S(1)}, bf16[128,512]{1,0:T(8,128)(2,1)}, u32[]{:S(2)}) copy-start(bf16[128,512]{1,0:T(8,128)(2,1)} %param.10) | copy-start | bytes 393220
  135.3 66.9 %all-to-all-start.1 = ((bf16[64,152,128]{2,1,0:T(8,128)(2,1)}), bf16[64,152,128]{2,1,0:T(8,128)(2,1)}, u32[]{:S(2)}, u32[]{:S(2)}) async-start(bf16[64,152,128]{2,1,0:T(8,128)(2,1)} %pad_maximum_fusion.1), calls=%async_computation.1 | async-start | bytes 4980736 | tf_op jit(solution)/shard_map/all_to_all | solution.py:15
  205.0 17.5 %all-to-all-start.2 = ((bf16[8,80,256]{2,1,0:T(8,128)(2,1)}), bf16[8,80,256]{2,1,0:T(8,128)(2,1)S(1)}, u32[]{:S(2)}, u32[]{:S(2)}) async-start(bf16[8,80,256]{2,1,0:T(8,128)(2,1)} %pad_maximum_fusion.3), calls=%async_computation.2 | async-start | bytes 655360 | tf_op jit(solution)/shard_map/all_to_all | solution.py:15
  216.4 15.5 %copy-start.4 = (bf16[128,256]{1,0:T(8,128)(2,1)S(1)}, bf16[128,256]{1,0:T(8,128)(2,1)}, u32[]{:S(2)}) copy-start(bf16[128,256]{1,0:T(8,128)(2,1)} %param.8) | copy-start | bytes 196612
  216.4 16.3 %copy-start.2 = (bf16[256,512]{1,0:T(8,128)(2,1)S(1)}, bf16[256,512]{1,0:T(8,128)(2,1)}, u32[]{:S(2)}) copy-start(bf16[256,512]{1,0:T(8,128)(2,1)} %param.9) | copy-start | bytes 786436
  223.3 18.6 %all-to-all-start.3 = ((bf16[8,80,256]{2,1,0:T(8,128)(2,1)}), bf16[8,80,256]{2,1,0:T(8,128)(2,1)S(1)}, u32[]{:S(2)}, u32[]{:S(2)}) async-start(bf16[8,80,256]{2,1,0:T(8,128)(2,1)} %broadcast_in_dim.8), calls=%async_computation.3 | async-start | bytes 655360 | tf_op jit(solution)/shard_map/all_to_all | solution.py:15
Sparse Core Ops, SparseCore 0:
  10.2 117.4 all-gather.1

commit v2 on v1

v2 whole, which is shorter than its diff:
```python
import jax
import jax.numpy as jnp
from jax import lax
from jax.sharding import Mesh
from jax.sharding import PartitionSpec as P

F32 = jnp.float32
BF16 = jnp.bfloat16
AXES = ("x", "ylo", "z", "yhi", "core")
SIZES = (4, 2, 8, 4, 2)
SHARD = ("x", "ylo", "z")
DP = ("yhi", "core")
THERE = [
    ((x * 2 + l) * 4 + h, ((2 * (h // 2) + l) * 2 + h % 2) * 4 + x)
    for x in range(4)
    for l in range(2)
    for h in range(4)
]
BACK = [(b, a) for a, b in THERE]
HOME = [
    [(l * 4 + h, ((h ^ j) % 2) * 4 + (h ^ j) // 2 * 2 + l) for l in range(2) for h in range(4)] for j in range(4)
]


SPREAD = [
    [(l * 4 + h, (h % 2) * 4 + ((h // 2 * 2 + l) ^ j)) for l in range(2) for h in range(4)] for j in range(4)
]


def dot(left, right, contract):
    return lax.dot_general(left, right, ((contract[0], contract[1]), ((), ())), preferred_element_type=F32)


def exchange(pieces, axes):
    return lax.all_to_all(pieces, axes, split_axis=0, concat_axis=0, tiled=True)


def to_all(block, axes):
    return jnp.broadcast_to(block[None], (lax.axis_size(axes), *block.shape))


def add_up(pieces):
    return jnp.sum(pieces.astype(F32), axis=0)


def trade(block, axis):
    return lax.ppermute(block, axis, [(0, 1), (1, 0)])


def local(tokens, weight, down, up, cotangent, directions):
    n_z = lax.axis_size("z")
    batch, block = tokens.shape
    rank = down.shape[1]
    past = directions.shape[1]
    depth, hidden = weight.shape

    weights = lax.all_gather(weight, ("ylo", "core"), axis=0, tiled=True).reshape(2, 2 * depth, hidden)
    moved = lax.ppermute(tokens, ("x", "ylo", "yhi"), THERE)
    high = lax.axis_index("yhi")
    arrived = jnp.stack([lax.ppermute(cotangent, ("ylo", "yhi"), SPREAD[j]) for j in range(4)])
    cotangents = [lax.dynamic_index_in_dim(arrived, high ^ p, 0, keepdims=False) for p in range(4)]

    share = jnp.concatenate(
        [
            dot(down, tokens, ((0,), (1,))),
            dot(directions, tokens, ((0,), (1,))),
            dot(up, cotangent, ((1,), (1,))),
        ],
        axis=0,
    ).astype(BF16)
    first = exchange(
        jnp.concatenate([to_all(moved, ("x", "z")), share.reshape(4 * n_z, -1, batch)], axis=1), ("x", "z")
    )
    summed = add_up(first[:, batch:])
    summed = (summed + trade(summed, "ylo")).astype(BF16)
    later, summed = lax.optimization_barrier((cotangent, summed))
    cotangent_column = lax.all_gather(later, DP, axis=0, tiled=True)

    panel = first[:, :batch].reshape(2, 2 * n_z, batch, block).transpose(0, 2, 1, 3)
    panel = panel.reshape(2 * batch, 2 * n_z * block)
    frozen = [dot(panel, weights[i], ((1,), (0,))).astype(BF16).reshape(2, batch, hidden) for i in range(2)]
    frozen = jnp.stack(frozen, axis=1).reshape(4, batch, hidden)
    frozen = sum(
        lax.ppermute(
            lax.dynamic_index_in_dim(frozen, lax.axis_index("yhi") ^ j, 0, keepdims=False), ("ylo", "yhi"), HOME[j]
        ).astype(F32)
        for j in range(4)
    )

    slabs = [
        (
            dot(weights[0], cotangents[2 * i], ((1,), (1,))) + dot(weights[1], cotangents[2 * i + 1], ((1,), (1,)))
        ).astype(BF16)
        for i in range(2)
    ]
    slabs = jnp.concatenate(slabs).reshape(4 * n_z, block, batch)
    second = exchange(jnp.concatenate([slabs, to_all(summed, ("x", "z"))], axis=1), ("x", "z"))
    second, frozen = lax.optimization_barrier((second, frozen))
    gradient = lax.ppermute(add_up(second[:, :block]), ("x", "ylo", "yhi"), BACK)
    whole = second[:, block:].reshape(share.shape)
    low, along, back_low = whole[:rank], whole[rank : rank + past], whole[rank + past :]

    projection_output = (frozen + dot(low, up, ((0,), (0,)))).astype(BF16)
    token_input_gradient = (gradient + dot(down, back_low, ((1,), (0,)))).T.astype(BF16)

    kept = tokens.astype(F32).T - dot(directions, along, ((1,), (0,)))
    kept_high = kept.astype(BF16)
    kept_rest = (kept - kept_high.astype(F32)).astype(BF16)
    down_part = dot(back_low, kept_high, ((1,), (1,))) + dot(back_low, kept_rest, ((1,), (1,)))
    pair = exchange(to_all(jnp.concatenate([low, down_part.astype(BF16)], axis=0), "yhi"), "yhi")
    lows = pair[:, :rank]
    down_sum = add_up(pair[:, rank:])
    lows_beside, down_beside = trade(lows, "core"), trade(down_sum, "core")
    grad_down = (down_sum + down_beside).T
    first_core = lax.axis_index("core") == 0
    both = jnp.stack([jnp.where(first_core, lows, lows_beside), jnp.where(first_core, lows_beside, lows)], axis=1)
    low_column = both.transpose(2, 0, 1, 3).reshape(rank, 8 * batch)
    grad_up = dot(low_column, cotangent_column, ((1,), (0,)))
    return projection_output, token_input_gradient, grad_down, grad_up


def solution(mesh):
    fine = Mesh(mesh.devices.reshape(SIZES), AXES)
    placed = (P(DP, SHARD), P(DP, SHARD), P(SHARD, None), P(None, SHARD), P(DP, SHARD), P(SHARD, None))
    return jax.shard_map(
        local,
        mesh=fine,
        in_specs=placed,
        out_specs=(P(DP, SHARD), P(DP, SHARD), P(SHARD, None), P(None, SHARD)),
        check_vma=False,
    )
```

time: 251 us -> 181 us (0.72)
  blocking collectives: 92.9 us -> 0 us
  starting transfers between devices: 23.5 us -> 74.1 us
  waiting for transfers between devices: 89.8 us -> 63.7 us
  local copies, waits for them, and re-layouts: 9.1 us -> 4.93 us
    all_to_all x1 -> x0, blocking collectives: 92.9 us -> none  [exchange(): return lax.all_to_all(pieces, axis, split_axis=0, concat_axis=0, tiled=True)]
    ppermute x0 -> x13, starting transfers between devices: none -> 38.1 us  [the longest x4 14.2 us: local(): lax.ppermute(lax.dynamic_index_in_dim(frozen, lax.axis_index('yhi') ^ j,...]
    all_to_all x3, waiting for transfers between devices: 66.3 us -> 44.2 us  [exchange(): return lax.all_to_all(pieces, axes, split_axis=0, concat_axis=0, tiled=True)]
    all_gather x1 -> x2, waiting for transfers between devices: 22.8 us -> 5.77 us  [the longest x1 5.74 us: local(): lax.all_gather(weight, ('ylo', 'core'), axis=0, tiled=True)]
    ppermute x0 -> x13, waiting for transfers between devices: none -> 13.1 us  [the longest x4 9.87 us: local(): lax.ppermute(lax.dynamic_index_in_dim(frozen, lax.axis_index('yhi') ^ j,...]
    all_to_all x3, starting transfers between devices: 23.5 us -> 36 us  [exchange(): return lax.all_to_all(pieces, axes, split_axis=0, concat_axis=0, tiled=True)]
    slice x4, local copies, waits for them, and re-layouts: 3.34 us -> 0.17 us  [the longest x1 0.12 us: local(): first[:, :batch].reshape(2, 2 * n_z, batch, block).transpose(0, 2, 1, 3)]
    unnamed x12 -> x14, local copies, waits for them, and re-layouts: 4.25 us -> 1.4 us
  transfers between devices with their start and end apart: 4 -> 18, of which waited for: 4 -> 7; matrix products, arithmetic and copies ran while one was open for 7% -> 6% of each run, Pallas kernels for 0% -> 0%
where the time goes in v2:
time: 181 us; the launch traced here: 180 us
  starting transfers between devices  74.1 us (41%)
  waiting for transfers between devices  63.7 us (35%)
  between operations  16 us (9%)
  matrix products  15.3 us (8%)
  other arithmetic  5.79 us (3%)
  local copies, waits for them, and re-layouts  4.93 us (3%)
    all_to_all x3, waiting for transfers between devices, exchange(): return lax.all_to_all(pieces, axes, split_axis=0, concat_axis=0, tiled=True)  44.2 us
    all_to_all x3, starting transfers between devices, exchange(): return lax.all_to_all(pieces, axes, split_axis=0, concat_axis=0, tiled=True)  36 us
    dot_general x15, matrix products, dot(): lax.dot_general(left, right, ((contract[0], contract[1]), ((), ())), pref...  15.3 us
    ppermute x4, starting transfers between devices, local(): lax.ppermute(lax.dynamic_index_in_dim(frozen, lax.axis_index('yhi') ^ j,...  14.2 us
    ppermute x4, starting transfers between devices, local(): lax.ppermute(cotangent, ('ylo', 'yhi'), SPREAD[j])  12.1 us
    ppermute x4, waiting for transfers between devices, local(): lax.ppermute(lax.dynamic_index_in_dim(frozen, lax.axis_index('yhi') ^ j,...  9.87 us
    ppermute x3, starting transfers between devices, trade(): return lax.ppermute(block, axis, [(0, 1), (1, 0)])  9.71 us
    all_gather x1, waiting for transfers between devices, local(): lax.all_gather(weight, ('ylo', 'core'), axis=0, tiled=True)  5.74 us
  transfers between devices with their start and end apart: 18, of which 7 were waited for; matrix products, arithmetic and copies ran while one was open for 6% of the time, Pallas kernels for 0%

profile of v2, /device:TPU:1, one launch (start us, length us, event | category | flops | bytes accessed | tf_op | source)
XLA Modules:
  0.0 179.9 jit_solution(18201261087453976385)
XLA Ops:
  8.7 1.4 collective-permute-start.4
  15.0 20.4 %all-to-all-start = ((bf16[32,176,128]{2,1,0:T(8,128)(2,1)}), bf16[32,176,128]{2,1,0:T(8,128)(2,1)S(1)}, u32[]{:S(2)}, u32[]{:S(2)}) async-start(bf16[32,176,128]{2,1,0:T(8,128)(2,1)} %pad_maximum_fusion), calls=%async_computation | async-start | bytes 2883584 | tf_op jit(solution)/shard_map/all_to_all | solution.py:35
  35.4 3.4 %collective-permute-start.3 = (bf16[128,512]{1,0:T(8,128)(2,1)S(1)}, bf16[128,512]{1,0:T(8,128)(2,1)S(1)}, u32[]{:S(2)}, u32[]{:S(2)}) collective-permute-start(bf16[128,512]{1,0:T(8,128)(2,1)S(1)} %copy-done.4), channel_id=1, source_target_pairs={{0,6},{2,70},{4,2},{6,66},{64,4},{66,68},{68,0},{70,64},{1,7},{3,7... | collective-permute-start | bytes 393224 | tf_op jit(solution)/shard_map/ppermute | solution.py:60
  38.8 4.8 %collective-permute-start.2 = (bf16[128,512]{1,0:T(8,128)(2,1)S(1)}, bf16[128,512]{1,0:T(8,128)(2,1)S(1)}, u32[]{:S(2)}, u32[]{:S(2)}) collective-permute-start(bf16[128,512]{1,0:T(8,128)(2,1)S(1)} %copy-done.4), channel_id=1, source_target_pairs={{0,4},{2,68},{4,0},{6,64},{64,6},{66,70},{68,2},{70,66},{1,5},{3,6... | collective-permute-start | bytes 393224 | tf_op jit(solution)/shard_map/ppermute | solution.py:60
  43.6 3.2 %collective-permute-start.1 = (bf16[128,512]{1,0:T(8,128)(2,1)S(1)}, bf16[128,512]{1,0:T(8,128)(2,1)S(1)}, u32[]{:S(2)}, u32[]{:S(2)}) collective-permute-start(bf16[128,512]{1,0:T(8,128)(2,1)S(1)} %copy-done.4), channel_id=1, source_target_pairs={{0,2},{2,66},{4,6},{6,70},{64,0},{66,64},{68,4},{70,68},{1,3},{3,6... | collective-permute-start | bytes 393224 | tf_op jit(solution)/shard_map/ppermute | solution.py:60
  47.5 21.8 %all-to-all-done = bf16[32,176,128]{2,1,0:T(8,128)(2,1)S(1)} async-done(((bf16[32,176,128]{2,1,0:T(8,128)(2,1)}), bf16[32,176,128]{2,1,0:T(8,128)(2,1)S(1)}, u32[]{:S(2)}, u32[]{:S(2)}) %all-to-all-start) | async-done | bytes 1441824 | tf_op jit(solution)/shard_map/all_to_all | solution.py:35
  69.3 2.2 %collective-permute-start.5 = (f32[48,128]{1,0:T(8,128)S(1)}, f32[48,128]{1,0:T(8,128)S(1)}, u32[]{:S(2)}, u32[]{:S(2)}) collective-permute-start(f32[48,128]{1,0:T(8,128)S(1)} %convert_reduce_fusion.1), channel_id=1, source_target_pairs={{0,64},{64,0},{1,65},{65,1},{2,66},{66,2},{3,67},{67,3},{4,68},{68... | collective-permute-start | bytes 73736 | tf_op jit(solution)/shard_map/ppermute | solution.py:47
  71.6 3.2 %collective-permute-done.5 = f32[48,128]{1,0:T(8,128)S(1)} collective-permute-done((f32[48,128]{1,0:T(8,128)S(1)}, f32[48,128]{1,0:T(8,128)S(1)}, u32[]{:S(2)}, u32[]{:S(2)}) %collective-permute-start.5) | collective-permute-done | bytes 24608 | tf_op jit(solution)/shard_map/ppermute | solution.py:47
  74.8 5.7 %all-gather.3.cloned.1.call-done = bf16[4096,512]{1,0:T(8,128)(2,1)} async-done(((bf16[1024,512]{1,0:T(8,128)(2,1)}), bf16[4096,512]{1,0:T(8,128)(2,1)}) %all-gather.3.cloned.1.call-update) | async-done | bytes 4194320 | tf_op jit(solution)/shard_map/all_gather | solution.py:57
  80.5 2.5 %fusion.10 = f32[128,2048]{1,0:T(8,128)S(1)} fusion(bf16[4096,512]{1,0:T(8,128)(2,1)} %all-gather.3.cloned.1.call-done, bf16[4,128,512]{2,1,0:T(8,128)(2,1)S(1)} %pad_maximum_fusion.3, s32[]{:T(128)S(6)} %select_n.31), kind=kOutput, calls=%fused_computation.13 | convolution fusion | flops 268435456 | bytes 3276804 | tf_op jit(solution)/shard_map/dot_general | solution.py:31
  83.1 2.4 %fusion.12 = f32[128,2048]{1,0:T(8,128)S(1)} fusion(bf16[4096,512]{1,0:T(8,128)(2,1)} %all-gather.3.cloned.1.call-done, bf16[4,128,512]{2,1,0:T(8,128)(2,1)S(1)} %pad_maximum_fusion.3, s32[]{:T(128)S(6)} %select_n.29), kind=kOutput, calls=%fused_computation.15 | convolution fusion | flops 268435456 | bytes 3276804 | tf_op jit(solution)/shard_map/dot_general | solution.py:31
  88.6 2.5 %pad_maximum_fusion.1 = bf16[32,176,128]{2,1,0:T(8,128)(2,1)} fusion(bf16[32,48,128]{2,1,0:T(8,128)(2,1)S(1)} %broadcast_in_dim.7, bf16[32,128,128]{2,1,0:T(8,128)(2,1)} %bitcast.83), kind=kLoop, calls=%fused_computation.18 | loop fusion | flops 2883584 | bytes 2883584 | tf_op jit(solution)/shard_map/concatenate | solution.py:97
  91.1 9.9 %all-to-all-start.1 = ((bf16[32,176,128]{2,1,0:T(8,128)(2,1)}), bf16[32,176,128]{2,1,0:T(8,128)(2,1)S(1)}, u32[]{:S(2)}, u32[]{:S(2)}) async-start(bf16[32,176,128]{2,1,0:T(8,128)(2,1)} %pad_maximum_fusion.1), calls=%async_computation.1 | async-start | bytes 2883584 | tf_op jit(solution)/shard_map/all_to_all | solution.py:35
  105.5 7.4 %collective-permute-start.9 = (bf16[128,512]{1,0:T(8,128)(2,1)S(1)}, bf16[128,512]{1,0:T(8,128)(2,1)S(1)}, u32[]{:S(2)}, u32[]{:S(2)}) collective-permute-start(bf16[128,512]{1,0:T(8,128)(2,1)S(1)} %get-tuple-element.15), channel_id=1, source_target_pairs={{0,68},{2,4},{4,64},{6,0},{64,70},{66,6},{68,66},{70,2},{1,69},{3,... | collective-permute-start | bytes 393224 | tf_op jit(solution)/shard_map/ppermute | solution.py:84
  113.0 4.2 %collective-permute-start.8 = (bf16[128,512]{1,0:T(8,128)(2,1)S(1)}, bf16[128,512]{1,0:T(8,128)(2,1)S(1)}, u32[]{:S(2)}, u32[]{:S(2)}) collective-permute-start(bf16[128,512]{1,0:T(8,128)(2,1)S(1)} %get-tuple-element.16), channel_id=1, source_target_pairs={{0,4},{2,68},{4,0},{6,64},{64,6},{66,70},{68,2},{70,66},{1,5},{3,6... | collective-permute-start | bytes 393224 | tf_op jit(solution)/shard_map/ppermute | solution.py:84
  117.2 1.9 %collective-permute-start.7 = (bf16[128,512]{1,0:T(8,128)(2,1)S(1)}, bf16[128,512]{1,0:T(8,128)(2,1)S(1)}, u32[]{:S(2)}, u32[]{:S(2)}) collective-permute-start(bf16[128,512]{1,0:T(8,128)(2,1)S(1)} %get-tuple-element.17), channel_id=1, source_target_pairs={{0,64},{2,0},{4,68},{6,4},{64,66},{66,2},{68,70},{70,6},{1,65},{3,... | collective-permute-start | bytes 393224 | tf_op jit(solution)/shard_map/ppermute | solution.py:84
  119.2 8.3 %collective-permute-done.8 = bf16[128,512]{1,0:T(8,128)(2,1)S(1)} collective-permute-done((bf16[128,512]{1,0:T(8,128)(2,1)S(1)}, bf16[128,512]{1,0:T(8,128)(2,1)S(1)}, u32[]{:S(2)}, u32[]{:S(2)}) %collective-permute-start.8) | collective-permute-done | bytes 131104 | tf_op jit(solution)/shard_map/ppermute | solution.py:84
  127.4 1.6 collective-permute-done.7
  129.1 8.3 %all-to-all-done.1 = bf16[32,176,128]{2,1,0:T(8,128)(2,1)S(1)} async-done(((bf16[32,176,128]{2,1,0:T(8,128)(2,1)}), bf16[32,176,128]{2,1,0:T(8,128)(2,1)S(1)}, u32[]{:S(2)}, u32[]{:S(2)}) %all-to-all-start.1) | async-done | bytes 1441824 | tf_op jit(solution)/shard_map/all_to_all | solution.py:35
  139.0 5.7 %all-to-all-start.2 = ((bf16[4,512,128]{1,2,0:T(8,128)(2,1)}), bf16[4,512,128]{1,2,0:T(8,128)(2,1)S(1)}, u32[]{:S(2)}, u32[]{:S(2)}) async-start(bf16[4,512,128]{1,2,0:T(8,128)(2,1)} %broadcast_in_dim.8), calls=%async_computation.2 | async-start | bytes 1048576 | tf_op jit(solution)/shard_map/all_to_all | solution.py:35
  146.6 14.1 %all-to-all-done.2 = bf16[4,512,128]{1,2,0:T(8,128)(2,1)S(1)} async-done(((bf16[4,512,128]{1,2,0:T(8,128)(2,1)}), bf16[4,512,128]{1,2,0:T(8,128)(2,1)S(1)}, u32[]{:S(2)}, u32[]{:S(2)}) %all-to-all-start.2) | async-done | bytes 524320 | tf_op jit(solution)/shard_map/all_to_all | solution.py:35
  160.7 5.6 %collective-permute-start.11 = (f32[256,128]{0,1:T(8,128)S(1)}, f32[256,128]{0,1:T(8,128)S(1)}, u32[]{:S(2)}, u32[]{:S(2)}) collective-permute-start(f32[256,128]{0,1:T(8,128)S(1)} %convert_reduce_fusion.2), channel_id=1, source_target_pairs={{0,1},{1,0},{2,3},{3,2},{4,5},{5,4},{6,7},{7,6},{8,9},{9,8},{10,11... | collective-permute-start | bytes 393224 | tf_op jit(solution)/shard_map/ppermute | solution.py:47
  166.4 1.9 %collective-permute-start.12 = (bf16[4,256,128]{1,2,0:T(8,128)(2,1)S(1)}, bf16[4,256,128]{1,2,0:T(8,128)(2,1)S(1)}, u32[]{:S(2)}, u32[]{:S(2)}) collective-permute-start(bf16[4,256,128]{1,2,0:T(8,128)(2,1)S(1)} %slice.58), channel_id=1, source_target_pairs={{0,1},{1,0},{2,3},{3,2},{4,5},{5,4},{6,7},{7,6},{8,9},{9,8},{10,11... | collective-permute-start | bytes 786440 | tf_op jit(solution)/shard_map/ppermute | solution.py:47
  170.0 2.5 %fusion.50 = f32[256,512]{1,0:T(8,128)} fusion(bf16[256,1024]{0,1:T(8,128)(2,1)S(1)} %bitcast.91, bf16[1024,512]{1,0:T(8,128)(2,1)} %all-gather.5.cloned.1.call-done), kind=kOutput, calls=%fused_computation.76 | convolution fusion | flops 268435456 | bytes 2097152 | tf_op jit(solution)/shard_map/dot_general | solution.py:31
  (71 shorter events, 19.0 us)
Async XLA Ops:
  8.0 4.4 %copy-start = (bf16[128,1024]{1,0:T(8,128)(2,1)S(1)}, bf16[128,1024]{1,0:T(8,128)(2,1)}, u32[]{:S(2)}) copy-start(bf16[128,1024]{1,0:T(8,128)(2,1)} %param.11) | copy-start | bytes 786436
  8.0 72.5 %all-gather.3.cloned.1.call-start = ((), (), s32[]{:S(2)}) async-start(), calls=%async_computation.3 | async-start | bytes 5242880 | tf_op jit(solution)/shard_map/all_gather | solution.py:57
  8.7 4.7 %collective-permute-start.4 = (bf16[128,128]{1,0:T(8,128)(2,1)}, bf16[128,128]{1,0:T(8,128)(2,1)S(1)}, u32[]{:S(2)}, u32[]{:S(2)}) collective-permute-start(bf16[128,128]{1,0:T(8,128)(2,1)} %param.6), channel_id=1, source_target_pairs={{0,0},{2,64},{4,256},{6,320},{64,128},{66,192},{68,384},{70,448},{... | collective-permute-start | bytes 98312 | tf_op jit(solution)/shard_map/ppermute | solution.py:58
  15.0 20.4 %copy-start.4 = (bf16[128,512]{1,0:T(8,128)(2,1)S(1)}, bf16[128,512]{1,0:T(8,128)(2,1)}, u32[]{:S(2)}) copy-start(bf16[128,512]{1,0:T(8,128)(2,1)} %param.10) | copy-start | bytes 393220
  15.0 54.3 %all-to-all-start = ((bf16[32,176,128]{2,1,0:T(8,128)(2,1)}), bf16[32,176,128]{2,1,0:T(8,128)(2,1)S(1)}, u32[]{:S(2)}, u32[]{:S(2)}) async-start(bf16[32,176,128]{2,1,0:T(8,128)(2,1)} %pad_maximum_fusion), calls=%async_computation | async-start | bytes 2883584 | tf_op jit(solution)/shard_map/all_to_all | solution.py:35
  35.4 36.1 %collective-permute-start.3 = (bf16[128,512]{1,0:T(8,128)(2,1)S(1)}, bf16[128,512]{1,0:T(8,128)(2,1)S(1)}, u32[]{:S(2)}, u32[]{:S(2)}) collective-permute-start(bf16[128,512]{1,0:T(8,128)(2,1)S(1)} %copy-done.4), channel_id=1, source_target_pairs={{0,6},{2,70},{4,2},{6,66},{64,4},{66,68},{68,0},{70,64},{1,7},{3,7... | collective-permute-start | bytes 393224 | tf_op jit(solution)/shard_map/ppermute | solution.py:60
  38.8 32.7 %collective-permute-start.2 = (bf16[128,512]{1,0:T(8,128)(2,1)S(1)}, bf16[128,512]{1,0:T(8,128)(2,1)S(1)}, u32[]{:S(2)}, u32[]{:S(2)}) collective-permute-start(bf16[128,512]{1,0:T(8,128)(2,1)S(1)} %copy-done.4), channel_id=1, source_target_pairs={{0,4},{2,68},{4,0},{6,64},{64,6},{66,70},{68,2},{70,66},{1,5},{3,6... | collective-permute-start | bytes 393224 | tf_op jit(solution)/shard_map/ppermute | solution.py:60
  43.6 28.0 %collective-permute-start.1 = (bf16[128,512]{1,0:T(8,128)(2,1)S(1)}, bf16[128,512]{1,0:T(8,128)(2,1)S(1)}, u32[]{:S(2)}, u32[]{:S(2)}) collective-permute-start(bf16[128,512]{1,0:T(8,128)(2,1)S(1)} %copy-done.4), channel_id=1, source_target_pairs={{0,2},{2,66},{4,6},{6,70},{64,0},{66,64},{68,4},{70,68},{1,3},{3,6... | collective-permute-start | bytes 393224 | tf_op jit(solution)/shard_map/ppermute | solution.py:60
  46.8 24.7 %collective-permute-start = (bf16[128,512]{1,0:T(8,128)(2,1)S(1)}, bf16[128,512]{1,0:T(8,128)(2,1)S(1)}, u32[]{:S(2)}, u32[]{:S(2)}) collective-permute-start(bf16[128,512]{1,0:T(8,128)(2,1)S(1)} %copy-done.4), channel_id=1, source_target_pairs={{0,0},{2,64},{4,4},{6,68},{64,2},{66,66},{68,6},{70,70},{1,1},{3,6... | collective-permute-start | bytes 393224 | tf_op jit(solution)/shard_map/ppermute | solution.py:60
  69.3 5.5 %collective-permute-start.5 = (f32[48,128]{1,0:T(8,128)S(1)}, f32[48,128]{1,0:T(8,128)S(1)}, u32[]{:S(2)}, u32[]{:S(2)}) collective-permute-start(f32[48,128]{1,0:T(8,128)S(1)} %convert_reduce_fusion.1), channel_id=1, source_target_pairs={{0,64},{64,0},{1,65},{65,1},{2,66},{66,2},{3,67},{67,3},{4,68},{68... | collective-permute-start | bytes 73736 | tf_op jit(solution)/shard_map/ppermute | solution.py:47
  80.5 5.0 %copy-start.1 = (bf16[4096,512]{1,0:T(8,128)(2,1)S(1)}, bf16[4096,512]{1,0:T(8,128)(2,1)}, u32[]{:S(2)}) copy-start(bf16[4096,512]{1,0:T(8,128)(2,1)} %all-gather.3.cloned.1.call-done) | copy-start | bytes 12582916
  91.1 46.3 %all-to-all-start.1 = ((bf16[32,176,128]{2,1,0:T(8,128)(2,1)}), bf16[32,176,128]{2,1,0:T(8,128)(2,1)S(1)}, u32[]{:S(2)}, u32[]{:S(2)}) async-start(bf16[32,176,128]{2,1,0:T(8,128)(2,1)} %pad_maximum_fusion.1), calls=%async_computation.1 | async-start | bytes 2883584 | tf_op jit(solution)/shard_map/all_to_all | solution.py:35
  101.0 68.9 %all-gather.5.cloned.1.call-start = ((), (), s32[]{:S(2)}) async-start(), calls=%async_computation.4 | async-start | bytes 1179648 | tf_op jit(solution)/shard_map/all_gather | solution.py:77
  104.7 32.7 %copy-start.5 = (bf16[128,128]{1,0:T(8,128)(2,1)S(1)}, bf16[128,128]{1,0:T(8,128)(2,1)}, u32[]{:S(2)}) copy-start(bf16[128,128]{1,0:T(8,128)(2,1)} %param.6) | copy-start | bytes 98308
  104.9 14.3 %collective-permute-start.6 = (bf16[128,512]{1,0:T(8,128)(2,1)S(1)}, bf16[128,512]{1,0:T(8,128)(2,1)S(1)}, u32[]{:S(2)}, u32[]{:S(2)}) collective-permute-start(bf16[128,512]{1,0:T(8,128)(2,1)S(1)} %get-tuple-element.14), channel_id=1, source_target_pairs={{0,0},{2,64},{4,4},{6,68},{64,2},{66,66},{68,6},{70,70},{1,1},{3,6... | collective-permute-start | bytes 393224 | tf_op jit(solution)/shard_map/ppermute | solution.py:84
  105.5 13.6 %collective-permute-start.9 = (bf16[128,512]{1,0:T(8,128)(2,1)S(1)}, bf16[128,512]{1,0:T(8,128)(2,1)S(1)}, u32[]{:S(2)}, u32[]{:S(2)}) collective-permute-start(bf16[128,512]{1,0:T(8,128)(2,1)S(1)} %get-tuple-element.15), channel_id=1, source_target_pairs={{0,68},{2,4},{4,64},{6,0},{64,70},{66,6},{68,66},{70,2},{1,69},{3,... | collective-permute-start | bytes 393224 | tf_op jit(solution)/shard_map/ppermute | solution.py:84
  113.0 14.5 %collective-permute-start.8 = (bf16[128,512]{1,0:T(8,128)(2,1)S(1)}, bf16[128,512]{1,0:T(8,128)(2,1)S(1)}, u32[]{:S(2)}, u32[]{:S(2)}) collective-permute-start(bf16[128,512]{1,0:T(8,128)(2,1)S(1)} %get-tuple-element.16), channel_id=1, source_target_pairs={{0,4},{2,68},{4,0},{6,64},{64,6},{66,70},{68,2},{70,66},{1,5},{3,6... | collective-permute-start | bytes 393224 | tf_op jit(solution)/shard_map/ppermute | solution.py:84
  117.2 11.8 %collective-permute-start.7 = (bf16[128,512]{1,0:T(8,128)(2,1)S(1)}, bf16[128,512]{1,0:T(8,128)(2,1)S(1)}, u32[]{:S(2)}, u32[]{:S(2)}) collective-permute-start(bf16[128,512]{1,0:T(8,128)(2,1)S(1)} %get-tuple-element.17), channel_id=1, source_target_pairs={{0,64},{2,0},{4,68},{6,4},{64,66},{66,2},{68,70},{70,6},{1,65},{3,... | collective-permute-start | bytes 393224 | tf_op jit(solution)/shard_map/ppermute | solution.py:84
  137.7 7.9 %copy-start.3 = (bf16[256,512]{1,0:T(8,128)(2,1)S(1)}, bf16[256,512]{1,0:T(8,128)(2,1)}, u32[]{:S(2)}) copy-start(bf16[256,512]{1,0:T(8,128)(2,1)} %param.9) | copy-start | bytes 786436
  139.0 29.3 %copy-start.6 = (bf16[128,256]{1,0:T(8,128)(2,1)S(1)}, bf16[128,256]{1,0:T(8,128)(2,1)}, u32[]{:S(2)}) copy-start(bf16[128,256]{1,0:T(8,128)(2,1)} %param.8) | copy-start | bytes 196612
  139.0 21.6 %all-to-all-start.2 = ((bf16[4,512,128]{1,2,0:T(8,128)(2,1)}), bf16[4,512,128]{1,2,0:T(8,128)(2,1)S(1)}, u32[]{:S(2)}, u32[]{:S(2)}) async-start(bf16[4,512,128]{1,2,0:T(8,128)(2,1)} %broadcast_in_dim.8), calls=%async_computation.2 | async-start | bytes 1048576 | tf_op jit(solution)/shard_map/all_to_all | solution.py:35
  145.0 23.3 %collective-permute-start.10 = (f32[128,128]{0,1:T(8,128)S(1)}, f32[128,128]{0,1:T(8,128)S(1)}, u32[]{:S(2)}, u32[]{:S(2)}) collective-permute-start(f32[128,128]{0,1:T(8,128)S(1)} %copy.32), channel_id=1, source_target_pairs={{0,0},{64,2},{256,4},{320,6},{128,64},{192,66},{384,68},{448,70},{... | collective-permute-start | bytes 196616 | tf_op jit(solution)/shard_map/ppermute | solution.py:99
  160.7 8.4 %collective-permute-start.11 = (f32[256,128]{0,1:T(8,128)S(1)}, f32[256,128]{0,1:T(8,128)S(1)}, u32[]{:S(2)}, u32[]{:S(2)}) collective-permute-start(f32[256,128]{0,1:T(8,128)S(1)} %convert_reduce_fusion.2), channel_id=1, source_target_pairs={{0,1},{1,0},{2,3},{3,2},{4,5},{5,4},{6,7},{7,6},{8,9},{9,8},{10,11... | collective-permute-start | bytes 393224 | tf_op jit(solution)/shard_map/ppermute | solution.py:47
  166.4 3.4 %collective-permute-start.12 = (bf16[4,256,128]{1,2,0:T(8,128)(2,1)S(1)}, bf16[4,256,128]{1,2,0:T(8,128)(2,1)S(1)}, u32[]{:S(2)}, u32[]{:S(2)}) collective-permute-start(bf16[4,256,128]{1,2,0:T(8,128)(2,1)S(1)} %slice.58), channel_id=1, source_target_pairs={{0,1},{1,0},{2,3},{3,2},{4,5},{5,4},{6,7},{7,6},{8,9},{9,8},{10,11... | collective-permute-start | bytes 786440 | tf_op jit(solution)/shard_map/ppermute | solution.py:47
  (1 other events, 2.2 us)
Sparse Core Ops, SparseCore 0:
  10.9 69.5 all-gather.2
Sparse Core Ops, SparseCore 1:
  119.2 38.9 all-gather.4

commit v3 on v2

v3 whole, which is shorter than its diff:
```python
import jax
import jax.numpy as jnp
from jax import lax
from jax.experimental import pallas as pl
from jax.experimental.pallas import tpu as pltpu
from jax.sharding import Mesh
from jax.sharding import PartitionSpec as P

F32 = jnp.float32
BF16 = jnp.bfloat16
AXES = ("x", "ylo", "z", "yhi", "core")
SIZES = (4, 2, 8, 4, 2)
SHARD = ("x", "ylo", "z")
DP = ("yhi", "core")
THERE = [
    ((x * 2 + l) * 4 + h, ((2 * (h // 2) + l) * 2 + h % 2) * 4 + x)
    for x in range(4)
    for l in range(2)
    for h in range(4)
]
BACK = [(b, a) for a, b in THERE]
HOME = [
    [(l * 4 + h, ((h ^ j) % 2) * 4 + (h ^ j) // 2 * 2 + l) for l in range(2) for h in range(4)] for j in range(4)
]


def dot(left, right, contract):
    return lax.dot_general(left, right, ((contract[0], contract[1]), ((), ())), preferred_element_type=F32)


def exchange(pieces, axes):
    return lax.all_to_all(pieces, axes, split_axis=0, concat_axis=0, tiled=True)


def to_all(block, axes):
    return jnp.broadcast_to(block[None], (lax.axis_size(axes), *block.shape))


def add_up(pieces):
    return jnp.sum(pieces.astype(F32), axis=0)


def trade(block, axis):
    return lax.ppermute(block, axis, [(0, 1), (1, 0)])


def slab_kernel(core_ref, near_ref, far_ref, near_beside_ref, far_beside_ref, own_ref, other_ref, out_ref):
    block = batch = out_ref.shape[4]

    def write(own_weight, other_weight):
        total = lax.dot_general(own_weight, own_ref[...], (((1,), (1,)), ((), ())), preferred_element_type=F32)
        total += lax.dot_general(other_weight, other_ref[...], (((1,), (1,)), ((), ())), preferred_element_type=F32)
        total = total.astype(BF16)
        for i in range(2):
            for j in range(out_ref.shape[2]):
                out_ref[i, 0, j, :block, :] = total[j * block : (j + 1) * block, i * batch : (i + 1) * batch]

    @pl.when(pl.program_id(0) == 0)
    def _():
        write(near_ref[...], far_ref[...])

    @pl.when(pl.program_id(0) == 1)
    def _():
        write(near_beside_ref[...], far_beside_ref[...])


def slabs_of(core, own_core, other_core, own, other, extra):
    batch = own.shape[0] // 2
    block, take = batch, 4
    depth, hidden = own_core[0].shape
    steps = depth // (take * block)
    early = pl.BlockSpec((take * block, hidden), lambda s, r, _: (jnp.where(s == 0, r, steps - 1), 0))
    late = pl.BlockSpec((take * block, hidden), lambda s, r, _: (jnp.where(s == 0, 0, r), 0))
    whole = pl.BlockSpec(own.shape, lambda s, r, _: (0, 0))
    out = pl.pallas_call(
        slab_kernel,
        grid_spec=pltpu.PrefetchScalarGridSpec(
            num_scalar_prefetch=1,
            grid=(2, steps),
            in_specs=[early, early, late, late, whole, whole],
            out_specs=pl.BlockSpec(
                (2, 1, take, block + extra, batch), lambda s, r, c: (0, s ^ c[0], r, 0, 0)
            ),
        ),
        out_shape=jax.ShapeDtypeStruct((2, 2, steps * take, block + extra, batch), BF16),
        cost_estimate=pl.CostEstimate(
            flops=16 * depth * hidden * batch, bytes_accessed=8 * depth * hidden, transcendentals=0
        ),
    )(core[None], *own_core, *other_core, own, other)
    return out.reshape(4 * steps * take, block + extra, batch)


def local(tokens, weight, down, up, cotangent, directions):
    n_z = lax.axis_size("z")
    batch, block = tokens.shape
    rank = down.shape[1]
    past = directions.shape[1]
    depth, hidden = weight.shape

    ylo, high, core = (lax.axis_index(a) for a in ("ylo", "yhi", "core"))
    columns = lax.all_gather(cotangent, ("yhi", "ylo"), axis=0).reshape(2, 2, 2, batch, hidden)
    moved = lax.ppermute(tokens, ("x", "ylo", "yhi"), THERE)

    share = jnp.concatenate(
        [
            dot(down, tokens, ((0,), (1,))),
            dot(directions, tokens, ((0,), (1,))),
            dot(up, cotangent, ((1,), (1,))),
        ],
        axis=0,
    ).astype(BF16)
    first = jnp.concatenate([to_all(moved, ("x", "z")), share.reshape(4 * n_z, -1, batch)], axis=1)
    first, weight = lax.optimization_barrier((first, weight))
    first = exchange(first, ("x", "z"))

    far = trade(weight, "ylo")
    own_core, other_core = (weight, far), (trade(weight, "core"), trade(far, "core"))
    own, other = (
        lax.dynamic_slice(columns, (0, ylo, l, 0, 0), (2, 1, 1, batch, hidden)).reshape(2 * batch, hidden)
        for l in (ylo, 1 - ylo)
    )
    cotangent_column = lax.dynamic_index_in_dim(columns, ylo, 2, keepdims=False).reshape(4 * batch, hidden)
    first, own_core, other_core, own, other = lax.optimization_barrier((first, own_core, other_core, own, other))
    summed = add_up(first[:, batch:])
    beside = trade(summed, "ylo")
    panels = first[:, :batch].reshape(2, 2, n_z, batch, block)
    panels = [
        lax.dynamic_index_in_dim(panels, c, 1, keepdims=False).transpose(0, 2, 1, 3).reshape(2 * batch, depth)
        for c in (core, 1 - core)
    ]
    frozen = [
        (dot(panels[0], own_core[i], ((1,), (0,))) + dot(panels[1], other_core[i], ((1,), (0,)))).astype(BF16)
        for i in range(2)
    ]
    frozen = jnp.stack([f.reshape(2, batch, hidden) for f in frozen], axis=1).reshape(4, batch, hidden)
    frozen = sum(
        lax.ppermute(
            lax.dynamic_index_in_dim(frozen, high ^ j ^ ylo, 0, keepdims=False), ("ylo", "yhi"), HOME[j]
        ).astype(F32)
        for j in range(4)
    )

    slabs = slabs_of(core, own_core, other_core, own, other, summed.shape[0])
    slabs, beside = lax.optimization_barrier((slabs, beside))
    summed = (summed + beside).astype(BF16)
    second = exchange(
        lax.dynamic_update_slice(slabs, to_all(summed, ("x", "z")), (0, block, 0)), ("x", "z")
    )
    second, frozen = lax.optimization_barrier((second, frozen))
    gradient = lax.ppermute(add_up(second[:, :block]), ("x", "ylo", "yhi"), BACK)
    whole = second[:, block:].reshape(share.shape)
    low, along, back_low = whole[:rank], whole[rank : rank + past], whole[rank + past :]

    projection_output = (frozen + dot(low, up, ((0,), (0,)))).astype(BF16)
    token_input_gradient = (gradient + dot(down, back_low, ((1,), (0,)))).T.astype(BF16)

    kept = tokens.astype(F32).T - dot(directions, along, ((1,), (0,)))
    kept_high = kept.astype(BF16)
    kept_rest = (kept - kept_high.astype(F32)).astype(BF16)
    down_part = dot(back_low, kept_high, ((1,), (1,))) + dot(back_low, kept_rest, ((1,), (1,)))
    pair = exchange(to_all(jnp.concatenate([low, down_part.astype(BF16)], axis=0), "yhi"), "yhi")
    low_column = pair[:, :rank].transpose(1, 0, 2).reshape(rank, 4 * batch)
    up_part = dot(low_column, cotangent_column, ((1,), (0,)))
    grad_up = up_part + trade(up_part, "core")
    down_part = add_up(pair[:, rank:])
    grad_down = (down_part + trade(down_part, "core")).T
    return projection_output, token_input_gradient, grad_down, grad_up


def solution(mesh):
    fine = Mesh(mesh.devices.reshape(SIZES), AXES)
    placed = (P(DP, SHARD), P(DP, SHARD), P(SHARD, None), P(None, SHARD), P(DP, SHARD), P(SHARD, None))
    return jax.shard_map(
        local,
        mesh=fine,
        in_specs=placed,
        out_specs=(P(DP, SHARD), P(DP, SHARD), P(SHARD, None), P(None, SHARD)),
        check_vma=False,
    )
```

time: 181 us -> 167 us (0.923)
  waiting for transfers between devices: 63.7 us -> 44.1 us
  Pallas kernels: 0 us -> 5.67 us
  starting transfers between devices: 74.1 us -> 79.4 us
  matrix products: 15.3 us -> 11.6 us
  other arithmetic: 5.79 us -> 3.88 us
    all_to_all x3, waiting for transfers between devices: 44.2 us -> 10.1 us  [exchange(): return lax.all_to_all(pieces, axes, split_axis=0, concat_axis=0, tiled=True)]
    ppermute x3 -> x6, starting transfers between devices: 9.71 us -> 28.6 us  [trade(): return lax.ppermute(block, axis, [(0, 1), (1, 0)])]
    ppermute x3 -> x6, waiting for transfers between devices: 3.18 us -> 21.8 us  [trade(): return lax.ppermute(block, axis, [(0, 1), (1, 0)])]
    ppermute x8 -> x4, starting transfers between devices: 26.3 us -> 13.9 us  [local(): lax.ppermute(lax.dynamic_index_in_dim(frozen, high ^ j ^ ylo, 0, keepdims...]
    pallas_call x0 -> x1, Pallas kernels: none -> 5.67 us  [slabs_of(): pl.pallas_call(slab_kernel, grid_spec=pltpu.PrefetchScalarGridSpec(num_sc...]
    ppermute x8 -> x4, waiting for transfers between devices: 9.88 us -> 5.33 us  [local(): lax.ppermute(lax.dynamic_index_in_dim(frozen, high ^ j ^ ylo, 0, keepdims...]
    dot_general x15 -> x13, matrix products: 15.3 us -> 11.6 us  [dot(): lax.dot_general(left, right, ((contract[0], contract[1]), ((), ())), pref...]
    dynamic_slice x0 -> x2, local copies, waits for them, and re-layouts: none -> 2.93 us  [the longest x1 1.86 us: local(): lax.dynamic_slice(columns, (0, ylo, l, 0, 0), (2, 1, 1, batch, hidden))]
  transfers between devices with their start and end apart: 18 -> 16, of which waited for: 7 -> 6; matrix products, arithmetic and copies ran while one was open for 6% -> 10% of each run, Pallas kernels for 0% -> 3%
where the time goes in v3:
time: 167 us; the launch traced here: 165 us
  starting transfers between devices  79.4 us (48%)
  waiting for transfers between devices  44.1 us (26%)
  between operations  14.5 us (9%)
  matrix products  11.6 us (7%)
  local copies, waits for them, and re-layouts  6.06 us (4%)
  Pallas kernels  5.67 us (3%)
  other arithmetic  3.88 us (2%)
    all_to_all x3, starting transfers between devices, exchange(): return lax.all_to_all(pieces, axes, split_axis=0, concat_axis=0, tiled=True)  34.6 us
    ppermute x6, starting transfers between devices, trade(): return lax.ppermute(block, axis, [(0, 1), (1, 0)])  28.6 us
    ppermute x6, waiting for transfers between devices, trade(): return lax.ppermute(block, axis, [(0, 1), (1, 0)])  21.8 us
    ppermute x4, starting transfers between devices, local(): lax.ppermute(lax.dynamic_index_in_dim(frozen, high ^ j ^ ylo, 0, keepdims...  13.9 us
    dot_general x13, matrix products, dot(): lax.dot_general(left, right, ((contract[0], contract[1]), ((), ())), pref...  11.6 us
    all_to_all x3, waiting for transfers between devices, exchange(): return lax.all_to_all(pieces, axes, split_axis=0, concat_axis=0, tiled=True)  10.1 us
    all_gather x1, waiting for transfers between devices, local(): lax.all_gather(cotangent, ('yhi', 'ylo'), axis=0)  6.83 us
    pallas_call x1, Pallas kernels, slabs_of(): pl.pallas_call(slab_kernel, grid_spec=pltpu.PrefetchScalarGridSpec(num_sc...  5.67 us
  transfers between devices with their start and end apart: 16, of which 6 were waited for; matrix products, arithmetic and copies ran while one was open for 10% of the time, Pallas kernels for 3%

profile of v3, /device:TPU:1, one launch (start us, length us, event | category | flops | bytes accessed | tf_op | source)
XLA Modules:
  0.0 165.1 jit_solution(9955727997507106226)
XLA Ops:
  7.2 1.5 collective-permute-start
  12.3 1.2 pad_maximum_fusion
  13.5 20.4 %all-to-all-start = ((bf16[32,176,128]{2,1,0:T(8,128)(2,1)}), bf16[32,176,128]{2,1,0:T(8,128)(2,1)S(1)}, u32[]{:S(2)}, u32[]{:S(2)}) async-start(bf16[32,176,128]{2,1,0:T(8,128)(2,1)} %pad_maximum_fusion), calls=%async_computation | async-start | bytes 2883584 | tf_op jit(solution)/shard_map/all_to_all | solution.py:32
  34.0 2.3 %collective-permute-start.1 = (bf16[1024,512]{1,0:T(8,128)(2,1)S(1)}, bf16[1024,512]{1,0:T(8,128)(2,1)}, u32[]{:S(2)}, u32[]{:S(2)}) collective-permute-start(bf16[1024,512]{1,0:T(8,128)(2,1)S(1)} %copy-done.1), channel_id=1, source_target_pairs={{0,64},{64,0},{1,65},{65,1},{2,66},{66,2},{3,67},{67,3},{4,68},{68... | collective-permute-start | bytes 3145736 | tf_op jit(solution)/shard_map/ppermute | solution.py:44
  36.3 4.5 %collective-permute-start.2 = (bf16[1024,512]{1,0:T(8,128)(2,1)S(1)}, bf16[1024,512]{1,0:T(8,128)(2,1)}, u32[]{:S(2)}, u32[]{:S(2)}) collective-permute-start(bf16[1024,512]{1,0:T(8,128)(2,1)S(1)} %copy-done.1), channel_id=1, source_target_pairs={{0,1},{1,0},{2,3},{3,2},{4,5},{5,4},{6,7},{7,6},{8,9},{9,8},{10,11... | collective-permute-start | bytes 3145736 | tf_op jit(solution)/shard_map/ppermute | solution.py:44
  40.8 21.3 %collective-permute-done.1.far_ref = bf16[1024,512]{1,0:T(8,128)(2,1)} collective-permute-done((bf16[1024,512]{1,0:T(8,128)(2,1)S(1)}, bf16[1024,512]{1,0:T(8,128)(2,1)}, u32[]{:S(2)}, u32[]{:S(2)}) %collective-permute-start.1) | collective-permute-done | bytes 1048608 | tf_op jit(solution)/shard_map/ppermute | solution.py:44
  62.2 6.0 %collective-permute-start.3 = (bf16[1024,512]{1,0:T(8,128)(2,1)}, bf16[1024,512]{1,0:T(8,128)(2,1)}, u32[]{:S(2)}, u32[]{:S(2)}) collective-permute-start(bf16[1024,512]{1,0:T(8,128)(2,1)} %collective-permute-done.1.far_ref), channel_id=1, source_target_pairs={{0,1},{1,0},{2,3},{3,2},{4,5},{5,4},{6,7},{7,6},{8,9},{9,8},{10,11... | collective-permute-start | bytes 3145736 | tf_op jit(solution)/shard_map/ppermute | solution.py:44
  68.2 6.8 %all-gather.3.cloned.1.call-done = bf16[1024,512]{1,0:T(8,128)(2,1)} async-done(((bf16[128,512]{1,0:T(8,128)(2,1)}), bf16[1024,512]{1,0:T(8,128)(2,1)}) %all-gather.3.cloned.1.call-update) | async-done | bytes 1048592 | tf_op jit(solution)/shard_map/all_gather | solution.py:101
  75.0 1.9 %constant_dynamic-slice_fusion.1 = (bf16[2,1,1,128,512]{4,3,2,1,0:T(8,128)(2,1)}, bf16[2,1,1,128,512]{4,3,2,1,0:T(8,128)(2,1)}) fusion(bf16[2,2,2,128,512]{4,3,2,1,0:T(8,128)(2,1)} %bitcast.100, s32[]{:T(128)S(6)} %select_n.30, s32[]{:T(128)S(6)} %select_n.31), kind=kLoop, calls=%fused_computation.52 | loop fusion | bytes 1048584 | tf_op jit(solution)/shard_map/dynamic_slice | solution.py:119
  77.0 2.6 %collective-permute-start.4 = (f32[48,128]{1,0:T(8,128)S(1)}, f32[48,128]{1,0:T(8,128)S(1)}, u32[]{:S(2)}, u32[]{:S(2)}) collective-permute-start(f32[48,128]{1,0:T(8,128)S(1)} %convert_reduce_fusion.1), channel_id=1, source_target_pairs={{0,64},{64,0},{1,65},{65,1},{2,66},{66,2},{3,67},{67,3},{4,68},{68... | collective-permute-start | bytes 73736 | tf_op jit(solution)/shard_map/ppermute | solution.py:44
  79.6 5.7 %shard_map.93 = bf16[2,2,8,176,128]{4,3,2,1,0:T(8,128)(2,1)} custom-call(s32[1]{0:T(128)} %bitcast.core_ref, bf16[1024,512]{1,0:T(8,128)(2,1)} %near_ref, bf16[1024,512]{1,0:T(8,128)(2,1)} %collective-permute-done.1.far_ref, bf16[1024,512]{1,0:T(8,128)(2,1)} %collective-permute-done.2.near_beside_ref, ...), custom_call_target="tpu_custom_call" | custom-call | flops 1073741824 | bytes 4194304 | tf_op jit(solution)/shard_map/pallas_call | solution.py:75
  86.1 10.2 %all-to-all-start.1 = ((bf16[32,176,128]{2,1,0:T(8,128)(2,1)}), bf16[32,176,128]{2,1,0:T(8,128)(2,1)S(1)}, u32[]{:S(2)}, u32[]{:S(2)}) async-start(bf16[32,176,128]{2,1,0:T(8,128)(2,1)} %broadcast_dynamic-update-slice_fusion), calls=%async_computation.1 | async-start | bytes 2883584 | tf_op jit(solution)/shard_map/all_to_all | solution.py:32
  97.2 1.7 %fusion.7 = f32[256,512]{1,0:T(8,128)S(1)} fusion(bf16[1024,512]{1,0:T(8,128)(2,1)} %collective-permute-done.3.far_beside_ref, bf16[32,8,8,128]{3,2,1,0:T(8,128)(2,1)S(1)} %bitcast.85), kind=kOutput, calls=%fused_computation.18 | convolution fusion | flops 268435456 | bytes 2097152 | tf_op jit(solution)/shard_map/dot_general | solution.py:28
  98.9 1.7 %fusion.9 = f32[256,512]{1,0:T(8,128)S(1)} fusion(bf16[1024,512]{1,0:T(8,128)(2,1)} %collective-permute-done.2.near_beside_ref, bf16[32,8,8,128]{3,2,1,0:T(8,128)(2,1)S(1)} %bitcast.86), kind=kOutput, calls=%fused_computation.20 | convolution fusion | flops 268435456 | bytes 2097152 | tf_op jit(solution)/shard_map/dot_general | solution.py:28
  100.5 1.7 %fusion.1 = bf16[256,512]{1,0:T(8,128)(2,1)S(1)} fusion(f32[256,512]{1,0:T(8,128)S(1)} %fusion.7, bf16[1024,512]{1,0:T(8,128)(2,1)} %collective-permute-done.1.far_ref, bf16[32,8,8,128]{3,2,1,0:T(8,128)(2,1)S(1)} %bitcast.83), kind=kOutput, calls=%fused_computation.5 | convolution fusion | flops 268697600 | bytes 2359296 | tf_op jit(solution)/shard_map/dot_general | solution.py:28
  103.5 6.7 %collective-permute-start.8 = (bf16[128,512]{1,0:T(8,128)(2,1)S(1)}, bf16[128,512]{1,0:T(8,128)(2,1)S(1)}, u32[]{:S(2)}, u32[]{:S(2)}) collective-permute-start(bf16[128,512]{1,0:T(8,128)(2,1)S(1)} %get-tuple-element.35), channel_id=1, source_target_pairs={{0,68},{2,4},{4,64},{6,0},{64,70},{66,6},{68,66},{70,2},{1,69},{3,... | collective-permute-start | bytes 393224 | tf_op jit(solution)/shard_map/ppermute | solution.py:137
  110.3 4.6 %collective-permute-start.7 = (bf16[128,512]{1,0:T(8,128)(2,1)S(1)}, bf16[128,512]{1,0:T(8,128)(2,1)S(1)}, u32[]{:S(2)}, u32[]{:S(2)}) collective-permute-start(bf16[128,512]{1,0:T(8,128)(2,1)S(1)} %get-tuple-element.36), channel_id=1, source_target_pairs={{0,4},{2,68},{4,0},{6,64},{64,6},{66,70},{68,2},{70,66},{1,5},{3,6... | collective-permute-start | bytes 393224 | tf_op jit(solution)/shard_map/ppermute | solution.py:137
  114.9 1.9 %collective-permute-start.6 = (bf16[128,512]{1,0:T(8,128)(2,1)S(1)}, bf16[128,512]{1,0:T(8,128)(2,1)S(1)}, u32[]{:S(2)}, u32[]{:S(2)}) collective-permute-start(bf16[128,512]{1,0:T(8,128)(2,1)S(1)} %get-tuple-element.37), channel_id=1, source_target_pairs={{0,64},{2,0},{4,68},{6,4},{64,66},{66,2},{68,70},{70,6},{1,65},{3,... | collective-permute-start | bytes 393224 | tf_op jit(solution)/shard_map/ppermute | solution.py:137
  116.8 5.3 %collective-permute-done.7 = bf16[128,512]{1,0:T(8,128)(2,1)S(1)} collective-permute-done((bf16[128,512]{1,0:T(8,128)(2,1)S(1)}, bf16[128,512]{1,0:T(8,128)(2,1)S(1)}, u32[]{:S(2)}, u32[]{:S(2)}) %collective-permute-start.7) | collective-permute-done | bytes 131104 | tf_op jit(solution)/shard_map/ppermute | solution.py:137
  122.2 3.6 %all-to-all-done.1 = bf16[32,176,128]{2,1,0:T(8,128)(2,1)S(1)} async-done(((bf16[32,176,128]{2,1,0:T(8,128)(2,1)}), bf16[32,176,128]{2,1,0:T(8,128)(2,1)S(1)}, u32[]{:S(2)}, u32[]{:S(2)}) %all-to-all-start.1) | async-done | bytes 1441824 | tf_op jit(solution)/shard_map/all_to_all | solution.py:32
  127.4 4.1 %all-to-all-start.2 = ((bf16[4,512,128]{1,2,0:T(8,128)(2,1)}), bf16[4,512,128]{1,2,0:T(8,128)(2,1)S(1)}, u32[]{:S(2)}, u32[]{:S(2)}) async-start(bf16[4,512,128]{1,2,0:T(8,128)(2,1)} %broadcast_in_dim.11), calls=%async_computation.2 | async-start | bytes 1048576 | tf_op jit(solution)/shard_map/all_to_all | solution.py:32
  135.3 6.5 %all-to-all-done.2 = bf16[4,512,128]{1,2,0:T(8,128)(2,1)S(1)} async-done(((bf16[4,512,128]{1,2,0:T(8,128)(2,1)}), bf16[4,512,128]{1,2,0:T(8,128)(2,1)S(1)}, u32[]{:S(2)}, u32[]{:S(2)}) %all-to-all-start.2) | async-done | bytes 524320 | tf_op jit(solution)/shard_map/all_to_all | solution.py:32
  142.2 11.3 %collective-permute-start.11 = (f32[256,512]{1,0:T(8,128)S(1)}, f32[256,512]{1,0:T(8,128)S(1)}, u32[]{:S(2)}, u32[]{:S(2)}) collective-permute-start(f32[256,512]{1,0:T(8,128)S(1)} %fusion.26), channel_id=1, source_target_pairs={{0,1},{1,0},{2,3},{3,2},{4,5},{5,4},{6,7},{7,6},{8,9},{9,8},{10,11... | collective-permute-start | bytes 1572872 | tf_op jit(solution)/shard_map/ppermute | solution.py:44
  153.5 1.9 %collective-permute-start.10 = (f32[256,128]{0,1:T(8,128)S(1)}, f32[256,128]{0,1:T(8,128)S(1)}, u32[]{:S(2)}, u32[]{:S(2)}) collective-permute-start(f32[256,128]{0,1:T(8,128)S(1)} %convert_reduce_fusion.2), channel_id=1, source_target_pairs={{0,1},{1,0},{2,3},{3,2},{4,5},{5,4},{6,7},{7,6},{8,9},{9,8},{10,11... | collective-permute-start | bytes 393224 | tf_op jit(solution)/shard_map/ppermute | solution.py:44
  (60 shorter events, 15.3 us)
Async XLA Ops:
  7.2 2.6 %copy-start = (bf16[128,1024]{1,0:T(8,128)(2,1)S(1)}, bf16[128,1024]{1,0:T(8,128)(2,1)}, u32[]{:S(2)}) copy-start(bf16[128,1024]{1,0:T(8,128)(2,1)} %param.11) | copy-start | bytes 786436
  7.2 4.9 %collective-permute-start = (bf16[128,128]{1,0:T(8,128)(2,1)}, bf16[128,128]{1,0:T(8,128)(2,1)S(1)}, u32[]{:S(2)}, u32[]{:S(2)}) collective-permute-start(bf16[128,128]{1,0:T(8,128)(2,1)} %param.6), channel_id=1, source_target_pairs={{0,0},{2,64},{4,256},{6,320},{64,128},{66,192},{68,384},{70,448},{... | collective-permute-start | bytes 98312 | tf_op jit(solution)/shard_map/ppermute | solution.py:102
  13.5 20.5 %copy-start.1 = (bf16[1024,512]{1,0:T(8,128)(2,1)S(1)}, bf16[1024,512]{1,0:T(8,128)(2,1)}, u32[]{:S(2)}) copy-start(bf16[1024,512]{1,0:T(8,128)(2,1)} %near_ref) | copy-start | bytes 3145732
  13.5 63.4 %all-to-all-start = ((bf16[32,176,128]{2,1,0:T(8,128)(2,1)}), bf16[32,176,128]{2,1,0:T(8,128)(2,1)S(1)}, u32[]{:S(2)}, u32[]{:S(2)}) async-start(bf16[32,176,128]{2,1,0:T(8,128)(2,1)} %pad_maximum_fusion), calls=%async_computation | async-start | bytes 2883584 | tf_op jit(solution)/shard_map/all_to_all | solution.py:32
  33.9 41.1 %all-gather.3.cloned.1.call-start = ((), (), s32[]{:S(2)}) async-start(), calls=%async_computation.3 | async-start | bytes 1179648 | tf_op jit(solution)/shard_map/all_gather | solution.py:101
  34.0 28.2 %collective-permute-start.1 = (bf16[1024,512]{1,0:T(8,128)(2,1)S(1)}, bf16[1024,512]{1,0:T(8,128)(2,1)}, u32[]{:S(2)}, u32[]{:S(2)}) collective-permute-start(bf16[1024,512]{1,0:T(8,128)(2,1)S(1)} %copy-done.1), channel_id=1, source_target_pairs={{0,64},{64,0},{1,65},{65,1},{2,66},{66,2},{3,67},{67,3},{4,68},{68... | collective-permute-start | bytes 3145736 | tf_op jit(solution)/shard_map/ppermute | solution.py:44
  36.3 40.6 %collective-permute-start.2 = (bf16[1024,512]{1,0:T(8,128)(2,1)S(1)}, bf16[1024,512]{1,0:T(8,128)(2,1)}, u32[]{:S(2)}, u32[]{:S(2)}) collective-permute-start(bf16[1024,512]{1,0:T(8,128)(2,1)S(1)} %copy-done.1), channel_id=1, source_target_pairs={{0,1},{1,0},{2,3},{3,2},{4,5},{5,4},{6,7},{7,6},{8,9},{9,8},{10,11... | collective-permute-start | bytes 3145736 | tf_op jit(solution)/shard_map/ppermute | solution.py:44
  62.2 14.8 %collective-permute-start.3 = (bf16[1024,512]{1,0:T(8,128)(2,1)}, bf16[1024,512]{1,0:T(8,128)(2,1)}, u32[]{:S(2)}, u32[]{:S(2)}) collective-permute-start(bf16[1024,512]{1,0:T(8,128)(2,1)} %collective-permute-done.1.far_ref), channel_id=1, source_target_pairs={{0,1},{1,0},{2,3},{3,2},{4,5},{5,4},{6,7},{7,6},{8,9},{9,8},{10,11... | collective-permute-start | bytes 3145736 | tf_op jit(solution)/shard_map/ppermute | solution.py:44
  77.0 8.2 %collective-permute-start.4 = (f32[48,128]{1,0:T(8,128)S(1)}, f32[48,128]{1,0:T(8,128)S(1)}, u32[]{:S(2)}, u32[]{:S(2)}) collective-permute-start(f32[48,128]{1,0:T(8,128)S(1)} %convert_reduce_fusion.1), channel_id=1, source_target_pairs={{0,64},{64,0},{1,65},{65,1},{2,66},{66,2},{3,67},{67,3},{4,68},{68... | collective-permute-start | bytes 73736 | tf_op jit(solution)/shard_map/ppermute | solution.py:44
  86.1 39.7 %all-to-all-start.1 = ((bf16[32,176,128]{2,1,0:T(8,128)(2,1)}), bf16[32,176,128]{2,1,0:T(8,128)(2,1)S(1)}, u32[]{:S(2)}, u32[]{:S(2)}) async-start(bf16[32,176,128]{2,1,0:T(8,128)(2,1)} %broadcast_dynamic-update-slice_fusion), calls=%async_computation.1 | async-start | bytes 2883584 | tf_op jit(solution)/shard_map/all_to_all | solution.py:32
  100.5 1.8 %copy-start.2 = (bf16[1024,512]{1,0:T(8,128)(2,1)S(1)}, bf16[1024,512]{1,0:T(8,128)(2,1)}, u32[]{:S(2)}) copy-start(bf16[1024,512]{1,0:T(8,128)(2,1)} %near_ref) | copy-start | bytes 3145732
  102.8 23.0 %copy-start.3 = (bf16[128,128]{1,0:T(8,128)(2,1)S(1)}, bf16[128,128]{1,0:T(8,128)(2,1)}, u32[]{:S(2)}) copy-start(bf16[128,128]{1,0:T(8,128)(2,1)} %param.6) | copy-start | bytes 98308
  102.9 13.9 %collective-permute-start.5 = (bf16[128,512]{1,0:T(8,128)(2,1)S(1)}, bf16[128,512]{1,0:T(8,128)(2,1)S(1)}, u32[]{:S(2)}, u32[]{:S(2)}) collective-permute-start(bf16[128,512]{1,0:T(8,128)(2,1)S(1)} %get-tuple-element.34), channel_id=1, source_target_pairs={{0,0},{2,64},{4,4},{6,68},{64,2},{66,66},{68,6},{70,70},{1,1},{3,6... | collective-permute-start | bytes 393224 | tf_op jit(solution)/shard_map/ppermute | solution.py:137
  103.5 13.3 %collective-permute-start.8 = (bf16[128,512]{1,0:T(8,128)(2,1)S(1)}, bf16[128,512]{1,0:T(8,128)(2,1)S(1)}, u32[]{:S(2)}, u32[]{:S(2)}) collective-permute-start(bf16[128,512]{1,0:T(8,128)(2,1)S(1)} %get-tuple-element.35), channel_id=1, source_target_pairs={{0,68},{2,4},{4,64},{6,0},{64,70},{66,6},{68,66},{70,2},{1,69},{3,... | collective-permute-start | bytes 393224 | tf_op jit(solution)/shard_map/ppermute | solution.py:137
  110.3 11.9 %collective-permute-start.7 = (bf16[128,512]{1,0:T(8,128)(2,1)S(1)}, bf16[128,512]{1,0:T(8,128)(2,1)S(1)}, u32[]{:S(2)}, u32[]{:S(2)}) collective-permute-start(bf16[128,512]{1,0:T(8,128)(2,1)S(1)} %get-tuple-element.36), channel_id=1, source_target_pairs={{0,4},{2,68},{4,0},{6,64},{64,6},{66,70},{68,2},{70,66},{1,5},{3,6... | collective-permute-start | bytes 393224 | tf_op jit(solution)/shard_map/ppermute | solution.py:137
  114.9 7.3 %collective-permute-start.6 = (bf16[128,512]{1,0:T(8,128)(2,1)S(1)}, bf16[128,512]{1,0:T(8,128)(2,1)S(1)}, u32[]{:S(2)}, u32[]{:S(2)}) collective-permute-start(bf16[128,512]{1,0:T(8,128)(2,1)S(1)} %get-tuple-element.37), channel_id=1, source_target_pairs={{0,64},{2,0},{4,68},{6,4},{64,66},{66,2},{68,70},{70,6},{1,65},{3,... | collective-permute-start | bytes 393224 | tf_op jit(solution)/shard_map/ppermute | solution.py:137
  127.4 14.4 %all-to-all-start.2 = ((bf16[4,512,128]{1,2,0:T(8,128)(2,1)}), bf16[4,512,128]{1,2,0:T(8,128)(2,1)S(1)}, u32[]{:S(2)}, u32[]{:S(2)}) async-start(bf16[4,512,128]{1,2,0:T(8,128)(2,1)} %broadcast_in_dim.11), calls=%async_computation.2 | async-start | bytes 1048576 | tf_op jit(solution)/shard_map/all_to_all | solution.py:32
  132.8 22.6 %collective-permute-start.9 = (f32[128,128]{0,1:T(8,128)S(1)}, f32[128,128]{0,1:T(8,128)S(1)}, u32[]{:S(2)}, u32[]{:S(2)}) collective-permute-start(f32[128,128]{0,1:T(8,128)S(1)} %copy.35), channel_id=1, source_target_pairs={{0,0},{64,2},{256,4},{320,6},{128,64},{192,66},{384,68},{448,70},{... | collective-permute-start | bytes 196616 | tf_op jit(solution)/shard_map/ppermute | solution.py:150
  134.6 20.8 %copy-start.4 = (bf16[128,256]{1,0:T(8,128)(2,1)S(1)}, bf16[128,256]{1,0:T(8,128)(2,1)}, u32[]{:S(2)}) copy-start(bf16[128,256]{1,0:T(8,128)(2,1)} %param.8) | copy-start | bytes 196612
  142.2 15.2 %collective-permute-start.11 = (f32[256,512]{1,0:T(8,128)S(1)}, f32[256,512]{1,0:T(8,128)S(1)}, u32[]{:S(2)}, u32[]{:S(2)}) collective-permute-start(f32[256,512]{1,0:T(8,128)S(1)} %fusion.26), channel_id=1, source_target_pairs={{0,1},{1,0},{2,3},{3,2},{4,5},{5,4},{6,7},{7,6},{8,9},{9,8},{10,11... | collective-permute-start | bytes 1572872 | tf_op jit(solution)/shard_map/ppermute | solution.py:44
  153.5 3.2 %collective-permute-start.10 = (f32[256,128]{0,1:T(8,128)S(1)}, f32[256,128]{0,1:T(8,128)S(1)}, u32[]{:S(2)}, u32[]{:S(2)}) collective-permute-start(f32[256,128]{0,1:T(8,128)S(1)} %convert_reduce_fusion.2), channel_id=1, source_target_pairs={{0,1},{1,0},{2,3},{3,2},{4,5},{5,4},{6,7},{7,6},{8,9},{9,8},{10,11... | collective-permute-start | bytes 393224 | tf_op jit(solution)/shard_map/ppermute | solution.py:44
Sparse Core Ops, SparseCore 0:
  36.8 38.1 all-gather.2

commit v4 on v3

--- a/solution.py
+++ b/solution.py
@@ -24,6 +24,11 @@
 ]
 
 
+SPREAD = [
+    [(l * 4 + h, (h % 2) * 4 + ((h // 2 * 2 + l) ^ j)) for l in range(2) for h in range(4)] for j in range(4)
+]
+
+
 def dot(left, right, contract):
     return lax.dot_general(left, right, ((contract[0], contract[1]), ((), ())), preferred_element_type=F32)
 
@@ -44,12 +49,16 @@
     return lax.ppermute(block, axis, [(0, 1), (1, 0)])
 
 
-def slab_kernel(core_ref, near_ref, far_ref, near_beside_ref, far_beside_ref, own_ref, other_ref, out_ref):
+def slab_kernel(where_ref, near_ref, far_ref, near_beside_ref, far_beside_ref, arrived_ref, out_ref):
+    first = where_ref[1]
     block = batch = out_ref.shape[4]
 
     def write(own_weight, other_weight):
-        total = lax.dot_general(own_weight, own_ref[...], (((1,), (1,)), ((), ())), preferred_element_type=F32)
-        total += lax.dot_general(other_weight, other_ref[...], (((1,), (1,)), ((), ())), preferred_element_type=F32)
+        total = None
+        for l, weight in enumerate((own_weight, other_weight)):
+            right = jnp.concatenate([arrived_ref[first ^ l], arrived_ref[first ^ l ^ 2]], axis=0)
+            part = lax.dot_general(weight, right, (((1,), (1,)), ((), ())), preferred_element_type=F32)
+            total = part if total is None else total + part
         total = total.astype(BF16)
         for i in range(2):
             for j in range(out_ref.shape[2]):
@@ -64,20 +73,20 @@
         write(near_beside_ref[...], far_beside_ref[...])
 
 
-def slabs_of(core, own_core, other_core, own, other, extra):
-    batch = own.shape[0] // 2
+def slabs_of(core, first, own_core, other_core, arrived, extra):
+    batch = arrived.shape[1]
     block, take = batch, 4
     depth, hidden = own_core[0].shape
     steps = depth // (take * block)
     early = pl.BlockSpec((take * block, hidden), lambda s, r, _: (jnp.where(s == 0, r, steps - 1), 0))
     late = pl.BlockSpec((take * block, hidden), lambda s, r, _: (jnp.where(s == 0, 0, r), 0))
-    whole = pl.BlockSpec(own.shape, lambda s, r, _: (0, 0))
+    whole = pl.BlockSpec(arrived.shape, lambda s, r, _: (0, 0, 0))
     out = pl.pallas_call(
         slab_kernel,
         grid_spec=pltpu.PrefetchScalarGridSpec(
             num_scalar_prefetch=1,
             grid=(2, steps),
-            in_specs=[early, early, late, late, whole, whole],
+            in_specs=[early, early, late, late, whole],
             out_specs=pl.BlockSpec(
                 (2, 1, take, block + extra, batch), lambda s, r, c: (0, s ^ c[0], r, 0, 0)
             ),
@@ -86,7 +95,7 @@
         cost_estimate=pl.CostEstimate(
             flops=16 * depth * hidden * batch, bytes_accessed=8 * depth * hidden, transcendentals=0
         ),
-    )(core[None], *own_core, *other_core, own, other)
+    )(jnp.stack([core, first]), *own_core, *other_core, arrived)
     return out.reshape(4 * steps * take, block + extra, batch)
 
 
@@ -98,7 +107,6 @@
     depth, hidden = weight.shape
 
     ylo, high, core = (lax.axis_index(a) for a in ("ylo", "yhi", "core"))
-    columns = lax.all_gather(cotangent, ("yhi", "ylo"), axis=0).reshape(2, 2, 2, batch, hidden)
     moved = lax.ppermute(tokens, ("x", "ylo", "yhi"), THERE)
 
     share = jnp.concatenate(
@@ -110,17 +118,13 @@
         axis=0,
     ).astype(BF16)
     first = jnp.concatenate([to_all(moved, ("x", "z")), share.reshape(4 * n_z, -1, batch)], axis=1)
-    first, weight = lax.optimization_barrier((first, weight))
+    first, weight, later = lax.optimization_barrier((first, weight, cotangent))
     first = exchange(first, ("x", "z"))
 
     far = trade(weight, "ylo")
     own_core, other_core = (weight, far), (trade(weight, "core"), trade(far, "core"))
-    own, other = (
-        lax.dynamic_slice(columns, (0, ylo, l, 0, 0), (2, 1, 1, batch, hidden)).reshape(2 * batch, hidden)
-        for l in (ylo, 1 - ylo)
-    )
-    cotangent_column = lax.dynamic_index_in_dim(columns, ylo, 2, keepdims=False).reshape(4 * batch, hidden)
-    first, own_core, other_core, own, other = lax.optimization_barrier((first, own_core, other_core, own, other))
+    arrived = jnp.stack([lax.ppermute(later, ("ylo", "yhi"), SPREAD[j]) for j in range(4)])
+    first, own_core, other_core, arrived = lax.optimization_barrier((first, own_core, other_core, arrived))
     summed = add_up(first[:, batch:])
     beside = trade(summed, "ylo")
     panels = first[:, :batch].reshape(2, 2, n_z, batch, block)
@@ -140,13 +144,15 @@
         for j in range(4)
     )
 
-    slabs = slabs_of(core, own_core, other_core, own, other, summed.shape[0])
+    slabs = slabs_of(core, high ^ ylo, own_core, other_core, arrived, summed.shape[0])
     slabs, beside = lax.optimization_barrier((slabs, beside))
     summed = (summed + beside).astype(BF16)
     second = exchange(
         lax.dynamic_update_slice(slabs, to_all(summed, ("x", "z")), (0, block, 0)), ("x", "z")
     )
-    second, frozen = lax.optimization_barrier((second, frozen))
+    kept = [lax.dynamic_index_in_dim(arrived, high ^ ylo ^ p, 0, keepdims=False) for p in (0, 2, 1, 3)]
+    column = jnp.concatenate([*kept[:2], trade(jnp.concatenate(kept[2:]), "ylo")])
+    second, frozen, column = lax.optimization_barrier((second, frozen, column))
     gradient = lax.ppermute(add_up(second[:, :block]), ("x", "ylo", "yhi"), BACK)
     whole = second[:, block:].reshape(share.shape)
     low, along, back_low = whole[:rank], whole[rank : rank + past], whole[rank + past :]
@@ -159,11 +165,12 @@
     kept_rest = (kept - kept_high.astype(F32)).astype(BF16)
     down_part = dot(back_low, kept_high, ((1,), (1,))) + dot(back_low, kept_rest, ((1,), (1,)))
     pair = exchange(to_all(jnp.concatenate([low, down_part.astype(BF16)], axis=0), "yhi"), "yhi")
-    low_column = pair[:, :rank].transpose(1, 0, 2).reshape(rank, 4 * batch)
-    up_part = dot(low_column, cotangent_column, ((1,), (0,)))
-    grad_up = up_part + trade(up_part, "core")
-    down_part = add_up(pair[:, rank:])
-    grad_down = (down_part + trade(down_part, "core")).T
+    lows = pair[:, :rank].reshape(2, 2, rank, batch)
+    lows = [lax.dynamic_index_in_dim(lows, l, 1, keepdims=False) for l in (ylo, 1 - ylo)]
+    up_part = dot(jnp.concatenate([*lows[0], *lows[1]], axis=1), column, ((1,), (0,)))
+    ours = jnp.concatenate([up_part, add_up(pair[:, rank:])], axis=1)
+    ours = ours + trade(ours.astype(BF16), "core").astype(F32)
+    grad_up, grad_down = ours[:, :hidden], ours[:, hidden:].T
     return projection_output, token_input_gradient, grad_down, grad_up
 
 

time: 167 us -> 165 us (0.988)
  starting transfers between devices: 79.4 us -> 93 us
  between operations: 14.5 us -> 1.22 us
    ppermute x0 -> x4, starting transfers between devices: none -> 12.1 us  [local(): lax.ppermute(later, ('ylo', 'yhi'), SPREAD[j])]
    all_gather x1 -> x0, waiting for transfers between devices: 6.83 us -> none  [local(): lax.all_gather(cotangent, ('yhi', 'ylo'), axis=0)]
    ppermute x0 -> x4, waiting for transfers between devices: none -> 6.49 us  [local(): lax.ppermute(later, ('ylo', 'yhi'), SPREAD[j])]
    ppermute x6, starting transfers between devices: 28.6 us -> 32.7 us  [trade(): return lax.ppermute(block, axis, [(0, 1), (1, 0)])]
    dynamic_slice x2 -> x0, local copies, waits for them, and re-layouts: 2.93 us -> none  [the longest x1 1.86 us: local(): lax.dynamic_slice(columns, (0, ylo, l, 0, 0), (2, 1, 1, batch, hidden))]
    ppermute x4, waiting for transfers between devices: 5.33 us -> 2.42 us  [local(): lax.ppermute(lax.dynamic_index_in_dim(frozen, high ^ j ^ ylo, 0, keepdims...]
    ppermute x6, waiting for transfers between devices: 21.8 us -> 24 us  [trade(): return lax.ppermute(block, axis, [(0, 1), (1, 0)])]
  transfers between devices with their start and end apart: 16 -> 19, of which waited for: 6 -> 8; matrix products, arithmetic and copies ran while one was open for 10% -> 9% of each run, Pallas kernels for 3% -> 4%
where the time goes in v4:
time: 165 us; the launch traced here: 164 us
  starting transfers between devices  93 us (56%)
  waiting for transfers between devices  43.5 us (26%)
  matrix products  10.6 us (6%)
  Pallas kernels  6.35 us (4%)
  local copies, waits for them, and re-layouts  4.78 us (3%)
  other arithmetic  4.77 us (3%)
    all_to_all x3, starting transfers between devices, exchange(): return lax.all_to_all(pieces, axes, split_axis=0, concat_axis=0, tiled=True)  33.1 us
    ppermute x6, starting transfers between devices, trade(): return lax.ppermute(block, axis, [(0, 1), (1, 0)])  32.7 us
    ppermute x6, waiting for transfers between devices, trade(): return lax.ppermute(block, axis, [(0, 1), (1, 0)])  24 us
    ppermute x4, starting transfers between devices, local(): lax.ppermute(lax.dynamic_index_in_dim(frozen, high ^ j ^ ylo, 0, keepdims...  12.8 us
    ppermute x4, starting transfers between devices, local(): lax.ppermute(later, ('ylo', 'yhi'), SPREAD[j])  12.1 us
    all_to_all x3, waiting for transfers between devices, exchange(): return lax.all_to_all(pieces, axes, split_axis=0, concat_axis=0, tiled=True)  10.7 us
    dot_general x13, matrix products, dot(): lax.dot_general(left, right, ((contract[0], contract[1]), ((), ())), pref...  10.6 us
    ppermute x4, waiting for transfers between devices, local(): lax.ppermute(later, ('ylo', 'yhi'), SPREAD[j])  6.49 us
  transfers between devices with their start and end apart: 19, of which 8 were waited for; matrix products, arithmetic and copies ran while one was open for 9% of the time, Pallas kernels for 4%

profile of v4, /device:TPU:1, one launch (start us, length us, event | category | flops | bytes accessed | tf_op | source)
XLA Modules:
  0.0 164.3 jit_solution(4605556080373346778)
XLA Ops:
  7.0 20.4 %all-to-all-start = ((bf16[32,176,128]{2,1,0:T(8,128)(2,1)}), bf16[32,176,128]{2,1,0:T(8,128)(2,1)S(1)}, u32[]{:S(2)}, u32[]{:S(2)}) async-start(bf16[32,176,128]{2,1,0:T(8,128)(2,1)} %pad_maximum_fusion), calls=%async_computation | async-start | bytes 2883584 | tf_op jit(solution)/shard_map/all_to_all | solution.py:37
  27.4 2.3 %collective-permute-start.1 = (bf16[1024,512]{1,0:T(8,128)(2,1)S(1)}, bf16[1024,512]{1,0:T(8,128)(2,1)}, u32[]{:S(2)}, u32[]{:S(2)}) collective-permute-start(bf16[1024,512]{1,0:T(8,128)(2,1)S(1)} %copy-done.2), channel_id=1, source_target_pairs={{0,64},{64,0},{1,65},{65,1},{2,66},{66,2},{3,67},{67,3},{4,68},{68... | collective-permute-start | bytes 3145736 | tf_op jit(solution)/shard_map/ppermute | solution.py:49
  29.7 4.5 %collective-permute-start.2 = (bf16[1024,512]{1,0:T(8,128)(2,1)S(1)}, bf16[1024,512]{1,0:T(8,128)(2,1)}, u32[]{:S(2)}, u32[]{:S(2)}) collective-permute-start(bf16[1024,512]{1,0:T(8,128)(2,1)S(1)} %copy-done.2), channel_id=1, source_target_pairs={{0,1},{1,0},{2,3},{3,2},{4,5},{5,4},{6,7},{7,6},{8,9},{9,8},{10,11... | collective-permute-start | bytes 3145736 | tf_op jit(solution)/shard_map/ppermute | solution.py:49
  34.2 17.8 %collective-permute-done.1.far_ref = bf16[1024,512]{1,0:T(8,128)(2,1)} collective-permute-done((bf16[1024,512]{1,0:T(8,128)(2,1)S(1)}, bf16[1024,512]{1,0:T(8,128)(2,1)}, u32[]{:S(2)}, u32[]{:S(2)}) %collective-permute-start.1) | collective-permute-done | bytes 1048608 | tf_op jit(solution)/shard_map/ppermute | solution.py:49
  52.1 4.8 %collective-permute-start.3 = (bf16[1024,512]{1,0:T(8,128)(2,1)}, bf16[1024,512]{1,0:T(8,128)(2,1)}, u32[]{:S(2)}, u32[]{:S(2)}) collective-permute-start(bf16[1024,512]{1,0:T(8,128)(2,1)} %collective-permute-done.1.far_ref), channel_id=1, source_target_pairs={{0,1},{1,0},{2,3},{3,2},{4,5},{5,4},{6,7},{7,6},{8,9},{9,8},{10,11... | collective-permute-start | bytes 3145736 | tf_op jit(solution)/shard_map/ppermute | solution.py:49
  56.9 3.4 %collective-permute-start.7 = (bf16[128,512]{1,0:T(8,128)(2,1)S(1)}, bf16[128,512]{1,0:T(8,128)(2,1)S(1)}, u32[]{:S(2)}, u32[]{:S(2)}) collective-permute-start(bf16[128,512]{1,0:T(8,128)(2,1)S(1)} %copy-done.8), channel_id=1, source_target_pairs={{0,6},{2,70},{4,2},{6,66},{64,4},{66,68},{68,0},{70,64},{1,7},{3,7... | collective-permute-start | bytes 393224 | tf_op jit(solution)/shard_map/ppermute | solution.py:126
  60.3 5.5 %collective-permute-start.6 = (bf16[128,512]{1,0:T(8,128)(2,1)S(1)}, bf16[128,512]{1,0:T(8,128)(2,1)S(1)}, u32[]{:S(2)}, u32[]{:S(2)}) collective-permute-start(bf16[128,512]{1,0:T(8,128)(2,1)S(1)} %copy-done.8), channel_id=1, source_target_pairs={{0,4},{2,68},{4,0},{6,64},{64,6},{66,70},{68,2},{70,66},{1,5},{3,6... | collective-permute-start | bytes 393224 | tf_op jit(solution)/shard_map/ppermute | solution.py:126
  65.8 2.5 %collective-permute-start.5 = (bf16[128,512]{1,0:T(8,128)(2,1)S(1)}, bf16[128,512]{1,0:T(8,128)(2,1)S(1)}, u32[]{:S(2)}, u32[]{:S(2)}) collective-permute-start(bf16[128,512]{1,0:T(8,128)(2,1)S(1)} %copy-done.8), channel_id=1, source_target_pairs={{0,2},{2,66},{4,6},{6,70},{64,0},{66,64},{68,4},{70,68},{1,3},{3,6... | collective-permute-start | bytes 393224 | tf_op jit(solution)/shard_map/ppermute | solution.py:126
  69.6 4.5 %collective-permute-done.6 = bf16[128,512]{1,0:T(8,128)(2,1)S(1)} collective-permute-done((bf16[128,512]{1,0:T(8,128)(2,1)S(1)}, bf16[128,512]{1,0:T(8,128)(2,1)S(1)}, u32[]{:S(2)}, u32[]{:S(2)}) %collective-permute-start.6) | collective-permute-done | bytes 131104 | tf_op jit(solution)/shard_map/ppermute | solution.py:126
  74.1 2.0 %collective-permute-done.5 = bf16[128,512]{1,0:T(8,128)(2,1)S(1)} collective-permute-done((bf16[128,512]{1,0:T(8,128)(2,1)S(1)}, bf16[128,512]{1,0:T(8,128)(2,1)S(1)}, u32[]{:S(2)}, u32[]{:S(2)}) %collective-permute-start.5) | collective-permute-done | bytes 131104 | tf_op jit(solution)/shard_map/ppermute | solution.py:126
  77.0 7.2 %collective-permute-start.8 = (f32[48,128]{1,0:T(8,128)S(1)}, f32[48,128]{1,0:T(8,128)S(1)}, u32[]{:S(2)}, u32[]{:S(2)}) collective-permute-start(f32[48,128]{1,0:T(8,128)S(1)} %convert_reduce_fusion.1), channel_id=1, source_target_pairs={{0,64},{64,0},{1,65},{65,1},{2,66},{66,2},{3,67},{67,3},{4,68},{68... | collective-permute-start | bytes 73736 | tf_op jit(solution)/shard_map/ppermute | solution.py:49
  84.2 6.4 %shard_map.93 = bf16[2,2,8,176,128]{4,3,2,1,0:T(8,128)(2,1)} custom-call(s32[2]{0:T(128)} %pad_add_fusion.where_ref, bf16[1024,512]{1,0:T(8,128)(2,1)} %near_ref, bf16[1024,512]{1,0:T(8,128)(2,1)} %collective-permute-done.1.far_ref, bf16[1024,512]{1,0:T(8,128)(2,1)} %collective-permute-done.2.near_beside_ref, ...), custom_call_target="tpu_custom_call" | custom-call | flops 1073741824 | bytes 4194304 | tf_op jit(solution)/shard_map/pallas_call | solution.py:84
  91.4 9.2 %all-to-all-start.1 = ((bf16[32,176,128]{2,1,0:T(8,128)(2,1)}), bf16[32,176,128]{2,1,0:T(8,128)(2,1)S(1)}, u32[]{:S(2)}, u32[]{:S(2)}) async-start(bf16[32,176,128]{2,1,0:T(8,128)(2,1)} %broadcast_dynamic-update-slice_fusion), calls=%async_computation.1 | async-start | bytes 2883584 | tf_op jit(solution)/shard_map/all_to_all | solution.py:37
  103.3 1.7 %fusion.10 = f32[256,512]{1,0:T(8,128)S(1)} fusion(bf16[1024,512]{1,0:T(8,128)(2,1)} %collective-permute-done.2.near_beside_ref, bf16[32,8,8,128]{3,2,1,0:T(8,128)(2,1)S(1)} %bitcast.96), kind=kOutput, calls=%fused_computation.23 | convolution fusion | flops 268435456 | bytes 2097152 | tf_op jit(solution)/shard_map/dot_general | solution.py:33
  105.0 1.7 %fusion.1 = bf16[256,512]{1,0:T(8,128)(2,1)S(1)} fusion(f32[256,512]{1,0:T(8,128)S(1)} %fusion.8, bf16[1024,512]{1,0:T(8,128)(2,1)} %collective-permute-done.1.far_ref, bf16[32,8,8,128]{3,2,1,0:T(8,128)(2,1)S(1)} %bitcast.93), kind=kOutput, calls=%fused_computation.5 | convolution fusion | flops 268697600 | bytes 2359296 | tf_op jit(solution)/shard_map/dot_general | solution.py:33
  108.1 3.4 %collective-permute-start.12 = (bf16[128,512]{1,0:T(8,128)(2,1)S(1)}, bf16[128,512]{1,0:T(8,128)(2,1)S(1)}, u32[]{:S(2)}, u32[]{:S(2)}) collective-permute-start(bf16[128,512]{1,0:T(8,128)(2,1)S(1)} %get-tuple-element.63), channel_id=1, source_target_pairs={{0,68},{2,4},{4,64},{6,0},{64,70},{66,6},{68,66},{70,2},{1,69},{3,... | collective-permute-start | bytes 393224 | tf_op jit(solution)/shard_map/ppermute | solution.py:141
  111.5 6.7 %collective-permute-start.11 = (bf16[128,512]{1,0:T(8,128)(2,1)S(1)}, bf16[128,512]{1,0:T(8,128)(2,1)S(1)}, u32[]{:S(2)}, u32[]{:S(2)}) collective-permute-start(bf16[128,512]{1,0:T(8,128)(2,1)S(1)} %get-tuple-element.64), channel_id=1, source_target_pairs={{0,4},{2,68},{4,0},{6,64},{64,6},{66,70},{68,2},{70,66},{1,5},{3,6... | collective-permute-start | bytes 393224 | tf_op jit(solution)/shard_map/ppermute | solution.py:141
  118.2 1.9 %collective-permute-start.10 = (bf16[128,512]{1,0:T(8,128)(2,1)S(1)}, bf16[128,512]{1,0:T(8,128)(2,1)S(1)}, u32[]{:S(2)}, u32[]{:S(2)}) collective-permute-start(bf16[128,512]{1,0:T(8,128)(2,1)S(1)} %get-tuple-element.65), channel_id=1, source_target_pairs={{0,64},{2,0},{4,68},{6,4},{64,66},{66,2},{68,70},{70,6},{1,65},{3,... | collective-permute-start | bytes 393224 | tf_op jit(solution)/shard_map/ppermute | solution.py:141
  120.3 3.7 %collective-permute-start.13 = (bf16[256,512]{1,0:T(8,128)(2,1)S(1)}, bf16[256,512]{1,0:T(8,128)(2,1)S(1)}, u32[]{:S(2)}, u32[]{:S(2)}) collective-permute-start(bf16[256,512]{1,0:T(8,128)(2,1)S(1)} %pad_maximum_fusion.6), channel_id=1, source_target_pairs={{0,64},{64,0},{1,65},{65,1},{2,66},{66,2},{3,67},{67,3},{4,68},{68... | collective-permute-start | bytes 786440 | tf_op jit(solution)/shard_map/ppermute | solution.py:49
  124.8 1.7 %collective-permute-done.10 = bf16[128,512]{1,0:T(8,128)(2,1)S(1)} collective-permute-done((bf16[128,512]{1,0:T(8,128)(2,1)S(1)}, bf16[128,512]{1,0:T(8,128)(2,1)S(1)}, u32[]{:S(2)}, u32[]{:S(2)}) %collective-permute-start.10) | collective-permute-done | bytes 131104 | tf_op jit(solution)/shard_map/ppermute | solution.py:141
  126.5 6.1 %collective-permute-done.13 = bf16[256,512]{1,0:T(8,128)(2,1)S(1)} collective-permute-done((bf16[256,512]{1,0:T(8,128)(2,1)S(1)}, bf16[256,512]{1,0:T(8,128)(2,1)S(1)}, u32[]{:S(2)}, u32[]{:S(2)}) %collective-permute-start.13) | collective-permute-done | bytes 262176 | tf_op jit(solution)/shard_map/ppermute | solution.py:49
  136.0 3.5 %all-to-all-start.2 = ((bf16[4,512,128]{2,1,0:T(8,128)(2,1)}), bf16[4,512,128]{2,1,0:T(8,128)(2,1)S(1)}, u32[]{:S(2)}, u32[]{:S(2)}) async-start(bf16[4,512,128]{2,1,0:T(8,128)(2,1)} %broadcast_in_dim.8), calls=%async_computation.2 | async-start | bytes 1048576 | tf_op jit(solution)/shard_map/all_to_all | solution.py:37
  140.8 9.6 %all-to-all-done.2 = bf16[4,512,128]{2,1,0:T(8,128)(2,1)S(1)} async-done(((bf16[4,512,128]{2,1,0:T(8,128)(2,1)}), bf16[4,512,128]{2,1,0:T(8,128)(2,1)S(1)}, u32[]{:S(2)}, u32[]{:S(2)}) %all-to-all-start.2) | async-done | bytes 524320 | tf_op jit(solution)/shard_map/all_to_all | solution.py:37
  150.9 10.2 %collective-permute-start.15 = (bf16[256,640]{1,0:T(8,128)(2,1)S(1)}, bf16[256,640]{1,0:T(8,128)(2,1)S(1)}, u32[]{:S(2)}, u32[]{:S(2)}) collective-permute-start(bf16[256,640]{1,0:T(8,128)(2,1)S(1)} %fusion.7), channel_id=1, source_target_pairs={{0,1},{1,0},{2,3},{3,2},{4,5},{5,4},{6,7},{7,6},{8,9},{9,8},{10,11... | collective-permute-start | bytes 983048 | tf_op jit(solution)/shard_map/ppermute | solution.py:49
  (79 shorter events, 22.4 us)
Async XLA Ops:
  0.6 4.9 %collective-permute-start = (bf16[128,128]{1,0:T(8,128)(2,1)}, bf16[128,128]{1,0:T(8,128)(2,1)S(1)}, u32[]{:S(2)}, u32[]{:S(2)}) collective-permute-start(bf16[128,128]{1,0:T(8,128)(2,1)} %param.6), channel_id=1, source_target_pairs={{0,0},{2,64},{4,256},{6,320},{64,128},{66,192},{68,384},{70,448},{... | collective-permute-start | bytes 98312 | tf_op jit(solution)/shard_map/ppermute | solution.py:110
  7.0 20.4 %copy-start.2 = (bf16[1024,512]{1,0:T(8,128)(2,1)S(1)}, bf16[1024,512]{1,0:T(8,128)(2,1)}, u32[]{:S(2)}) copy-start(bf16[1024,512]{1,0:T(8,128)(2,1)} %near_ref) | copy-start | bytes 3145732
  7.0 49.9 %copy-start.8 = (bf16[128,512]{1,0:T(8,128)(2,1)S(1)}, bf16[128,512]{1,0:T(8,128)(2,1)}, u32[]{:S(2)}) copy-start(bf16[128,512]{1,0:T(8,128)(2,1)} %param.10) | copy-start | bytes 393220
  7.0 70.0 %all-to-all-start = ((bf16[32,176,128]{2,1,0:T(8,128)(2,1)}), bf16[32,176,128]{2,1,0:T(8,128)(2,1)S(1)}, u32[]{:S(2)}, u32[]{:S(2)}) async-start(bf16[32,176,128]{2,1,0:T(8,128)(2,1)} %pad_maximum_fusion), calls=%async_computation | async-start | bytes 2883584 | tf_op jit(solution)/shard_map/all_to_all | solution.py:37
  27.4 24.7 %collective-permute-start.1 = (bf16[1024,512]{1,0:T(8,128)(2,1)S(1)}, bf16[1024,512]{1,0:T(8,128)(2,1)}, u32[]{:S(2)}, u32[]{:S(2)}) collective-permute-start(bf16[1024,512]{1,0:T(8,128)(2,1)S(1)} %copy-done.2), channel_id=1, source_target_pairs={{0,64},{64,0},{1,65},{65,1},{2,66},{66,2},{3,67},{67,3},{4,68},{68... | collective-permute-start | bytes 3145736 | tf_op jit(solution)/shard_map/ppermute | solution.py:49
  29.7 47.2 %collective-permute-start.2 = (bf16[1024,512]{1,0:T(8,128)(2,1)S(1)}, bf16[1024,512]{1,0:T(8,128)(2,1)}, u32[]{:S(2)}, u32[]{:S(2)}) collective-permute-start(bf16[1024,512]{1,0:T(8,128)(2,1)S(1)} %copy-done.2), channel_id=1, source_target_pairs={{0,1},{1,0},{2,3},{3,2},{4,5},{5,4},{6,7},{7,6},{8,9},{9,8},{10,11... | collective-permute-start | bytes 3145736 | tf_op jit(solution)/shard_map/ppermute | solution.py:49
  52.1 24.9 %collective-permute-start.3 = (bf16[1024,512]{1,0:T(8,128)(2,1)}, bf16[1024,512]{1,0:T(8,128)(2,1)}, u32[]{:S(2)}, u32[]{:S(2)}) collective-permute-start(bf16[1024,512]{1,0:T(8,128)(2,1)} %collective-permute-done.1.far_ref), channel_id=1, source_target_pairs={{0,1},{1,0},{2,3},{3,2},{4,5},{5,4},{6,7},{7,6},{8,9},{9,8},{10,11... | collective-permute-start | bytes 3145736 | tf_op jit(solution)/shard_map/ppermute | solution.py:49
  56.9 11.4 %collective-permute-start.7 = (bf16[128,512]{1,0:T(8,128)(2,1)S(1)}, bf16[128,512]{1,0:T(8,128)(2,1)S(1)}, u32[]{:S(2)}, u32[]{:S(2)}) collective-permute-start(bf16[128,512]{1,0:T(8,128)(2,1)S(1)} %copy-done.8), channel_id=1, source_target_pairs={{0,6},{2,70},{4,2},{6,66},{64,4},{66,68},{68,0},{70,64},{1,7},{3,7... | collective-permute-start | bytes 393224 | tf_op jit(solution)/shard_map/ppermute | solution.py:126
  60.3 13.8 %collective-permute-start.6 = (bf16[128,512]{1,0:T(8,128)(2,1)S(1)}, bf16[128,512]{1,0:T(8,128)(2,1)S(1)}, u32[]{:S(2)}, u32[]{:S(2)}) collective-permute-start(bf16[128,512]{1,0:T(8,128)(2,1)S(1)} %copy-done.8), channel_id=1, source_target_pairs={{0,4},{2,68},{4,0},{6,64},{64,6},{66,70},{68,2},{70,66},{1,5},{3,6... | collective-permute-start | bytes 393224 | tf_op jit(solution)/shard_map/ppermute | solution.py:126
  65.8 10.3 %collective-permute-start.5 = (bf16[128,512]{1,0:T(8,128)(2,1)S(1)}, bf16[128,512]{1,0:T(8,128)(2,1)S(1)}, u32[]{:S(2)}, u32[]{:S(2)}) collective-permute-start(bf16[128,512]{1,0:T(8,128)(2,1)S(1)} %copy-done.8), channel_id=1, source_target_pairs={{0,2},{2,66},{4,6},{6,70},{64,0},{66,64},{68,4},{70,68},{1,3},{3,6... | collective-permute-start | bytes 393224 | tf_op jit(solution)/shard_map/ppermute | solution.py:126
  68.3 7.8 %collective-permute-start.4 = (bf16[128,512]{1,0:T(8,128)(2,1)S(1)}, bf16[128,512]{1,0:T(8,128)(2,1)S(1)}, u32[]{:S(2)}, u32[]{:S(2)}) collective-permute-start(bf16[128,512]{1,0:T(8,128)(2,1)S(1)} %copy-done.8), channel_id=1, source_target_pairs={{0,0},{2,64},{4,4},{6,68},{64,2},{66,66},{68,6},{70,70},{1,1},{3,6... | collective-permute-start | bytes 393224 | tf_op jit(solution)/shard_map/ppermute | solution.py:126
  77.0 13.6 %collective-permute-start.8 = (f32[48,128]{1,0:T(8,128)S(1)}, f32[48,128]{1,0:T(8,128)S(1)}, u32[]{:S(2)}, u32[]{:S(2)}) collective-permute-start(f32[48,128]{1,0:T(8,128)S(1)} %convert_reduce_fusion.1), channel_id=1, source_target_pairs={{0,64},{64,0},{1,65},{65,1},{2,66},{66,2},{3,67},{67,3},{4,68},{68... | collective-permute-start | bytes 73736 | tf_op jit(solution)/shard_map/ppermute | solution.py:49
  91.4 43.1 %all-to-all-start.1 = ((bf16[32,176,128]{2,1,0:T(8,128)(2,1)}), bf16[32,176,128]{2,1,0:T(8,128)(2,1)S(1)}, u32[]{:S(2)}, u32[]{:S(2)}) async-start(bf16[32,176,128]{2,1,0:T(8,128)(2,1)} %broadcast_dynamic-update-slice_fusion), calls=%async_computation.1 | async-start | bytes 2883584 | tf_op jit(solution)/shard_map/all_to_all | solution.py:37
  107.2 13.0 %copy-start.1 = (bf16[4,128,512]{2,1,0:T(8,128)(2,1)S(1)}, bf16[4,128,512]{2,1,0:T(8,128)(2,1)}, u32[]{:S(2)}) copy-start(bf16[4,128,512]{2,1,0:T(8,128)(2,1)} %pad_maximum_fusion.2.arrived_ref) | copy-start | bytes 1572868
  107.3 16.7 %collective-permute-start.9 = (bf16[128,512]{1,0:T(8,128)(2,1)S(1)}, bf16[128,512]{1,0:T(8,128)(2,1)S(1)}, u32[]{:S(2)}, u32[]{:S(2)}) collective-permute-start(bf16[128,512]{1,0:T(8,128)(2,1)S(1)} %get-tuple-element.62), channel_id=1, source_target_pairs={{0,0},{2,64},{4,4},{6,68},{64,2},{66,66},{68,6},{70,70},{1,1},{3,6... | collective-permute-start | bytes 393224 | tf_op jit(solution)/shard_map/ppermute | solution.py:141
  108.1 15.9 %collective-permute-start.12 = (bf16[128,512]{1,0:T(8,128)(2,1)S(1)}, bf16[128,512]{1,0:T(8,128)(2,1)S(1)}, u32[]{:S(2)}, u32[]{:S(2)}) collective-permute-start(bf16[128,512]{1,0:T(8,128)(2,1)S(1)} %get-tuple-element.63), channel_id=1, source_target_pairs={{0,68},{2,4},{4,64},{6,0},{64,70},{66,6},{68,66},{70,2},{1,69},{3,... | collective-permute-start | bytes 393224 | tf_op jit(solution)/shard_map/ppermute | solution.py:141
  111.5 13.3 %collective-permute-start.11 = (bf16[128,512]{1,0:T(8,128)(2,1)S(1)}, bf16[128,512]{1,0:T(8,128)(2,1)S(1)}, u32[]{:S(2)}, u32[]{:S(2)}) collective-permute-start(bf16[128,512]{1,0:T(8,128)(2,1)S(1)} %get-tuple-element.64), channel_id=1, source_target_pairs={{0,4},{2,68},{4,0},{6,64},{64,6},{66,70},{68,2},{70,66},{1,5},{3,6... | collective-permute-start | bytes 393224 | tf_op jit(solution)/shard_map/ppermute | solution.py:141
  118.2 8.2 %collective-permute-start.10 = (bf16[128,512]{1,0:T(8,128)(2,1)S(1)}, bf16[128,512]{1,0:T(8,128)(2,1)S(1)}, u32[]{:S(2)}, u32[]{:S(2)}) collective-permute-start(bf16[128,512]{1,0:T(8,128)(2,1)S(1)} %get-tuple-element.65), channel_id=1, source_target_pairs={{0,64},{2,0},{4,68},{6,4},{64,66},{66,2},{68,70},{70,6},{1,65},{3,... | collective-permute-start | bytes 393224 | tf_op jit(solution)/shard_map/ppermute | solution.py:141
  120.3 14.3 %copy-start.6 = (bf16[128,128]{1,0:T(8,128)(2,1)S(1)}, bf16[128,128]{1,0:T(8,128)(2,1)}, u32[]{:S(2)}) copy-start(bf16[128,128]{1,0:T(8,128)(2,1)} %param.6) | copy-start | bytes 98308
  120.3 12.4 %collective-permute-start.13 = (bf16[256,512]{1,0:T(8,128)(2,1)S(1)}, bf16[256,512]{1,0:T(8,128)(2,1)S(1)}, u32[]{:S(2)}, u32[]{:S(2)}) collective-permute-start(bf16[256,512]{1,0:T(8,128)(2,1)S(1)} %pad_maximum_fusion.6), channel_id=1, source_target_pairs={{0,64},{64,0},{1,65},{65,1},{2,66},{66,2},{3,67},{67,3},{4,68},{68... | collective-permute-start | bytes 786440 | tf_op jit(solution)/shard_map/ppermute | solution.py:49
  136.0 14.4 %all-to-all-start.2 = ((bf16[4,512,128]{2,1,0:T(8,128)(2,1)}), bf16[4,512,128]{2,1,0:T(8,128)(2,1)S(1)}, u32[]{:S(2)}, u32[]{:S(2)}) async-start(bf16[4,512,128]{2,1,0:T(8,128)(2,1)} %broadcast_in_dim.8), calls=%async_computation.2 | async-start | bytes 1048576 | tf_op jit(solution)/shard_map/all_to_all | solution.py:37
  139.8 22.0 %collective-permute-start.14 = (f32[128,128]{0,1:T(8,128)S(1)}, f32[128,128]{0,1:T(8,128)S(1)}, u32[]{:S(2)}, u32[]{:S(2)}) collective-permute-start(f32[128,128]{0,1:T(8,128)S(1)} %copy.32), channel_id=1, source_target_pairs={{0,0},{64,2},{256,4},{320,6},{128,64},{192,66},{384,68},{448,70},{... | collective-permute-start | bytes 196616 | tf_op jit(solution)/shard_map/ppermute | solution.py:156
  150.5 11.3 %copy-start.7 = (bf16[128,256]{1,0:T(8,128)(2,1)S(1)}, bf16[128,256]{1,0:T(8,128)(2,1)}, u32[]{:S(2)}) copy-start(bf16[128,256]{1,0:T(8,128)(2,1)} %param.8) | copy-start | bytes 196612
  150.9 11.7 %collective-permute-start.15 = (bf16[256,640]{1,0:T(8,128)(2,1)S(1)}, bf16[256,640]{1,0:T(8,128)(2,1)S(1)}, u32[]{:S(2)}, u32[]{:S(2)}) collective-permute-start(bf16[256,640]{1,0:T(8,128)(2,1)S(1)} %fusion.7), channel_id=1, source_target_pairs={{0,1},{1,0},{2,3},{3,2},{4,5},{5,4},{6,7},{7,6},{8,9},{9,8},{10,11... | collective-permute-start | bytes 983048 | tf_op jit(solution)/shard_map/ppermute | solution.py:49
  (4 other events, 20.6 us)

commit v5 on v4

--- a/solution.py
+++ b/solution.py
@@ -121,9 +121,11 @@
     first, weight, later = lax.optimization_barrier((first, weight, cotangent))
     first = exchange(first, ("x", "z"))
 
+    arrived = [lax.ppermute(later, ("ylo", "yhi"), SPREAD[j]) for j in range(4)]
     far = trade(weight, "ylo")
+    far, arrived = lax.optimization_barrier((far, arrived))
     own_core, other_core = (weight, far), (trade(weight, "core"), trade(far, "core"))
-    arrived = jnp.stack([lax.ppermute(later, ("ylo", "yhi"), SPREAD[j]) for j in range(4)])
+    arrived = jnp.stack(arrived)
     first, own_core, other_core, arrived = lax.optimization_barrier((first, own_core, other_core, arrived))
     summed = add_up(first[:, batch:])
     beside = trade(summed, "ylo")

time: 165 us -> 158 us (0.958)
  starting transfers between devices: 93 us -> 88.8 us
  waiting for transfers between devices: 43.5 us -> 39.6 us
    ppermute x6, waiting for transfers between devices: 24 us -> 6.67 us  [trade(): return lax.ppermute(block, axis, [(0, 1), (1, 0)])]
    ppermute x4, waiting for transfers between devices: 6.49 us -> 14.6 us  [local(): arrived = [lax.ppermute(later, ('ylo', 'yhi'), SPREAD[j]) for j in range(4)]]
    ppermute x6, starting transfers between devices: 32.7 us -> 25.9 us  [trade(): return lax.ppermute(block, axis, [(0, 1), (1, 0)])]
    ppermute x4, waiting for transfers between devices: 2.42 us -> 5.6 us  [local(): lax.ppermute(lax.dynamic_index_in_dim(frozen, high ^ j ^ ylo, 0, keepdims...]
    all_to_all x3, waiting for transfers between devices: 10.7 us -> 12.8 us  [exchange(): return lax.all_to_all(pieces, axes, split_axis=0, concat_axis=0, tiled=True)]
  transfers between devices with their start and end apart: 19 -> 19, of which waited for: 8 -> 7; matrix products, arithmetic and copies ran while one was open for 9% -> 9% of each run, Pallas kernels for 4% -> 4%
where the time goes in v5:
time: 158 us; the launch traced here: 156 us
  starting transfers between devices  88.8 us (56%)
  waiting for transfers between devices  39.6 us (25%)
  matrix products  10.6 us (7%)
  Pallas kernels  6.35 us (4%)
  local copies, waits for them, and re-layouts  4.78 us (3%)
  other arithmetic  4.77 us (3%)
    all_to_all x3, starting transfers between devices, exchange(): return lax.all_to_all(pieces, axes, split_axis=0, concat_axis=0, tiled=True)  34.3 us
    ppermute x6, starting transfers between devices, trade(): return lax.ppermute(block, axis, [(0, 1), (1, 0)])  25.9 us
    ppermute x4, waiting for transfers between devices, local(): arrived = [lax.ppermute(later, ('ylo', 'yhi'), SPREAD[j]) for j in range(4)]  14.6 us
    ppermute x4, starting transfers between devices, local(): lax.ppermute(lax.dynamic_index_in_dim(frozen, high ^ j ^ ylo, 0, keepdims...  13.7 us
    all_to_all x3, waiting for transfers between devices, exchange(): return lax.all_to_all(pieces, axes, split_axis=0, concat_axis=0, tiled=True)  12.8 us
    ppermute x4, starting transfers between devices, local(): arrived = [lax.ppermute(later, ('ylo', 'yhi'), SPREAD[j]) for j in range(4)]  12.5 us
    dot_general x13, matrix products, dot(): lax.dot_general(left, right, ((contract[0], contract[1]), ((), ())), pref...  10.6 us
    ppermute x6, waiting for transfers between devices, trade(): return lax.ppermute(block, axis, [(0, 1), (1, 0)])  6.67 us
  transfers between devices with their start and end apart: 19, of which 7 were waited for; matrix products, arithmetic and copies ran while one was open for 9% of the time, Pallas kernels for 4%

profile of v5, /device:TPU:1, one launch (start us, length us, event | category | flops | bytes accessed | tf_op | source)
XLA Modules:
  0.0 156.2 jit_solution(9000028037446560664)
XLA Ops:
  7.0 20.4 %all-to-all-start = ((bf16[32,176,128]{2,1,0:T(8,128)(2,1)}), bf16[32,176,128]{2,1,0:T(8,128)(2,1)S(1)}, u32[]{:S(2)}, u32[]{:S(2)}) async-start(bf16[32,176,128]{2,1,0:T(8,128)(2,1)} %pad_maximum_fusion), calls=%async_computation | async-start | bytes 2883584 | tf_op jit(solution)/shard_map/all_to_all | solution.py:37
  27.4 2.3 %collective-permute-start.1 = (bf16[1024,512]{1,0:T(8,128)(2,1)S(1)}, bf16[1024,512]{1,0:T(8,128)(2,1)}, u32[]{:S(2)}, u32[]{:S(2)}) collective-permute-start(bf16[1024,512]{1,0:T(8,128)(2,1)S(1)} %copy-done.2), channel_id=1, source_target_pairs={{0,64},{64,0},{1,65},{65,1},{2,66},{66,2},{3,67},{67,3},{4,68},{68... | collective-permute-start | bytes 3145736 | tf_op jit(solution)/shard_map/ppermute | solution.py:49
  29.7 4.3 %collective-permute-start.5 = (bf16[128,512]{1,0:T(8,128)(2,1)S(1)}, bf16[128,512]{1,0:T(8,128)(2,1)S(1)}, u32[]{:S(2)}, u32[]{:S(2)}) collective-permute-start(bf16[128,512]{1,0:T(8,128)(2,1)S(1)} %copy-done.8), channel_id=1, source_target_pairs={{0,6},{2,70},{4,2},{6,66},{64,4},{66,68},{68,0},{70,64},{1,7},{3,7... | collective-permute-start | bytes 393224 | tf_op jit(solution)/shard_map/ppermute | solution.py:124
  34.0 5.7 %collective-permute-start.4 = (bf16[128,512]{1,0:T(8,128)(2,1)S(1)}, bf16[128,512]{1,0:T(8,128)(2,1)S(1)}, u32[]{:S(2)}, u32[]{:S(2)}) collective-permute-start(bf16[128,512]{1,0:T(8,128)(2,1)S(1)} %copy-done.8), channel_id=1, source_target_pairs={{0,4},{2,68},{4,0},{6,64},{64,6},{66,70},{68,2},{70,66},{1,5},{3,6... | collective-permute-start | bytes 393224 | tf_op jit(solution)/shard_map/ppermute | solution.py:124
  39.7 1.9 %collective-permute-start.3 = (bf16[128,512]{1,0:T(8,128)(2,1)S(1)}, bf16[128,512]{1,0:T(8,128)(2,1)S(1)}, u32[]{:S(2)}, u32[]{:S(2)}) collective-permute-start(bf16[128,512]{1,0:T(8,128)(2,1)S(1)} %copy-done.8), channel_id=1, source_target_pairs={{0,2},{2,66},{4,6},{6,70},{64,0},{66,64},{68,4},{70,68},{1,3},{3,6... | collective-permute-start | bytes 393224 | tf_op jit(solution)/shard_map/ppermute | solution.py:124
  42.3 4.9 %collective-permute-start.6 = (bf16[1024,512]{1,0:T(8,128)(2,1)S(1)}, bf16[1024,512]{1,0:T(8,128)(2,1)}, u32[]{:S(2)}, u32[]{:S(2)}) collective-permute-start(bf16[1024,512]{1,0:T(8,128)(2,1)S(1)} %copy-done.2), channel_id=1, source_target_pairs={{0,1},{1,0},{2,3},{3,2},{4,5},{5,4},{6,7},{7,6},{8,9},{9,8},{10,11... | collective-permute-start | bytes 3145736 | tf_op jit(solution)/shard_map/ppermute | solution.py:49
  47.2 12.1 %collective-permute-done.4 = bf16[128,512]{1,0:T(8,128)(2,1)S(1)} collective-permute-done((bf16[128,512]{1,0:T(8,128)(2,1)S(1)}, bf16[128,512]{1,0:T(8,128)(2,1)S(1)}, u32[]{:S(2)}, u32[]{:S(2)}) %collective-permute-start.4) | collective-permute-done | bytes 131104 | tf_op jit(solution)/shard_map/ppermute | solution.py:124
  59.3 2.5 %collective-permute-done.3 = bf16[128,512]{1,0:T(8,128)(2,1)S(1)} collective-permute-done((bf16[128,512]{1,0:T(8,128)(2,1)S(1)}, bf16[128,512]{1,0:T(8,128)(2,1)S(1)}, u32[]{:S(2)}, u32[]{:S(2)}) %collective-permute-start.3) | collective-permute-done | bytes 131104 | tf_op jit(solution)/shard_map/ppermute | solution.py:124
  61.8 6.2 %collective-permute-start.7 = (bf16[1024,512]{1,0:T(8,128)(2,1)}, bf16[1024,512]{1,0:T(8,128)(2,1)}, u32[]{:S(2)}, u32[]{:S(2)}) collective-permute-start(bf16[1024,512]{1,0:T(8,128)(2,1)} %collective-permute-done.1.far_ref), channel_id=1, source_target_pairs={{0,1},{1,0},{2,3},{3,2},{4,5},{5,4},{6,7},{7,6},{8,9},{9,8},{10,11... | collective-permute-start | bytes 3145736 | tf_op jit(solution)/shard_map/ppermute | solution.py:49
  70.7 3.7 %collective-permute-start.8 = (f32[48,128]{1,0:T(8,128)S(1)}, f32[48,128]{1,0:T(8,128)S(1)}, u32[]{:S(2)}, u32[]{:S(2)}) collective-permute-start(f32[48,128]{1,0:T(8,128)S(1)} %convert_reduce_fusion.1), channel_id=1, source_target_pairs={{0,64},{64,0},{1,65},{65,1},{2,66},{66,2},{3,67},{67,3},{4,68},{68... | collective-permute-start | bytes 73736 | tf_op jit(solution)/shard_map/ppermute | solution.py:49
  74.4 6.4 %shard_map.93 = bf16[2,2,8,176,128]{4,3,2,1,0:T(8,128)(2,1)} custom-call(s32[2]{0:T(128)} %pad_add_fusion.where_ref, bf16[1024,512]{1,0:T(8,128)(2,1)} %near_ref, bf16[1024,512]{1,0:T(8,128)(2,1)} %collective-permute-done.1.far_ref, bf16[1024,512]{1,0:T(8,128)(2,1)} %collective-permute-done.6.near_beside_ref, ...), custom_call_target="tpu_custom_call" | custom-call | flops 1073741824 | bytes 4194304 | tf_op jit(solution)/shard_map/pallas_call | solution.py:84
  81.6 9.2 %all-to-all-start.1 = ((bf16[32,176,128]{2,1,0:T(8,128)(2,1)}), bf16[32,176,128]{2,1,0:T(8,128)(2,1)S(1)}, u32[]{:S(2)}, u32[]{:S(2)}) async-start(bf16[32,176,128]{2,1,0:T(8,128)(2,1)} %broadcast_dynamic-update-slice_fusion), calls=%async_computation.1 | async-start | bytes 2883584 | tf_op jit(solution)/shard_map/all_to_all | solution.py:37
  91.8 1.7 %fusion.8 = f32[256,512]{1,0:T(8,128)S(1)} fusion(bf16[1024,512]{1,0:T(8,128)(2,1)} %collective-permute-done.7.far_beside_ref, bf16[32,8,8,128]{3,2,1,0:T(8,128)(2,1)S(1)} %bitcast.95), kind=kOutput, calls=%fused_computation.21 | convolution fusion | flops 268435456 | bytes 2097152 | tf_op jit(solution)/shard_map/dot_general | solution.py:33
  93.5 1.7 %fusion.10 = f32[256,512]{1,0:T(8,128)S(1)} fusion(bf16[1024,512]{1,0:T(8,128)(2,1)} %collective-permute-done.6.near_beside_ref, bf16[32,8,8,128]{3,2,1,0:T(8,128)(2,1)S(1)} %bitcast.96), kind=kOutput, calls=%fused_computation.23 | convolution fusion | flops 268435456 | bytes 2097152 | tf_op jit(solution)/shard_map/dot_general | solution.py:33
  95.1 1.7 %fusion.1 = bf16[256,512]{1,0:T(8,128)(2,1)S(1)} fusion(f32[256,512]{1,0:T(8,128)S(1)} %fusion.8, bf16[1024,512]{1,0:T(8,128)(2,1)} %collective-permute-done.1.far_ref, bf16[32,8,8,128]{3,2,1,0:T(8,128)(2,1)S(1)} %bitcast.93), kind=kOutput, calls=%fused_computation.5 | convolution fusion | flops 268697600 | bytes 2359296 | tf_op jit(solution)/shard_map/dot_general | solution.py:33
  98.3 5.3 %collective-permute-start.12 = (bf16[128,512]{1,0:T(8,128)(2,1)S(1)}, bf16[128,512]{1,0:T(8,128)(2,1)S(1)}, u32[]{:S(2)}, u32[]{:S(2)}) collective-permute-start(bf16[128,512]{1,0:T(8,128)(2,1)S(1)} %get-tuple-element.73), channel_id=1, source_target_pairs={{0,68},{2,4},{4,64},{6,0},{64,70},{66,6},{68,66},{70,2},{1,69},{3,... | collective-permute-start | bytes 393224 | tf_op jit(solution)/shard_map/ppermute | solution.py:143
  103.6 5.7 %collective-permute-start.11 = (bf16[128,512]{1,0:T(8,128)(2,1)S(1)}, bf16[128,512]{1,0:T(8,128)(2,1)S(1)}, u32[]{:S(2)}, u32[]{:S(2)}) collective-permute-start(bf16[128,512]{1,0:T(8,128)(2,1)S(1)} %get-tuple-element.74), channel_id=1, source_target_pairs={{0,4},{2,68},{4,0},{6,64},{64,6},{66,70},{68,2},{70,66},{1,5},{3,6... | collective-permute-start | bytes 393224 | tf_op jit(solution)/shard_map/ppermute | solution.py:143
  109.3 1.9 %collective-permute-start.10 = (bf16[128,512]{1,0:T(8,128)(2,1)S(1)}, bf16[128,512]{1,0:T(8,128)(2,1)S(1)}, u32[]{:S(2)}, u32[]{:S(2)}) collective-permute-start(bf16[128,512]{1,0:T(8,128)(2,1)S(1)} %get-tuple-element.75), channel_id=1, source_target_pairs={{0,64},{2,0},{4,68},{6,4},{64,66},{66,2},{68,70},{70,6},{1,65},{3,... | collective-permute-start | bytes 393224 | tf_op jit(solution)/shard_map/ppermute | solution.py:143
  111.3 3.1 %collective-permute-start.13 = (bf16[256,512]{1,0:T(8,128)(2,1)S(1)}, bf16[256,512]{1,0:T(8,128)(2,1)S(1)}, u32[]{:S(2)}, u32[]{:S(2)}) collective-permute-start(bf16[256,512]{1,0:T(8,128)(2,1)S(1)} %pad_maximum_fusion.6), channel_id=1, source_target_pairs={{0,64},{64,0},{1,65},{65,1},{2,66},{66,2},{3,67},{67,3},{4,68},{68... | collective-permute-start | bytes 786440 | tf_op jit(solution)/shard_map/ppermute | solution.py:49
  114.4 4.6 %collective-permute-done.11 = bf16[128,512]{1,0:T(8,128)(2,1)S(1)} collective-permute-done((bf16[128,512]{1,0:T(8,128)(2,1)S(1)}, bf16[128,512]{1,0:T(8,128)(2,1)S(1)}, u32[]{:S(2)}, u32[]{:S(2)}) %collective-permute-start.11) | collective-permute-done | bytes 131104 | tf_op jit(solution)/shard_map/ppermute | solution.py:143
  120.1 5.5 %collective-permute-done.13 = bf16[256,512]{1,0:T(8,128)(2,1)S(1)} collective-permute-done((bf16[256,512]{1,0:T(8,128)(2,1)S(1)}, bf16[256,512]{1,0:T(8,128)(2,1)S(1)}, u32[]{:S(2)}, u32[]{:S(2)}) %collective-permute-start.13) | collective-permute-done | bytes 262176 | tf_op jit(solution)/shard_map/ppermute | solution.py:49
  128.0 4.7 %all-to-all-start.2 = ((bf16[4,512,128]{2,1,0:T(8,128)(2,1)}), bf16[4,512,128]{2,1,0:T(8,128)(2,1)S(1)}, u32[]{:S(2)}, u32[]{:S(2)}) async-start(bf16[4,512,128]{2,1,0:T(8,128)(2,1)} %broadcast_in_dim.8), calls=%async_computation.2 | async-start | bytes 1048576 | tf_op jit(solution)/shard_map/all_to_all | solution.py:37
  134.0 12.8 %all-to-all-done.2 = bf16[4,512,128]{2,1,0:T(8,128)(2,1)S(1)} async-done(((bf16[4,512,128]{2,1,0:T(8,128)(2,1)}), bf16[4,512,128]{2,1,0:T(8,128)(2,1)S(1)}, u32[]{:S(2)}, u32[]{:S(2)}) %all-to-all-start.2) | async-done | bytes 524320 | tf_op jit(solution)/shard_map/all_to_all | solution.py:37
  147.2 5.7 %collective-permute-start.15 = (bf16[256,640]{1,0:T(8,128)(2,1)S(1)}, bf16[256,640]{1,0:T(8,128)(2,1)S(1)}, u32[]{:S(2)}, u32[]{:S(2)}) collective-permute-start(bf16[256,640]{1,0:T(8,128)(2,1)S(1)} %fusion.7), channel_id=1, source_target_pairs={{0,1},{1,0},{2,3},{3,2},{4,5},{5,4},{6,7},{7,6},{8,9},{9,8},{10,11... | collective-permute-start | bytes 983048 | tf_op jit(solution)/shard_map/ppermute | solution.py:49
  (79 shorter events, 21.1 us)
Async XLA Ops:
  0.6 4.9 %collective-permute-start = (bf16[128,128]{1,0:T(8,128)(2,1)}, bf16[128,128]{1,0:T(8,128)(2,1)S(1)}, u32[]{:S(2)}, u32[]{:S(2)}) collective-permute-start(bf16[128,128]{1,0:T(8,128)(2,1)} %param.6), channel_id=1, source_target_pairs={{0,0},{2,64},{4,256},{6,320},{64,128},{66,192},{68,384},{70,448},{... | collective-permute-start | bytes 98312 | tf_op jit(solution)/shard_map/ppermute | solution.py:110
  7.0 20.4 %copy-start.2 = (bf16[1024,512]{1,0:T(8,128)(2,1)S(1)}, bf16[1024,512]{1,0:T(8,128)(2,1)}, u32[]{:S(2)}) copy-start(bf16[1024,512]{1,0:T(8,128)(2,1)} %near_ref) | copy-start | bytes 3145732
  7.0 22.7 %copy-start.8 = (bf16[128,512]{1,0:T(8,128)(2,1)S(1)}, bf16[128,512]{1,0:T(8,128)(2,1)}, u32[]{:S(2)}) copy-start(bf16[128,512]{1,0:T(8,128)(2,1)} %param.10) | copy-start | bytes 393220
  7.0 63.6 %all-to-all-start = ((bf16[32,176,128]{2,1,0:T(8,128)(2,1)}), bf16[32,176,128]{2,1,0:T(8,128)(2,1)S(1)}, u32[]{:S(2)}, u32[]{:S(2)}) async-start(bf16[32,176,128]{2,1,0:T(8,128)(2,1)} %pad_maximum_fusion), calls=%async_computation | async-start | bytes 2883584 | tf_op jit(solution)/shard_map/all_to_all | solution.py:37
  27.4 34.4 %collective-permute-start.1 = (bf16[1024,512]{1,0:T(8,128)(2,1)S(1)}, bf16[1024,512]{1,0:T(8,128)(2,1)}, u32[]{:S(2)}, u32[]{:S(2)}) collective-permute-start(bf16[1024,512]{1,0:T(8,128)(2,1)S(1)} %copy-done.2), channel_id=1, source_target_pairs={{0,64},{64,0},{1,65},{65,1},{2,66},{66,2},{3,67},{67,3},{4,68},{68... | collective-permute-start | bytes 3145736 | tf_op jit(solution)/shard_map/ppermute | solution.py:49
  29.7 12.6 %collective-permute-start.5 = (bf16[128,512]{1,0:T(8,128)(2,1)S(1)}, bf16[128,512]{1,0:T(8,128)(2,1)S(1)}, u32[]{:S(2)}, u32[]{:S(2)}) collective-permute-start(bf16[128,512]{1,0:T(8,128)(2,1)S(1)} %copy-done.8), channel_id=1, source_target_pairs={{0,6},{2,70},{4,2},{6,66},{64,4},{66,68},{68,0},{70,64},{1,7},{3,7... | collective-permute-start | bytes 393224 | tf_op jit(solution)/shard_map/ppermute | solution.py:124
  34.0 25.3 %collective-permute-start.4 = (bf16[128,512]{1,0:T(8,128)(2,1)S(1)}, bf16[128,512]{1,0:T(8,128)(2,1)S(1)}, u32[]{:S(2)}, u32[]{:S(2)}) collective-permute-start(bf16[128,512]{1,0:T(8,128)(2,1)S(1)} %copy-done.8), channel_id=1, source_target_pairs={{0,4},{2,68},{4,0},{6,64},{64,6},{66,70},{68,2},{70,66},{1,5},{3,6... | collective-permute-start | bytes 393224 | tf_op jit(solution)/shard_map/ppermute | solution.py:124
  39.7 22.1 %collective-permute-start.3 = (bf16[128,512]{1,0:T(8,128)(2,1)S(1)}, bf16[128,512]{1,0:T(8,128)(2,1)S(1)}, u32[]{:S(2)}, u32[]{:S(2)}) collective-permute-start(bf16[128,512]{1,0:T(8,128)(2,1)S(1)} %copy-done.8), channel_id=1, source_target_pairs={{0,2},{2,66},{4,6},{6,70},{64,0},{66,64},{68,4},{70,68},{1,3},{3,6... | collective-permute-start | bytes 393224 | tf_op jit(solution)/shard_map/ppermute | solution.py:124
  41.6 20.2 %collective-permute-start.2 = (bf16[128,512]{1,0:T(8,128)(2,1)S(1)}, bf16[128,512]{1,0:T(8,128)(2,1)S(1)}, u32[]{:S(2)}, u32[]{:S(2)}) collective-permute-start(bf16[128,512]{1,0:T(8,128)(2,1)S(1)} %copy-done.8), channel_id=1, source_target_pairs={{0,0},{2,64},{4,4},{6,68},{64,2},{66,66},{68,6},{70,70},{1,1},{3,6... | collective-permute-start | bytes 393224 | tf_op jit(solution)/shard_map/ppermute | solution.py:124
  42.3 27.2 %collective-permute-start.6 = (bf16[1024,512]{1,0:T(8,128)(2,1)S(1)}, bf16[1024,512]{1,0:T(8,128)(2,1)}, u32[]{:S(2)}, u32[]{:S(2)}) collective-permute-start(bf16[1024,512]{1,0:T(8,128)(2,1)S(1)} %copy-done.2), channel_id=1, source_target_pairs={{0,1},{1,0},{2,3},{3,2},{4,5},{5,4},{6,7},{7,6},{8,9},{9,8},{10,11... | collective-permute-start | bytes 3145736 | tf_op jit(solution)/shard_map/ppermute | solution.py:49
  61.8 8.8 %collective-permute-start.7 = (bf16[1024,512]{1,0:T(8,128)(2,1)}, bf16[1024,512]{1,0:T(8,128)(2,1)}, u32[]{:S(2)}, u32[]{:S(2)}) collective-permute-start(bf16[1024,512]{1,0:T(8,128)(2,1)} %collective-permute-done.1.far_ref), channel_id=1, source_target_pairs={{0,1},{1,0},{2,3},{3,2},{4,5},{5,4},{6,7},{7,6},{8,9},{9,8},{10,11... | collective-permute-start | bytes 3145736 | tf_op jit(solution)/shard_map/ppermute | solution.py:49
  70.7 10.0 %collective-permute-start.8 = (f32[48,128]{1,0:T(8,128)S(1)}, f32[48,128]{1,0:T(8,128)S(1)}, u32[]{:S(2)}, u32[]{:S(2)}) collective-permute-start(f32[48,128]{1,0:T(8,128)S(1)} %convert_reduce_fusion.1), channel_id=1, source_target_pairs={{0,64},{64,0},{1,65},{65,1},{2,66},{66,2},{3,67},{67,3},{4,68},{68... | collective-permute-start | bytes 73736 | tf_op jit(solution)/shard_map/ppermute | solution.py:49
  81.6 44.9 %all-to-all-start.1 = ((bf16[32,176,128]{2,1,0:T(8,128)(2,1)}), bf16[32,176,128]{2,1,0:T(8,128)(2,1)S(1)}, u32[]{:S(2)}, u32[]{:S(2)}) async-start(bf16[32,176,128]{2,1,0:T(8,128)(2,1)} %broadcast_dynamic-update-slice_fusion), calls=%async_computation.1 | async-start | bytes 2883584 | tf_op jit(solution)/shard_map/all_to_all | solution.py:37
  97.4 13.9 %copy-start.1 = (bf16[4,128,512]{2,1,0:T(8,128)(2,1)S(1)}, bf16[4,128,512]{2,1,0:T(8,128)(2,1)}, u32[]{:S(2)}) copy-start(bf16[4,128,512]{2,1,0:T(8,128)(2,1)} %pad_maximum_fusion.2.arrived_ref) | copy-start | bytes 1572868
  97.5 16.9 %collective-permute-start.9 = (bf16[128,512]{1,0:T(8,128)(2,1)S(1)}, bf16[128,512]{1,0:T(8,128)(2,1)S(1)}, u32[]{:S(2)}, u32[]{:S(2)}) collective-permute-start(bf16[128,512]{1,0:T(8,128)(2,1)S(1)} %get-tuple-element.72), channel_id=1, source_target_pairs={{0,0},{2,64},{4,4},{6,68},{64,2},{66,66},{68,6},{70,70},{1,1},{3,6... | collective-permute-start | bytes 393224 | tf_op jit(solution)/shard_map/ppermute | solution.py:143
  98.3 16.1 %collective-permute-start.12 = (bf16[128,512]{1,0:T(8,128)(2,1)S(1)}, bf16[128,512]{1,0:T(8,128)(2,1)S(1)}, u32[]{:S(2)}, u32[]{:S(2)}) collective-permute-start(bf16[128,512]{1,0:T(8,128)(2,1)S(1)} %get-tuple-element.73), channel_id=1, source_target_pairs={{0,68},{2,4},{4,64},{6,0},{64,70},{66,6},{68,66},{70,2},{1,69},{3,... | collective-permute-start | bytes 393224 | tf_op jit(solution)/shard_map/ppermute | solution.py:143
  103.6 15.4 %collective-permute-start.11 = (bf16[128,512]{1,0:T(8,128)(2,1)S(1)}, bf16[128,512]{1,0:T(8,128)(2,1)S(1)}, u32[]{:S(2)}, u32[]{:S(2)}) collective-permute-start(bf16[128,512]{1,0:T(8,128)(2,1)S(1)} %get-tuple-element.74), channel_id=1, source_target_pairs={{0,4},{2,68},{4,0},{6,64},{64,6},{66,70},{68,2},{70,66},{1,5},{3,6... | collective-permute-start | bytes 393224 | tf_op jit(solution)/shard_map/ppermute | solution.py:143
  109.3 10.7 %collective-permute-start.10 = (bf16[128,512]{1,0:T(8,128)(2,1)S(1)}, bf16[128,512]{1,0:T(8,128)(2,1)S(1)}, u32[]{:S(2)}, u32[]{:S(2)}) collective-permute-start(bf16[128,512]{1,0:T(8,128)(2,1)S(1)} %get-tuple-element.75), channel_id=1, source_target_pairs={{0,64},{2,0},{4,68},{6,4},{64,66},{66,2},{68,70},{70,6},{1,65},{3,... | collective-permute-start | bytes 393224 | tf_op jit(solution)/shard_map/ppermute | solution.py:143
  111.3 15.2 %copy-start.6 = (bf16[128,128]{1,0:T(8,128)(2,1)S(1)}, bf16[128,128]{1,0:T(8,128)(2,1)}, u32[]{:S(2)}) copy-start(bf16[128,128]{1,0:T(8,128)(2,1)} %param.6) | copy-start | bytes 98308
  111.3 14.3 %collective-permute-start.13 = (bf16[256,512]{1,0:T(8,128)(2,1)S(1)}, bf16[256,512]{1,0:T(8,128)(2,1)S(1)}, u32[]{:S(2)}, u32[]{:S(2)}) collective-permute-start(bf16[256,512]{1,0:T(8,128)(2,1)S(1)} %pad_maximum_fusion.6), channel_id=1, source_target_pairs={{0,64},{64,0},{1,65},{65,1},{2,66},{66,2},{3,67},{67,3},{4,68},{68... | collective-permute-start | bytes 786440 | tf_op jit(solution)/shard_map/ppermute | solution.py:49
  128.0 18.8 %all-to-all-start.2 = ((bf16[4,512,128]{2,1,0:T(8,128)(2,1)}), bf16[4,512,128]{2,1,0:T(8,128)(2,1)S(1)}, u32[]{:S(2)}, u32[]{:S(2)}) async-start(bf16[4,512,128]{2,1,0:T(8,128)(2,1)} %broadcast_in_dim.8), calls=%async_computation.2 | async-start | bytes 1048576 | tf_op jit(solution)/shard_map/all_to_all | solution.py:37
  132.9 13.9 %copy-start.5 = (bf16[512,512]{1,0:T(8,128)(2,1)S(1)}, bf16[512,512]{1,0:T(8,128)(2,1)}, u32[]{:S(2)}) copy-start(bf16[512,512]{1,0:T(8,128)(2,1)} %pad_maximum_fusion.4) | copy-start | bytes 1572868
  133.0 20.7 %collective-permute-start.14 = (f32[128,128]{0,1:T(8,128)S(1)}, f32[128,128]{0,1:T(8,128)S(1)}, u32[]{:S(2)}, u32[]{:S(2)}) collective-permute-start(f32[128,128]{0,1:T(8,128)S(1)} %copy.32), channel_id=1, source_target_pairs={{0,0},{64,2},{256,4},{320,6},{128,64},{192,66},{384,68},{448,70},{... | collective-permute-start | bytes 196616 | tf_op jit(solution)/shard_map/ppermute | solution.py:158
  147.2 7.3 %collective-permute-start.15 = (bf16[256,640]{1,0:T(8,128)(2,1)S(1)}, bf16[256,640]{1,0:T(8,128)(2,1)S(1)}, u32[]{:S(2)}, u32[]{:S(2)}) collective-permute-start(bf16[256,640]{1,0:T(8,128)(2,1)S(1)} %fusion.7), channel_id=1, source_target_pairs={{0,1},{1,0},{2,3},{3,2},{4,5},{5,4},{6,7},{7,6},{8,9},{9,8},{10,11... | collective-permute-start | bytes 983048 | tf_op jit(solution)/shard_map/ppermute | solution.py:49
  (4 other events, 17.9 us)

commit v6 on v5

--- a/solution.py
+++ b/solution.py
@@ -139,6 +139,9 @@
         for i in range(2)
     ]
     frozen = jnp.stack([f.reshape(2, batch, hidden) for f in frozen], axis=1).reshape(4, batch, hidden)
+    kept = [lax.dynamic_index_in_dim(arrived, high ^ ylo ^ p, 0, keepdims=False) for p in (0, 2, 1, 3)]
+    column = jnp.concatenate([*kept[:2], trade(jnp.concatenate(kept[2:]), "ylo")])
+    frozen, column = lax.optimization_barrier((frozen, column))
     frozen = sum(
         lax.ppermute(
             lax.dynamic_index_in_dim(frozen, high ^ j ^ ylo, 0, keepdims=False), ("ylo", "yhi"), HOME[j]
@@ -152,9 +155,7 @@
     second = exchange(
         lax.dynamic_update_slice(slabs, to_all(summed, ("x", "z")), (0, block, 0)), ("x", "z")
     )
-    kept = [lax.dynamic_index_in_dim(arrived, high ^ ylo ^ p, 0, keepdims=False) for p in (0, 2, 1, 3)]
-    column = jnp.concatenate([*kept[:2], trade(jnp.concatenate(kept[2:]), "ylo")])
-    second, frozen, column = lax.optimization_barrier((second, frozen, column))
+    second, frozen = lax.optimization_barrier((second, frozen))
     gradient = lax.ppermute(add_up(second[:, :block]), ("x", "ylo", "yhi"), BACK)
     whole = second[:, block:].reshape(share.shape)
     low, along, back_low = whole[:rank], whole[rank : rank + past], whole[rank + past :]

time: 158 us -> 157 us (level)
  waiting for transfers between devices: 39.6 us -> 34.9 us
  starting transfers between devices: 88.8 us -> 91.4 us
    ppermute x6, waiting for transfers between devices: 6.67 us -> 2.05 us  [trade(): return lax.ppermute(block, axis, [(0, 1), (1, 0)])]
    all_to_all x3, waiting for transfers between devices: 12.8 us -> 9.36 us  [exchange(): return lax.all_to_all(pieces, axes, split_axis=0, concat_axis=0, tiled=True)]
    ppermute x4, waiting for transfers between devices: 5.6 us -> 8.86 us  [local(): lax.ppermute(lax.dynamic_index_in_dim(frozen, high ^ j ^ ylo, 0, keepdims...]
    ppermute x6, starting transfers between devices: 25.9 us -> 29 us  [trade(): return lax.ppermute(block, axis, [(0, 1), (1, 0)])]
  transfers between devices with their start and end apart: 19 -> 19, of which waited for: 7 -> 8; matrix products, arithmetic and copies ran while one was open for 9% -> 9% of each run, Pallas kernels for 4% -> 4%
where the time goes in v6:
time: 157 us; the launch traced here: 155 us
  starting transfers between devices  91.4 us (58%)
  waiting for transfers between devices  34.9 us (22%)
  matrix products  10.6 us (7%)
  Pallas kernels  6.35 us (4%)
  local copies, waits for them, and re-layouts  5.32 us (3%)
  other arithmetic  4.77 us (3%)
    all_to_all x3, starting transfers between devices, exchange(): return lax.all_to_all(pieces, axes, split_axis=0, concat_axis=0, tiled=True)  34 us
    ppermute x6, starting transfers between devices, trade(): return lax.ppermute(block, axis, [(0, 1), (1, 0)])  29 us
    ppermute x4, waiting for transfers between devices, local(): arrived = [lax.ppermute(later, ('ylo', 'yhi'), SPREAD[j]) for j in range(4)]  14.6 us
    ppermute x4, starting transfers between devices, local(): lax.ppermute(lax.dynamic_index_in_dim(frozen, high ^ j ^ ylo, 0, keepdims...  13.6 us
    ppermute x4, starting transfers between devices, local(): arrived = [lax.ppermute(later, ('ylo', 'yhi'), SPREAD[j]) for j in range(4)]  12.5 us
    dot_general x13, matrix products, dot(): lax.dot_general(left, right, ((contract[0], contract[1]), ((), ())), pref...  10.6 us
    all_to_all x3, waiting for transfers between devices, exchange(): return lax.all_to_all(pieces, axes, split_axis=0, concat_axis=0, tiled=True)  9.36 us
    ppermute x4, waiting for transfers between devices, local(): lax.ppermute(lax.dynamic_index_in_dim(frozen, high ^ j ^ ylo, 0, keepdims...  8.86 us
  transfers between devices with their start and end apart: 19, of which 8 were waited for; matrix products, arithmetic and copies ran while one was open for 9% of the time, Pallas kernels for 4%

profile of v6, /device:TPU:1, one launch (start us, length us, event | category | flops | bytes accessed | tf_op | source)
XLA Modules:
  0.0 154.5 jit_solution(5891305240104533716)
XLA Ops:
  0.6 1.5 %collective-permute-start = (bf16[128,128]{1,0:T(8,128)(2,1)}, bf16[128,128]{1,0:T(8,128)(2,1)S(1)}, u32[]{:S(2)}, u32[]{:S(2)}) collective-permute-start(bf16[128,128]{1,0:T(8,128)(2,1)} %param.6), channel_id=1, source_target_pairs={{0,0},{2,64},{4,256},{6,320},{64,128},{66,192},{68,384},{70,448},{... | collective-permute-start | bytes 98312 | tf_op jit(solution)/shard_map/ppermute | solution.py:110
  7.0 20.4 %all-to-all-start = ((bf16[32,176,128]{2,1,0:T(8,128)(2,1)}), bf16[32,176,128]{2,1,0:T(8,128)(2,1)S(1)}, u32[]{:S(2)}, u32[]{:S(2)}) async-start(bf16[32,176,128]{2,1,0:T(8,128)(2,1)} %pad_maximum_fusion), calls=%async_computation | async-start | bytes 2883584 | tf_op jit(solution)/shard_map/all_to_all | solution.py:37
  27.4 2.3 %collective-permute-start.1 = (bf16[1024,512]{1,0:T(8,128)(2,1)S(1)}, bf16[1024,512]{1,0:T(8,128)(2,1)}, u32[]{:S(2)}, u32[]{:S(2)}) collective-permute-start(bf16[1024,512]{1,0:T(8,128)(2,1)S(1)} %copy-done.2), channel_id=1, source_target_pairs={{0,64},{64,0},{1,65},{65,1},{2,66},{66,2},{3,67},{67,3},{4,68},{68... | collective-permute-start | bytes 3145736 | tf_op jit(solution)/shard_map/ppermute | solution.py:49
  29.7 4.3 %collective-permute-start.5 = (bf16[128,512]{1,0:T(8,128)(2,1)S(1)}, bf16[128,512]{1,0:T(8,128)(2,1)S(1)}, u32[]{:S(2)}, u32[]{:S(2)}) collective-permute-start(bf16[128,512]{1,0:T(8,128)(2,1)S(1)} %copy-done.8), channel_id=1, source_target_pairs={{0,6},{2,70},{4,2},{6,66},{64,4},{66,68},{68,0},{70,64},{1,7},{3,7... | collective-permute-start | bytes 393224 | tf_op jit(solution)/shard_map/ppermute | solution.py:124
  34.0 5.7 %collective-permute-start.4 = (bf16[128,512]{1,0:T(8,128)(2,1)S(1)}, bf16[128,512]{1,0:T(8,128)(2,1)S(1)}, u32[]{:S(2)}, u32[]{:S(2)}) collective-permute-start(bf16[128,512]{1,0:T(8,128)(2,1)S(1)} %copy-done.8), channel_id=1, source_target_pairs={{0,4},{2,68},{4,0},{6,64},{64,6},{66,70},{68,2},{70,66},{1,5},{3,6... | collective-permute-start | bytes 393224 | tf_op jit(solution)/shard_map/ppermute | solution.py:124
  39.7 1.9 %collective-permute-start.3 = (bf16[128,512]{1,0:T(8,128)(2,1)S(1)}, bf16[128,512]{1,0:T(8,128)(2,1)S(1)}, u32[]{:S(2)}, u32[]{:S(2)}) collective-permute-start(bf16[128,512]{1,0:T(8,128)(2,1)S(1)} %copy-done.8), channel_id=1, source_target_pairs={{0,2},{2,66},{4,6},{6,70},{64,0},{66,64},{68,4},{70,68},{1,3},{3,6... | collective-permute-start | bytes 393224 | tf_op jit(solution)/shard_map/ppermute | solution.py:124
  42.3 4.9 %collective-permute-start.6 = (bf16[1024,512]{1,0:T(8,128)(2,1)S(1)}, bf16[1024,512]{1,0:T(8,128)(2,1)}, u32[]{:S(2)}, u32[]{:S(2)}) collective-permute-start(bf16[1024,512]{1,0:T(8,128)(2,1)S(1)} %copy-done.2), channel_id=1, source_target_pairs={{0,1},{1,0},{2,3},{3,2},{4,5},{5,4},{6,7},{7,6},{8,9},{9,8},{10,11... | collective-permute-start | bytes 3145736 | tf_op jit(solution)/shard_map/ppermute | solution.py:49
  47.2 12.1 %collective-permute-done.4 = bf16[128,512]{1,0:T(8,128)(2,1)S(1)} collective-permute-done((bf16[128,512]{1,0:T(8,128)(2,1)S(1)}, bf16[128,512]{1,0:T(8,128)(2,1)S(1)}, u32[]{:S(2)}, u32[]{:S(2)}) %collective-permute-start.4) | collective-permute-done | bytes 131104 | tf_op jit(solution)/shard_map/ppermute | solution.py:124
  59.3 2.5 %collective-permute-done.3 = bf16[128,512]{1,0:T(8,128)(2,1)S(1)} collective-permute-done((bf16[128,512]{1,0:T(8,128)(2,1)S(1)}, bf16[128,512]{1,0:T(8,128)(2,1)S(1)}, u32[]{:S(2)}, u32[]{:S(2)}) %collective-permute-start.3) | collective-permute-done | bytes 131104 | tf_op jit(solution)/shard_map/ppermute | solution.py:124
  61.8 6.2 %collective-permute-start.7 = (bf16[1024,512]{1,0:T(8,128)(2,1)}, bf16[1024,512]{1,0:T(8,128)(2,1)}, u32[]{:S(2)}, u32[]{:S(2)}) collective-permute-start(bf16[1024,512]{1,0:T(8,128)(2,1)} %collective-permute-done.1.far_ref), channel_id=1, source_target_pairs={{0,1},{1,0},{2,3},{3,2},{4,5},{5,4},{6,7},{7,6},{8,9},{9,8},{10,11... | collective-permute-start | bytes 3145736 | tf_op jit(solution)/shard_map/ppermute | solution.py:49
  70.7 3.7 %collective-permute-start.8 = (f32[48,128]{1,0:T(8,128)S(1)}, f32[48,128]{1,0:T(8,128)S(1)}, u32[]{:S(2)}, u32[]{:S(2)}) collective-permute-start(f32[48,128]{1,0:T(8,128)S(1)} %convert_reduce_fusion.1), channel_id=1, source_target_pairs={{0,64},{64,0},{1,65},{65,1},{2,66},{66,2},{3,67},{67,3},{4,68},{68... | collective-permute-start | bytes 73736 | tf_op jit(solution)/shard_map/ppermute | solution.py:49
  74.4 6.4 %shard_map.93 = bf16[2,2,8,176,128]{4,3,2,1,0:T(8,128)(2,1)} custom-call(s32[2]{0:T(128)} %pad_add_fusion.where_ref, bf16[1024,512]{1,0:T(8,128)(2,1)} %near_ref, bf16[1024,512]{1,0:T(8,128)(2,1)} %collective-permute-done.1.far_ref, bf16[1024,512]{1,0:T(8,128)(2,1)} %collective-permute-done.6.near_beside_ref, ...), custom_call_target="tpu_custom_call" | custom-call | flops 1073741824 | bytes 4194304 | tf_op jit(solution)/shard_map/pallas_call | solution.py:84
  81.6 9.2 %all-to-all-start.1 = ((bf16[32,176,128]{2,1,0:T(8,128)(2,1)}), bf16[32,176,128]{2,1,0:T(8,128)(2,1)S(1)}, u32[]{:S(2)}, u32[]{:S(2)}) async-start(bf16[32,176,128]{2,1,0:T(8,128)(2,1)} %broadcast_dynamic-update-slice_fusion), calls=%async_computation.1 | async-start | bytes 2883584 | tf_op jit(solution)/shard_map/all_to_all | solution.py:37
  92.1 1.9 %collective-permute-start.9 = (bf16[256,512]{1,0:T(8,128)(2,1)S(1)}, bf16[256,512]{1,0:T(8,128)(2,1)S(1)}, u32[]{:S(2)}, u32[]{:S(2)}) collective-permute-start(bf16[256,512]{1,0:T(8,128)(2,1)S(1)} %pad_maximum_fusion.6), channel_id=1, source_target_pairs={{0,64},{64,0},{1,65},{65,1},{2,66},{66,2},{3,67},{67,3},{4,68},{68... | collective-permute-start | bytes 786440 | tf_op jit(solution)/shard_map/ppermute | solution.py:49
  94.4 1.7 %fusion.8 = f32[256,512]{1,0:T(8,128)S(1)} fusion(bf16[1024,512]{1,0:T(8,128)(2,1)} %collective-permute-done.7.far_beside_ref, bf16[32,8,8,128]{3,2,1,0:T(8,128)(2,1)S(1)} %bitcast.95), kind=kOutput, calls=%fused_computation.21 | convolution fusion | flops 268435456 | bytes 2097152 | tf_op jit(solution)/shard_map/dot_general | solution.py:33
  96.1 1.7 %fusion.10 = f32[256,512]{1,0:T(8,128)S(1)} fusion(bf16[1024,512]{1,0:T(8,128)(2,1)} %collective-permute-done.6.near_beside_ref, bf16[32,8,8,128]{3,2,1,0:T(8,128)(2,1)S(1)} %bitcast.96), kind=kOutput, calls=%fused_computation.23 | convolution fusion | flops 268435456 | bytes 2097152 | tf_op jit(solution)/shard_map/dot_general | solution.py:33
  97.7 1.7 %fusion.1 = bf16[256,512]{1,0:T(8,128)(2,1)S(1)} fusion(f32[256,512]{1,0:T(8,128)S(1)} %fusion.8, bf16[1024,512]{1,0:T(8,128)(2,1)} %collective-permute-done.1.far_ref, bf16[32,8,8,128]{3,2,1,0:T(8,128)(2,1)S(1)} %bitcast.93), kind=kOutput, calls=%fused_computation.5 | convolution fusion | flops 268697600 | bytes 2359296 | tf_op jit(solution)/shard_map/dot_general | solution.py:33
  102.5 5.6 %collective-permute-start.13 = (bf16[128,512]{1,0:T(8,128)(2,1)S(1)}, bf16[128,512]{1,0:T(8,128)(2,1)S(1)}, u32[]{:S(2)}, u32[]{:S(2)}) collective-permute-start(bf16[128,512]{1,0:T(8,128)(2,1)S(1)} %get-tuple-element.71), channel_id=1, source_target_pairs={{0,68},{2,4},{4,64},{6,0},{64,70},{66,6},{68,66},{70,2},{1,69},{3,... | collective-permute-start | bytes 393224 | tf_op jit(solution)/shard_map/ppermute | solution.py:146
  108.1 5.4 %collective-permute-start.12 = (bf16[128,512]{1,0:T(8,128)(2,1)S(1)}, bf16[128,512]{1,0:T(8,128)(2,1)S(1)}, u32[]{:S(2)}, u32[]{:S(2)}) collective-permute-start(bf16[128,512]{1,0:T(8,128)(2,1)S(1)} %get-tuple-element.72), channel_id=1, source_target_pairs={{0,4},{2,68},{4,0},{6,64},{64,6},{66,70},{68,2},{70,66},{1,5},{3,6... | collective-permute-start | bytes 393224 | tf_op jit(solution)/shard_map/ppermute | solution.py:146
  113.5 1.9 %collective-permute-start.11 = (bf16[128,512]{1,0:T(8,128)(2,1)S(1)}, bf16[128,512]{1,0:T(8,128)(2,1)S(1)}, u32[]{:S(2)}, u32[]{:S(2)}) collective-permute-start(bf16[128,512]{1,0:T(8,128)(2,1)S(1)} %get-tuple-element.73), channel_id=1, source_target_pairs={{0,64},{2,0},{4,68},{6,4},{64,66},{66,2},{68,70},{70,6},{1,65},{3,... | collective-permute-start | bytes 393224 | tf_op jit(solution)/shard_map/ppermute | solution.py:146
  115.4 8.1 %collective-permute-done.12 = bf16[128,512]{1,0:T(8,128)(2,1)S(1)} collective-permute-done((bf16[128,512]{1,0:T(8,128)(2,1)S(1)}, bf16[128,512]{1,0:T(8,128)(2,1)S(1)}, u32[]{:S(2)}, u32[]{:S(2)}) %collective-permute-start.12) | collective-permute-done | bytes 131104 | tf_op jit(solution)/shard_map/ppermute | solution.py:146
  126.4 4.4 %all-to-all-start.2 = ((bf16[4,512,128]{2,1,0:T(8,128)(2,1)}), bf16[4,512,128]{2,1,0:T(8,128)(2,1)S(1)}, u32[]{:S(2)}, u32[]{:S(2)}) async-start(bf16[4,512,128]{2,1,0:T(8,128)(2,1)} %broadcast_in_dim.8), calls=%async_computation.2 | async-start | bytes 1048576 | tf_op jit(solution)/shard_map/all_to_all | solution.py:37
  132.1 8.8 %all-to-all-done.2 = bf16[4,512,128]{2,1,0:T(8,128)(2,1)S(1)} async-done(((bf16[4,512,128]{2,1,0:T(8,128)(2,1)}), bf16[4,512,128]{2,1,0:T(8,128)(2,1)S(1)}, u32[]{:S(2)}, u32[]{:S(2)}) %all-to-all-start.2) | async-done | bytes 524320 | tf_op jit(solution)/shard_map/all_to_all | solution.py:37
  141.3 10.0 %collective-permute-start.15 = (bf16[256,640]{1,0:T(8,128)(2,1)S(1)}, bf16[256,640]{1,0:T(8,128)(2,1)S(1)}, u32[]{:S(2)}, u32[]{:S(2)}) collective-permute-start(bf16[256,640]{1,0:T(8,128)(2,1)S(1)} %fusion.7), channel_id=1, source_target_pairs={{0,1},{1,0},{2,3},{3,2},{4,5},{5,4},{6,7},{7,6},{8,9},{9,8},{10,11... | collective-permute-start | bytes 983048 | tf_op jit(solution)/shard_map/ppermute | solution.py:49
  (79 shorter events, 21.1 us)
Async XLA Ops:
  0.6 4.9 %collective-permute-start = (bf16[128,128]{1,0:T(8,128)(2,1)}, bf16[128,128]{1,0:T(8,128)(2,1)S(1)}, u32[]{:S(2)}, u32[]{:S(2)}) collective-permute-start(bf16[128,128]{1,0:T(8,128)(2,1)} %param.6), channel_id=1, source_target_pairs={{0,0},{2,64},{4,256},{6,320},{64,128},{66,192},{68,384},{70,448},{... | collective-permute-start | bytes 98312 | tf_op jit(solution)/shard_map/ppermute | solution.py:110
  7.0 20.4 %copy-start.2 = (bf16[1024,512]{1,0:T(8,128)(2,1)S(1)}, bf16[1024,512]{1,0:T(8,128)(2,1)}, u32[]{:S(2)}) copy-start(bf16[1024,512]{1,0:T(8,128)(2,1)} %near_ref) | copy-start | bytes 3145732
  7.0 22.7 %copy-start.8 = (bf16[128,512]{1,0:T(8,128)(2,1)S(1)}, bf16[128,512]{1,0:T(8,128)(2,1)}, u32[]{:S(2)}) copy-start(bf16[128,512]{1,0:T(8,128)(2,1)} %param.10) | copy-start | bytes 393220
  7.0 63.6 %all-to-all-start = ((bf16[32,176,128]{2,1,0:T(8,128)(2,1)}), bf16[32,176,128]{2,1,0:T(8,128)(2,1)S(1)}, u32[]{:S(2)}, u32[]{:S(2)}) async-start(bf16[32,176,128]{2,1,0:T(8,128)(2,1)} %pad_maximum_fusion), calls=%async_computation | async-start | bytes 2883584 | tf_op jit(solution)/shard_map/all_to_all | solution.py:37
  27.4 34.4 %collective-permute-start.1 = (bf16[1024,512]{1,0:T(8,128)(2,1)S(1)}, bf16[1024,512]{1,0:T(8,128)(2,1)}, u32[]{:S(2)}, u32[]{:S(2)}) collective-permute-start(bf16[1024,512]{1,0:T(8,128)(2,1)S(1)} %copy-done.2), channel_id=1, source_target_pairs={{0,64},{64,0},{1,65},{65,1},{2,66},{66,2},{3,67},{67,3},{4,68},{68... | collective-permute-start | bytes 3145736 | tf_op jit(solution)/shard_map/ppermute | solution.py:49
  29.7 12.6 %collective-permute-start.5 = (bf16[128,512]{1,0:T(8,128)(2,1)S(1)}, bf16[128,512]{1,0:T(8,128)(2,1)S(1)}, u32[]{:S(2)}, u32[]{:S(2)}) collective-permute-start(bf16[128,512]{1,0:T(8,128)(2,1)S(1)} %copy-done.8), channel_id=1, source_target_pairs={{0,6},{2,70},{4,2},{6,66},{64,4},{66,68},{68,0},{70,64},{1,7},{3,7... | collective-permute-start | bytes 393224 | tf_op jit(solution)/shard_map/ppermute | solution.py:124
  34.0 25.3 %collective-permute-start.4 = (bf16[128,512]{1,0:T(8,128)(2,1)S(1)}, bf16[128,512]{1,0:T(8,128)(2,1)S(1)}, u32[]{:S(2)}, u32[]{:S(2)}) collective-permute-start(bf16[128,512]{1,0:T(8,128)(2,1)S(1)} %copy-done.8), channel_id=1, source_target_pairs={{0,4},{2,68},{4,0},{6,64},{64,6},{66,70},{68,2},{70,66},{1,5},{3,6... | collective-permute-start | bytes 393224 | tf_op jit(solution)/shard_map/ppermute | solution.py:124
  39.7 22.1 %collective-permute-start.3 = (bf16[128,512]{1,0:T(8,128)(2,1)S(1)}, bf16[128,512]{1,0:T(8,128)(2,1)S(1)}, u32[]{:S(2)}, u32[]{:S(2)}) collective-permute-start(bf16[128,512]{1,0:T(8,128)(2,1)S(1)} %copy-done.8), channel_id=1, source_target_pairs={{0,2},{2,66},{4,6},{6,70},{64,0},{66,64},{68,4},{70,68},{1,3},{3,6... | collective-permute-start | bytes 393224 | tf_op jit(solution)/shard_map/ppermute | solution.py:124
  41.6 20.2 %collective-permute-start.2 = (bf16[128,512]{1,0:T(8,128)(2,1)S(1)}, bf16[128,512]{1,0:T(8,128)(2,1)S(1)}, u32[]{:S(2)}, u32[]{:S(2)}) collective-permute-start(bf16[128,512]{1,0:T(8,128)(2,1)S(1)} %copy-done.8), channel_id=1, source_target_pairs={{0,0},{2,64},{4,4},{6,68},{64,2},{66,66},{68,6},{70,70},{1,1},{3,6... | collective-permute-start | bytes 393224 | tf_op jit(solution)/shard_map/ppermute | solution.py:124
  42.3 27.2 %collective-permute-start.6 = (bf16[1024,512]{1,0:T(8,128)(2,1)S(1)}, bf16[1024,512]{1,0:T(8,128)(2,1)}, u32[]{:S(2)}, u32[]{:S(2)}) collective-permute-start(bf16[1024,512]{1,0:T(8,128)(2,1)S(1)} %copy-done.2), channel_id=1, source_target_pairs={{0,1},{1,0},{2,3},{3,2},{4,5},{5,4},{6,7},{7,6},{8,9},{9,8},{10,11... | collective-permute-start | bytes 3145736 | tf_op jit(solution)/shard_map/ppermute | solution.py:49
  61.8 8.8 %collective-permute-start.7 = (bf16[1024,512]{1,0:T(8,128)(2,1)}, bf16[1024,512]{1,0:T(8,128)(2,1)}, u32[]{:S(2)}, u32[]{:S(2)}) collective-permute-start(bf16[1024,512]{1,0:T(8,128)(2,1)} %collective-permute-done.1.far_ref), channel_id=1, source_target_pairs={{0,1},{1,0},{2,3},{3,2},{4,5},{5,4},{6,7},{7,6},{8,9},{9,8},{10,11... | collective-permute-start | bytes 3145736 | tf_op jit(solution)/shard_map/ppermute | solution.py:49
  70.7 10.0 %collective-permute-start.8 = (f32[48,128]{1,0:T(8,128)S(1)}, f32[48,128]{1,0:T(8,128)S(1)}, u32[]{:S(2)}, u32[]{:S(2)}) collective-permute-start(f32[48,128]{1,0:T(8,128)S(1)} %convert_reduce_fusion.1), channel_id=1, source_target_pairs={{0,64},{64,0},{1,65},{65,1},{2,66},{66,2},{3,67},{67,3},{4,68},{68... | collective-permute-start | bytes 73736 | tf_op jit(solution)/shard_map/ppermute | solution.py:49
  81.6 43.3 %all-to-all-start.1 = ((bf16[32,176,128]{2,1,0:T(8,128)(2,1)}), bf16[32,176,128]{2,1,0:T(8,128)(2,1)S(1)}, u32[]{:S(2)}, u32[]{:S(2)}) async-start(bf16[32,176,128]{2,1,0:T(8,128)(2,1)} %broadcast_dynamic-update-slice_fusion), calls=%async_computation.1 | async-start | bytes 2883584 | tf_op jit(solution)/shard_map/all_to_all | solution.py:37
  92.1 8.8 %collective-permute-start.9 = (bf16[256,512]{1,0:T(8,128)(2,1)S(1)}, bf16[256,512]{1,0:T(8,128)(2,1)S(1)}, u32[]{:S(2)}, u32[]{:S(2)}) collective-permute-start(bf16[256,512]{1,0:T(8,128)(2,1)S(1)} %pad_maximum_fusion.6), channel_id=1, source_target_pairs={{0,64},{64,0},{1,65},{65,1},{2,66},{66,2},{3,67},{67,3},{4,68},{68... | collective-permute-start | bytes 786440 | tf_op jit(solution)/shard_map/ppermute | solution.py:49
  101.7 23.2 %copy-start.6 = (bf16[128,128]{1,0:T(8,128)(2,1)S(1)}, bf16[128,128]{1,0:T(8,128)(2,1)}, u32[]{:S(2)}) copy-start(bf16[128,128]{1,0:T(8,128)(2,1)} %param.6) | copy-start | bytes 98308
  101.8 13.6 %collective-permute-start.10 = (bf16[128,512]{1,0:T(8,128)(2,1)S(1)}, bf16[128,512]{1,0:T(8,128)(2,1)S(1)}, u32[]{:S(2)}, u32[]{:S(2)}) collective-permute-start(bf16[128,512]{1,0:T(8,128)(2,1)S(1)} %get-tuple-element.70), channel_id=1, source_target_pairs={{0,0},{2,64},{4,4},{6,68},{64,2},{66,66},{68,6},{70,70},{1,1},{3,6... | collective-permute-start | bytes 393224 | tf_op jit(solution)/shard_map/ppermute | solution.py:146
  102.5 12.9 %collective-permute-start.13 = (bf16[128,512]{1,0:T(8,128)(2,1)S(1)}, bf16[128,512]{1,0:T(8,128)(2,1)S(1)}, u32[]{:S(2)}, u32[]{:S(2)}) collective-permute-start(bf16[128,512]{1,0:T(8,128)(2,1)S(1)} %get-tuple-element.71), channel_id=1, source_target_pairs={{0,68},{2,4},{4,64},{6,0},{64,70},{66,6},{68,66},{70,2},{1,69},{3,... | collective-permute-start | bytes 393224 | tf_op jit(solution)/shard_map/ppermute | solution.py:146
  108.1 15.5 %collective-permute-start.12 = (bf16[128,512]{1,0:T(8,128)(2,1)S(1)}, bf16[128,512]{1,0:T(8,128)(2,1)S(1)}, u32[]{:S(2)}, u32[]{:S(2)}) collective-permute-start(bf16[128,512]{1,0:T(8,128)(2,1)S(1)} %get-tuple-element.72), channel_id=1, source_target_pairs={{0,4},{2,68},{4,0},{6,64},{64,6},{66,70},{68,2},{70,66},{1,5},{3,6... | collective-permute-start | bytes 393224 | tf_op jit(solution)/shard_map/ppermute | solution.py:146
  113.5 10.8 %collective-permute-start.11 = (bf16[128,512]{1,0:T(8,128)(2,1)S(1)}, bf16[128,512]{1,0:T(8,128)(2,1)S(1)}, u32[]{:S(2)}, u32[]{:S(2)}) collective-permute-start(bf16[128,512]{1,0:T(8,128)(2,1)S(1)} %get-tuple-element.73), channel_id=1, source_target_pairs={{0,64},{2,0},{4,68},{6,4},{64,66},{66,2},{68,70},{70,6},{1,65},{3,... | collective-permute-start | bytes 393224 | tf_op jit(solution)/shard_map/ppermute | solution.py:146
  126.4 14.4 %all-to-all-start.2 = ((bf16[4,512,128]{2,1,0:T(8,128)(2,1)}), bf16[4,512,128]{2,1,0:T(8,128)(2,1)S(1)}, u32[]{:S(2)}, u32[]{:S(2)}) async-start(bf16[4,512,128]{2,1,0:T(8,128)(2,1)} %broadcast_in_dim.8), calls=%async_computation.2 | async-start | bytes 1048576 | tf_op jit(solution)/shard_map/all_to_all | solution.py:37
  131.0 10.0 %copy-start.5 = (bf16[512,512]{1,0:T(8,128)(2,1)S(1)}, bf16[512,512]{1,0:T(8,128)(2,1)}, u32[]{:S(2)}) copy-start(bf16[512,512]{1,0:T(8,128)(2,1)} %pad_maximum_fusion.4) | copy-start | bytes 1572868
  131.1 20.9 %collective-permute-start.14 = (f32[128,128]{0,1:T(8,128)S(1)}, f32[128,128]{0,1:T(8,128)S(1)}, u32[]{:S(2)}, u32[]{:S(2)}) collective-permute-start(f32[128,128]{0,1:T(8,128)S(1)} %copy.32), channel_id=1, source_target_pairs={{0,0},{64,2},{256,4},{320,6},{128,64},{192,66},{384,68},{448,70},{... | collective-permute-start | bytes 196616 | tf_op jit(solution)/shard_map/ppermute | solution.py:159
  140.9 11.1 %copy-start.7 = (bf16[128,256]{1,0:T(8,128)(2,1)S(1)}, bf16[128,256]{1,0:T(8,128)(2,1)}, u32[]{:S(2)}) copy-start(bf16[128,256]{1,0:T(8,128)(2,1)} %param.8) | copy-start | bytes 196612
  141.3 11.5 %collective-permute-start.15 = (bf16[256,640]{1,0:T(8,128)(2,1)S(1)}, bf16[256,640]{1,0:T(8,128)(2,1)S(1)}, u32[]{:S(2)}, u32[]{:S(2)}) collective-permute-start(bf16[256,640]{1,0:T(8,128)(2,1)S(1)} %fusion.7), channel_id=1, source_target_pairs={{0,1},{1,0},{2,3},{3,2},{4,5},{5,4},{6,7},{7,6},{8,9},{9,8},{10,11... | collective-permute-start | bytes 983048 | tf_op jit(solution)/shard_map/ppermute | solution.py:49
  (4 other events, 11.7 us)

commit v7 on v6

--- a/solution.py
+++ b/solution.py
@@ -108,6 +108,8 @@
 
     ylo, high, core = (lax.axis_index(a) for a in ("ylo", "yhi", "core"))
     moved = lax.ppermute(tokens, ("x", "ylo", "yhi"), THERE)
+    moved, weight = lax.optimization_barrier((moved, weight))
+    far = trade(weight, "ylo")
 
     share = jnp.concatenate(
         [
@@ -122,7 +124,6 @@
     first = exchange(first, ("x", "z"))
 
     arrived = [lax.ppermute(later, ("ylo", "yhi"), SPREAD[j]) for j in range(4)]
-    far = trade(weight, "ylo")
     far, arrived = lax.optimization_barrier((far, arrived))
     own_core, other_core = (weight, far), (trade(weight, "core"), trade(far, "core"))
     arrived = jnp.stack(arrived)

time: 157 us -> 157 us (level)
  no operation moved by 1% of the time
where the time goes in v7:
time: 157 us; the launch traced here: 155 us
  starting transfers between devices  91.4 us (58%)
  waiting for transfers between devices  34.9 us (22%)
  matrix products  10.6 us (7%)
  Pallas kernels  6.35 us (4%)
  local copies, waits for them, and re-layouts  5.32 us (3%)
  other arithmetic  4.77 us (3%)
    all_to_all x3, starting transfers between devices, exchange(): return lax.all_to_all(pieces, axes, split_axis=0, concat_axis=0, tiled=True)  34 us
    ppermute x6, starting transfers between devices, trade(): return lax.ppermute(block, axis, [(0, 1), (1, 0)])  29 us
    ppermute x4, waiting for transfers between devices, local(): arrived = [lax.ppermute(later, ('ylo', 'yhi'), SPREAD[j]) for j in range(4)]  14.6 us
    ppermute x4, starting transfers between devices, local(): lax.ppermute(lax.dynamic_index_in_dim(frozen, high ^ j ^ ylo, 0, keepdims...  13.6 us
    ppermute x4, starting transfers between devices, local(): arrived = [lax.ppermute(later, ('ylo', 'yhi'), SPREAD[j]) for j in range(4)]  12.5 us
    dot_general x13, matrix products, dot(): lax.dot_general(left, right, ((contract[0], contract[1]), ((), ())), pref...  10.6 us
    all_to_all x3, waiting for transfers between devices, exchange(): return lax.all_to_all(pieces, axes, split_axis=0, concat_axis=0, tiled=True)  9.36 us
    ppermute x4, waiting for transfers between devices, local(): lax.ppermute(lax.dynamic_index_in_dim(frozen, high ^ j ^ ylo, 0, keepdims...  8.86 us
  transfers between devices with their start and end apart: 19, of which 8 were waited for; matrix products, arithmetic and copies ran while one was open for 9% of the time, Pallas kernels for 4%

profile of v7, /device:TPU:1, one launch (start us, length us, event | category | flops | bytes accessed | tf_op | source)
XLA Modules:
  0.0 154.5 jit_solution(5891305240104533716)
XLA Ops:
  0.6 1.5 %collective-permute-start = (bf16[128,128]{1,0:T(8,128)(2,1)}, bf16[128,128]{1,0:T(8,128)(2,1)S(1)}, u32[]{:S(2)}, u32[]{:S(2)}) collective-permute-start(bf16[128,128]{1,0:T(8,128)(2,1)} %param.6), channel_id=1, source_target_pairs={{0,0},{2,64},{4,256},{6,320},{64,128},{66,192},{68,384},{70,448},{... | collective-permute-start | bytes 98312 | tf_op jit(solution)/shard_map/ppermute | solution.py:110
  7.0 20.4 %all-to-all-start = ((bf16[32,176,128]{2,1,0:T(8,128)(2,1)}), bf16[32,176,128]{2,1,0:T(8,128)(2,1)S(1)}, u32[]{:S(2)}, u32[]{:S(2)}) async-start(bf16[32,176,128]{2,1,0:T(8,128)(2,1)} %pad_maximum_fusion), calls=%async_computation | async-start | bytes 2883584 | tf_op jit(solution)/shard_map/all_to_all | solution.py:37
  27.4 2.3 %collective-permute-start.1 = (bf16[1024,512]{1,0:T(8,128)(2,1)S(1)}, bf16[1024,512]{1,0:T(8,128)(2,1)}, u32[]{:S(2)}, u32[]{:S(2)}) collective-permute-start(bf16[1024,512]{1,0:T(8,128)(2,1)S(1)} %copy-done.2), channel_id=1, source_target_pairs={{0,64},{64,0},{1,65},{65,1},{2,66},{66,2},{3,67},{67,3},{4,68},{68... | collective-permute-start | bytes 3145736 | tf_op jit(solution)/shard_map/ppermute | solution.py:49
  29.7 4.3 %collective-permute-start.5 = (bf16[128,512]{1,0:T(8,128)(2,1)S(1)}, bf16[128,512]{1,0:T(8,128)(2,1)S(1)}, u32[]{:S(2)}, u32[]{:S(2)}) collective-permute-start(bf16[128,512]{1,0:T(8,128)(2,1)S(1)} %copy-done.8), channel_id=1, source_target_pairs={{0,6},{2,70},{4,2},{6,66},{64,4},{66,68},{68,0},{70,64},{1,7},{3,7... | collective-permute-start | bytes 393224 | tf_op jit(solution)/shard_map/ppermute | solution.py:126
  34.0 5.7 %collective-permute-start.4 = (bf16[128,512]{1,0:T(8,128)(2,1)S(1)}, bf16[128,512]{1,0:T(8,128)(2,1)S(1)}, u32[]{:S(2)}, u32[]{:S(2)}) collective-permute-start(bf16[128,512]{1,0:T(8,128)(2,1)S(1)} %copy-done.8), channel_id=1, source_target_pairs={{0,4},{2,68},{4,0},{6,64},{64,6},{66,70},{68,2},{70,66},{1,5},{3,6... | collective-permute-start | bytes 393224 | tf_op jit(solution)/shard_map/ppermute | solution.py:126
  39.7 1.9 %collective-permute-start.3 = (bf16[128,512]{1,0:T(8,128)(2,1)S(1)}, bf16[128,512]{1,0:T(8,128)(2,1)S(1)}, u32[]{:S(2)}, u32[]{:S(2)}) collective-permute-start(bf16[128,512]{1,0:T(8,128)(2,1)S(1)} %copy-done.8), channel_id=1, source_target_pairs={{0,2},{2,66},{4,6},{6,70},{64,0},{66,64},{68,4},{70,68},{1,3},{3,6... | collective-permute-start | bytes 393224 | tf_op jit(solution)/shard_map/ppermute | solution.py:126
  42.3 4.9 %collective-permute-start.6 = (bf16[1024,512]{1,0:T(8,128)(2,1)S(1)}, bf16[1024,512]{1,0:T(8,128)(2,1)}, u32[]{:S(2)}, u32[]{:S(2)}) collective-permute-start(bf16[1024,512]{1,0:T(8,128)(2,1)S(1)} %copy-done.2), channel_id=1, source_target_pairs={{0,1},{1,0},{2,3},{3,2},{4,5},{5,4},{6,7},{7,6},{8,9},{9,8},{10,11... | collective-permute-start | bytes 3145736 | tf_op jit(solution)/shard_map/ppermute | solution.py:49
  47.2 12.1 %collective-permute-done.4 = bf16[128,512]{1,0:T(8,128)(2,1)S(1)} collective-permute-done((bf16[128,512]{1,0:T(8,128)(2,1)S(1)}, bf16[128,512]{1,0:T(8,128)(2,1)S(1)}, u32[]{:S(2)}, u32[]{:S(2)}) %collective-permute-start.4) | collective-permute-done | bytes 131104 | tf_op jit(solution)/shard_map/ppermute | solution.py:126
  59.3 2.5 %collective-permute-done.3 = bf16[128,512]{1,0:T(8,128)(2,1)S(1)} collective-permute-done((bf16[128,512]{1,0:T(8,128)(2,1)S(1)}, bf16[128,512]{1,0:T(8,128)(2,1)S(1)}, u32[]{:S(2)}, u32[]{:S(2)}) %collective-permute-start.3) | collective-permute-done | bytes 131104 | tf_op jit(solution)/shard_map/ppermute | solution.py:126
  61.8 6.2 %collective-permute-start.7 = (bf16[1024,512]{1,0:T(8,128)(2,1)}, bf16[1024,512]{1,0:T(8,128)(2,1)}, u32[]{:S(2)}, u32[]{:S(2)}) collective-permute-start(bf16[1024,512]{1,0:T(8,128)(2,1)} %collective-permute-done.1.far_ref), channel_id=1, source_target_pairs={{0,1},{1,0},{2,3},{3,2},{4,5},{5,4},{6,7},{7,6},{8,9},{9,8},{10,11... | collective-permute-start | bytes 3145736 | tf_op jit(solution)/shard_map/ppermute | solution.py:49
  70.7 3.7 %collective-permute-start.8 = (f32[48,128]{1,0:T(8,128)S(1)}, f32[48,128]{1,0:T(8,128)S(1)}, u32[]{:S(2)}, u32[]{:S(2)}) collective-permute-start(f32[48,128]{1,0:T(8,128)S(1)} %convert_reduce_fusion.1), channel_id=1, source_target_pairs={{0,64},{64,0},{1,65},{65,1},{2,66},{66,2},{3,67},{67,3},{4,68},{68... | collective-permute-start | bytes 73736 | tf_op jit(solution)/shard_map/ppermute | solution.py:49
  74.4 6.4 %shard_map.93 = bf16[2,2,8,176,128]{4,3,2,1,0:T(8,128)(2,1)} custom-call(s32[2]{0:T(128)} %pad_add_fusion.where_ref, bf16[1024,512]{1,0:T(8,128)(2,1)} %near_ref, bf16[1024,512]{1,0:T(8,128)(2,1)} %collective-permute-done.1.far_ref, bf16[1024,512]{1,0:T(8,128)(2,1)} %collective-permute-done.6.near_beside_ref, ...), custom_call_target="tpu_custom_call" | custom-call | flops 1073741824 | bytes 4194304 | tf_op jit(solution)/shard_map/pallas_call | solution.py:84
  81.6 9.2 %all-to-all-start.1 = ((bf16[32,176,128]{2,1,0:T(8,128)(2,1)}), bf16[32,176,128]{2,1,0:T(8,128)(2,1)S(1)}, u32[]{:S(2)}, u32[]{:S(2)}) async-start(bf16[32,176,128]{2,1,0:T(8,128)(2,1)} %broadcast_dynamic-update-slice_fusion), calls=%async_computation.1 | async-start | bytes 2883584 | tf_op jit(solution)/shard_map/all_to_all | solution.py:37
  92.1 1.9 %collective-permute-start.9 = (bf16[256,512]{1,0:T(8,128)(2,1)S(1)}, bf16[256,512]{1,0:T(8,128)(2,1)S(1)}, u32[]{:S(2)}, u32[]{:S(2)}) collective-permute-start(bf16[256,512]{1,0:T(8,128)(2,1)S(1)} %pad_maximum_fusion.6), channel_id=1, source_target_pairs={{0,64},{64,0},{1,65},{65,1},{2,66},{66,2},{3,67},{67,3},{4,68},{68... | collective-permute-start | bytes 786440 | tf_op jit(solution)/shard_map/ppermute | solution.py:49
  94.4 1.7 %fusion.8 = f32[256,512]{1,0:T(8,128)S(1)} fusion(bf16[1024,512]{1,0:T(8,128)(2,1)} %collective-permute-done.7.far_beside_ref, bf16[32,8,8,128]{3,2,1,0:T(8,128)(2,1)S(1)} %bitcast.95), kind=kOutput, calls=%fused_computation.21 | convolution fusion | flops 268435456 | bytes 2097152 | tf_op jit(solution)/shard_map/dot_general | solution.py:33
  96.1 1.7 %fusion.10 = f32[256,512]{1,0:T(8,128)S(1)} fusion(bf16[1024,512]{1,0:T(8,128)(2,1)} %collective-permute-done.6.near_beside_ref, bf16[32,8,8,128]{3,2,1,0:T(8,128)(2,1)S(1)} %bitcast.96), kind=kOutput, calls=%fused_computation.23 | convolution fusion | flops 268435456 | bytes 2097152 | tf_op jit(solution)/shard_map/dot_general | solution.py:33
  97.7 1.7 %fusion.1 = bf16[256,512]{1,0:T(8,128)(2,1)S(1)} fusion(f32[256,512]{1,0:T(8,128)S(1)} %fusion.8, bf16[1024,512]{1,0:T(8,128)(2,1)} %collective-permute-done.1.far_ref, bf16[32,8,8,128]{3,2,1,0:T(8,128)(2,1)S(1)} %bitcast.93), kind=kOutput, calls=%fused_computation.5 | convolution fusion | flops 268697600 | bytes 2359296 | tf_op jit(solution)/shard_map/dot_general | solution.py:33
  102.5 5.6 %collective-permute-start.13 = (bf16[128,512]{1,0:T(8,128)(2,1)S(1)}, bf16[128,512]{1,0:T(8,128)(2,1)S(1)}, u32[]{:S(2)}, u32[]{:S(2)}) collective-permute-start(bf16[128,512]{1,0:T(8,128)(2,1)S(1)} %get-tuple-element.75), channel_id=1, source_target_pairs={{0,68},{2,4},{4,64},{6,0},{64,70},{66,6},{68,66},{70,2},{1,69},{3,... | collective-permute-start | bytes 393224 | tf_op jit(solution)/shard_map/ppermute | solution.py:147
  108.1 5.4 %collective-permute-start.12 = (bf16[128,512]{1,0:T(8,128)(2,1)S(1)}, bf16[128,512]{1,0:T(8,128)(2,1)S(1)}, u32[]{:S(2)}, u32[]{:S(2)}) collective-permute-start(bf16[128,512]{1,0:T(8,128)(2,1)S(1)} %get-tuple-element.76), channel_id=1, source_target_pairs={{0,4},{2,68},{4,0},{6,64},{64,6},{66,70},{68,2},{70,66},{1,5},{3,6... | collective-permute-start | bytes 393224 | tf_op jit(solution)/shard_map/ppermute | solution.py:147
  113.5 1.9 %collective-permute-start.11 = (bf16[128,512]{1,0:T(8,128)(2,1)S(1)}, bf16[128,512]{1,0:T(8,128)(2,1)S(1)}, u32[]{:S(2)}, u32[]{:S(2)}) collective-permute-start(bf16[128,512]{1,0:T(8,128)(2,1)S(1)} %get-tuple-element.77), channel_id=1, source_target_pairs={{0,64},{2,0},{4,68},{6,4},{64,66},{66,2},{68,70},{70,6},{1,65},{3,... | collective-permute-start | bytes 393224 | tf_op jit(solution)/shard_map/ppermute | solution.py:147
  115.4 8.1 %collective-permute-done.12 = bf16[128,512]{1,0:T(8,128)(2,1)S(1)} collective-permute-done((bf16[128,512]{1,0:T(8,128)(2,1)S(1)}, bf16[128,512]{1,0:T(8,128)(2,1)S(1)}, u32[]{:S(2)}, u32[]{:S(2)}) %collective-permute-start.12) | collective-permute-done | bytes 131104 | tf_op jit(solution)/shard_map/ppermute | solution.py:147
  126.4 4.4 %all-to-all-start.2 = ((bf16[4,512,128]{2,1,0:T(8,128)(2,1)}), bf16[4,512,128]{2,1,0:T(8,128)(2,1)S(1)}, u32[]{:S(2)}, u32[]{:S(2)}) async-start(bf16[4,512,128]{2,1,0:T(8,128)(2,1)} %broadcast_in_dim.8), calls=%async_computation.2 | async-start | bytes 1048576 | tf_op jit(solution)/shard_map/all_to_all | solution.py:37
  132.1 8.8 %all-to-all-done.2 = bf16[4,512,128]{2,1,0:T(8,128)(2,1)S(1)} async-done(((bf16[4,512,128]{2,1,0:T(8,128)(2,1)}), bf16[4,512,128]{2,1,0:T(8,128)(2,1)S(1)}, u32[]{:S(2)}, u32[]{:S(2)}) %all-to-all-start.2) | async-done | bytes 524320 | tf_op jit(solution)/shard_map/all_to_all | solution.py:37
  141.3 10.0 %collective-permute-start.15 = (bf16[256,640]{1,0:T(8,128)(2,1)S(1)}, bf16[256,640]{1,0:T(8,128)(2,1)S(1)}, u32[]{:S(2)}, u32[]{:S(2)}) collective-permute-start(bf16[256,640]{1,0:T(8,128)(2,1)S(1)} %fusion.7), channel_id=1, source_target_pairs={{0,1},{1,0},{2,3},{3,2},{4,5},{5,4},{6,7},{7,6},{8,9},{9,8},{10,11... | collective-permute-start | bytes 983048 | tf_op jit(solution)/shard_map/ppermute | solution.py:49
  (79 shorter events, 21.1 us)
Async XLA Ops:
  0.6 4.9 %collective-permute-start = (bf16[128,128]{1,0:T(8,128)(2,1)}, bf16[128,128]{1,0:T(8,128)(2,1)S(1)}, u32[]{:S(2)}, u32[]{:S(2)}) collective-permute-start(bf16[128,128]{1,0:T(8,128)(2,1)} %param.6), channel_id=1, source_target_pairs={{0,0},{2,64},{4,256},{6,320},{64,128},{66,192},{68,384},{70,448},{... | collective-permute-start | bytes 98312 | tf_op jit(solution)/shard_map/ppermute | solution.py:110
  7.0 20.4 %copy-start.2 = (bf16[1024,512]{1,0:T(8,128)(2,1)S(1)}, bf16[1024,512]{1,0:T(8,128)(2,1)}, u32[]{:S(2)}) copy-start(bf16[1024,512]{1,0:T(8,128)(2,1)} %near_ref) | copy-start | bytes 3145732
  7.0 22.7 %copy-start.8 = (bf16[128,512]{1,0:T(8,128)(2,1)S(1)}, bf16[128,512]{1,0:T(8,128)(2,1)}, u32[]{:S(2)}) copy-start(bf16[128,512]{1,0:T(8,128)(2,1)} %param.10) | copy-start | bytes 393220
  7.0 63.6 %all-to-all-start = ((bf16[32,176,128]{2,1,0:T(8,128)(2,1)}), bf16[32,176,128]{2,1,0:T(8,128)(2,1)S(1)}, u32[]{:S(2)}, u32[]{:S(2)}) async-start(bf16[32,176,128]{2,1,0:T(8,128)(2,1)} %pad_maximum_fusion), calls=%async_computation | async-start | bytes 2883584 | tf_op jit(solution)/shard_map/all_to_all | solution.py:37
  27.4 34.4 %collective-permute-start.1 = (bf16[1024,512]{1,0:T(8,128)(2,1)S(1)}, bf16[1024,512]{1,0:T(8,128)(2,1)}, u32[]{:S(2)}, u32[]{:S(2)}) collective-permute-start(bf16[1024,512]{1,0:T(8,128)(2,1)S(1)} %copy-done.2), channel_id=1, source_target_pairs={{0,64},{64,0},{1,65},{65,1},{2,66},{66,2},{3,67},{67,3},{4,68},{68... | collective-permute-start | bytes 3145736 | tf_op jit(solution)/shard_map/ppermute | solution.py:49
  29.7 12.6 %collective-permute-start.5 = (bf16[128,512]{1,0:T(8,128)(2,1)S(1)}, bf16[128,512]{1,0:T(8,128)(2,1)S(1)}, u32[]{:S(2)}, u32[]{:S(2)}) collective-permute-start(bf16[128,512]{1,0:T(8,128)(2,1)S(1)} %copy-done.8), channel_id=1, source_target_pairs={{0,6},{2,70},{4,2},{6,66},{64,4},{66,68},{68,0},{70,64},{1,7},{3,7... | collective-permute-start | bytes 393224 | tf_op jit(solution)/shard_map/ppermute | solution.py:126
  34.0 25.3 %collective-permute-start.4 = (bf16[128,512]{1,0:T(8,128)(2,1)S(1)}, bf16[128,512]{1,0:T(8,128)(2,1)S(1)}, u32[]{:S(2)}, u32[]{:S(2)}) collective-permute-start(bf16[128,512]{1,0:T(8,128)(2,1)S(1)} %copy-done.8), channel_id=1, source_target_pairs={{0,4},{2,68},{4,0},{6,64},{64,6},{66,70},{68,2},{70,66},{1,5},{3,6... | collective-permute-start | bytes 393224 | tf_op jit(solution)/shard_map/ppermute | solution.py:126
  39.7 22.1 %collective-permute-start.3 = (bf16[128,512]{1,0:T(8,128)(2,1)S(1)}, bf16[128,512]{1,0:T(8,128)(2,1)S(1)}, u32[]{:S(2)}, u32[]{:S(2)}) collective-permute-start(bf16[128,512]{1,0:T(8,128)(2,1)S(1)} %copy-done.8), channel_id=1, source_target_pairs={{0,2},{2,66},{4,6},{6,70},{64,0},{66,64},{68,4},{70,68},{1,3},{3,6... | collective-permute-start | bytes 393224 | tf_op jit(solution)/shard_map/ppermute | solution.py:126
  41.6 20.2 %collective-permute-start.2 = (bf16[128,512]{1,0:T(8,128)(2,1)S(1)}, bf16[128,512]{1,0:T(8,128)(2,1)S(1)}, u32[]{:S(2)}, u32[]{:S(2)}) collective-permute-start(bf16[128,512]{1,0:T(8,128)(2,1)S(1)} %copy-done.8), channel_id=1, source_target_pairs={{0,0},{2,64},{4,4},{6,68},{64,2},{66,66},{68,6},{70,70},{1,1},{3,6... | collective-permute-start | bytes 393224 | tf_op jit(solution)/shard_map/ppermute | solution.py:126
  42.3 27.2 %collective-permute-start.6 = (bf16[1024,512]{1,0:T(8,128)(2,1)S(1)}, bf16[1024,512]{1,0:T(8,128)(2,1)}, u32[]{:S(2)}, u32[]{:S(2)}) collective-permute-start(bf16[1024,512]{1,0:T(8,128)(2,1)S(1)} %copy-done.2), channel_id=1, source_target_pairs={{0,1},{1,0},{2,3},{3,2},{4,5},{5,4},{6,7},{7,6},{8,9},{9,8},{10,11... | collective-permute-start | bytes 3145736 | tf_op jit(solution)/shard_map/ppermute | solution.py:49
  61.8 8.8 %collective-permute-start.7 = (bf16[1024,512]{1,0:T(8,128)(2,1)}, bf16[1024,512]{1,0:T(8,128)(2,1)}, u32[]{:S(2)}, u32[]{:S(2)}) collective-permute-start(bf16[1024,512]{1,0:T(8,128)(2,1)} %collective-permute-done.1.far_ref), channel_id=1, source_target_pairs={{0,1},{1,0},{2,3},{3,2},{4,5},{5,4},{6,7},{7,6},{8,9},{9,8},{10,11... | collective-permute-start | bytes 3145736 | tf_op jit(solution)/shard_map/ppermute | solution.py:49
  70.7 10.0 %collective-permute-start.8 = (f32[48,128]{1,0:T(8,128)S(1)}, f32[48,128]{1,0:T(8,128)S(1)}, u32[]{:S(2)}, u32[]{:S(2)}) collective-permute-start(f32[48,128]{1,0:T(8,128)S(1)} %convert_reduce_fusion.1), channel_id=1, source_target_pairs={{0,64},{64,0},{1,65},{65,1},{2,66},{66,2},{3,67},{67,3},{4,68},{68... | collective-permute-start | bytes 73736 | tf_op jit(solution)/shard_map/ppermute | solution.py:49
  81.6 43.3 %all-to-all-start.1 = ((bf16[32,176,128]{2,1,0:T(8,128)(2,1)}), bf16[32,176,128]{2,1,0:T(8,128)(2,1)S(1)}, u32[]{:S(2)}, u32[]{:S(2)}) async-start(bf16[32,176,128]{2,1,0:T(8,128)(2,1)} %broadcast_dynamic-update-slice_fusion), calls=%async_computation.1 | async-start | bytes 2883584 | tf_op jit(solution)/shard_map/all_to_all | solution.py:37
  92.1 8.8 %collective-permute-start.9 = (bf16[256,512]{1,0:T(8,128)(2,1)S(1)}, bf16[256,512]{1,0:T(8,128)(2,1)S(1)}, u32[]{:S(2)}, u32[]{:S(2)}) collective-permute-start(bf16[256,512]{1,0:T(8,128)(2,1)S(1)} %pad_maximum_fusion.6), channel_id=1, source_target_pairs={{0,64},{64,0},{1,65},{65,1},{2,66},{66,2},{3,67},{67,3},{4,68},{68... | collective-permute-start | bytes 786440 | tf_op jit(solution)/shard_map/ppermute | solution.py:49
  101.7 23.2 %copy-start.6 = (bf16[128,128]{1,0:T(8,128)(2,1)S(1)}, bf16[128,128]{1,0:T(8,128)(2,1)}, u32[]{:S(2)}) copy-start(bf16[128,128]{1,0:T(8,128)(2,1)} %param.6) | copy-start | bytes 98308
  101.8 13.6 %collective-permute-start.10 = (bf16[128,512]{1,0:T(8,128)(2,1)S(1)}, bf16[128,512]{1,0:T(8,128)(2,1)S(1)}, u32[]{:S(2)}, u32[]{:S(2)}) collective-permute-start(bf16[128,512]{1,0:T(8,128)(2,1)S(1)} %get-tuple-element.74), channel_id=1, source_target_pairs={{0,0},{2,64},{4,4},{6,68},{64,2},{66,66},{68,6},{70,70},{1,1},{3,6... | collective-permute-start | bytes 393224 | tf_op jit(solution)/shard_map/ppermute | solution.py:147
  102.5 12.9 %collective-permute-start.13 = (bf16[128,512]{1,0:T(8,128)(2,1)S(1)}, bf16[128,512]{1,0:T(8,128)(2,1)S(1)}, u32[]{:S(2)}, u32[]{:S(2)}) collective-permute-start(bf16[128,512]{1,0:T(8,128)(2,1)S(1)} %get-tuple-element.75), channel_id=1, source_target_pairs={{0,68},{2,4},{4,64},{6,0},{64,70},{66,6},{68,66},{70,2},{1,69},{3,... | collective-permute-start | bytes 393224 | tf_op jit(solution)/shard_map/ppermute | solution.py:147
  108.1 15.5 %collective-permute-start.12 = (bf16[128,512]{1,0:T(8,128)(2,1)S(1)}, bf16[128,512]{1,0:T(8,128)(2,1)S(1)}, u32[]{:S(2)}, u32[]{:S(2)}) collective-permute-start(bf16[128,512]{1,0:T(8,128)(2,1)S(1)} %get-tuple-element.76), channel_id=1, source_target_pairs={{0,4},{2,68},{4,0},{6,64},{64,6},{66,70},{68,2},{70,66},{1,5},{3,6... | collective-permute-start | bytes 393224 | tf_op jit(solution)/shard_map/ppermute | solution.py:147
  113.5 10.8 %collective-permute-start.11 = (bf16[128,512]{1,0:T(8,128)(2,1)S(1)}, bf16[128,512]{1,0:T(8,128)(2,1)S(1)}, u32[]{:S(2)}, u32[]{:S(2)}) collective-permute-start(bf16[128,512]{1,0:T(8,128)(2,1)S(1)} %get-tuple-element.77), channel_id=1, source_target_pairs={{0,64},{2,0},{4,68},{6,4},{64,66},{66,2},{68,70},{70,6},{1,65},{3,... | collective-permute-start | bytes 393224 | tf_op jit(solution)/shard_map/ppermute | solution.py:147
  126.4 14.4 %all-to-all-start.2 = ((bf16[4,512,128]{2,1,0:T(8,128)(2,1)}), bf16[4,512,128]{2,1,0:T(8,128)(2,1)S(1)}, u32[]{:S(2)}, u32[]{:S(2)}) async-start(bf16[4,512,128]{2,1,0:T(8,128)(2,1)} %broadcast_in_dim.8), calls=%async_computation.2 | async-start | bytes 1048576 | tf_op jit(solution)/shard_map/all_to_all | solution.py:37
  131.0 10.0 %copy-start.5 = (bf16[512,512]{1,0:T(8,128)(2,1)S(1)}, bf16[512,512]{1,0:T(8,128)(2,1)}, u32[]{:S(2)}) copy-start(bf16[512,512]{1,0:T(8,128)(2,1)} %pad_maximum_fusion.4) | copy-start | bytes 1572868
  131.1 20.9 %collective-permute-start.14 = (f32[128,128]{0,1:T(8,128)S(1)}, f32[128,128]{0,1:T(8,128)S(1)}, u32[]{:S(2)}, u32[]{:S(2)}) collective-permute-start(f32[128,128]{0,1:T(8,128)S(1)} %copy.32), channel_id=1, source_target_pairs={{0,0},{64,2},{256,4},{320,6},{128,64},{192,66},{384,68},{448,70},{... | collective-permute-start | bytes 196616 | tf_op jit(solution)/shard_map/ppermute | solution.py:160
  140.9 11.1 %copy-start.7 = (bf16[128,256]{1,0:T(8,128)(2,1)S(1)}, bf16[128,256]{1,0:T(8,128)(2,1)}, u32[]{:S(2)}) copy-start(bf16[128,256]{1,0:T(8,128)(2,1)} %param.8) | copy-start | bytes 196612
  141.3 11.5 %collective-permute-start.15 = (bf16[256,640]{1,0:T(8,128)(2,1)S(1)}, bf16[256,640]{1,0:T(8,128)(2,1)S(1)}, u32[]{:S(2)}, u32[]{:S(2)}) collective-permute-start(bf16[256,640]{1,0:T(8,128)(2,1)S(1)} %fusion.7), channel_id=1, source_target_pairs={{0,1},{1,0},{2,3},{3,2},{4,5},{5,4},{6,7},{7,6},{8,9},{9,8},{10,11... | collective-permute-start | bytes 983048 | tf_op jit(solution)/shard_map/ppermute | solution.py:49
  (4 other events, 11.7 us)

commit v8 on v7

--- a/solution.py
+++ b/solution.py
@@ -142,6 +142,9 @@
     frozen = jnp.stack([f.reshape(2, batch, hidden) for f in frozen], axis=1).reshape(4, batch, hidden)
     kept = [lax.dynamic_index_in_dim(arrived, high ^ ylo ^ p, 0, keepdims=False) for p in (0, 2, 1, 3)]
     column = jnp.concatenate([*kept[:2], trade(jnp.concatenate(kept[2:]), "ylo")])
+    column = column.reshape(4, batch, hidden)
+    order = [2 * ((high ^ j ^ ylo) & 1) + ((high ^ j) >> 1) for j in range(4)]
+    column = jnp.concatenate([lax.dynamic_index_in_dim(column, i, 0, keepdims=False) for i in order])
     frozen, column = lax.optimization_barrier((frozen, column))
     frozen = sum(
         lax.ppermute(
@@ -168,11 +171,11 @@
     kept_high = kept.astype(BF16)
     kept_rest = (kept - kept_high.astype(F32)).astype(BF16)
     down_part = dot(back_low, kept_high, ((1,), (1,))) + dot(back_low, kept_rest, ((1,), (1,)))
-    pair = exchange(to_all(jnp.concatenate([low, down_part.astype(BF16)], axis=0), "yhi"), "yhi")
-    lows = pair[:, :rank].reshape(2, 2, rank, batch)
-    lows = [lax.dynamic_index_in_dim(lows, l, 1, keepdims=False) for l in (ylo, 1 - ylo)]
-    up_part = dot(jnp.concatenate([*lows[0], *lows[1]], axis=1), column, ((1,), (0,)))
-    ours = jnp.concatenate([up_part, add_up(pair[:, rank:])], axis=1)
+    pair = jnp.concatenate([low, down_part.astype(BF16)], axis=0)
+    pair = [pair] + [lax.ppermute(pair, "yhi", [(h, h ^ j) for h in range(4)]) for j in range(1, 4)]
+    up_part = dot(jnp.concatenate([p[:rank] for p in pair], axis=1), column, ((1,), (0,)))
+    down_part = sum(p[rank:].astype(F32) for p in pair)
+    ours = jnp.concatenate([up_part, down_part], axis=1)
     ours = ours + trade(ours.astype(BF16), "core").astype(F32)
     grad_up, grad_down = ours[:, :hidden], ours[:, hidden:].T
     return projection_output, token_input_gradient, grad_down, grad_up

time: 157 us -> 158 us (level)
  starting transfers between devices: 91.4 us -> 94.5 us
    ppermute x0 -> x3, starting transfers between devices: none -> 11.4 us  [local(): lax.ppermute(pair, 'yhi', [(h, h ^ j) for h in range(4)])]
    all_to_all x3 -> x2, waiting for transfers between devices: 9.36 us -> 0.44 us  [exchange(): return lax.all_to_all(pieces, axes, split_axis=0, concat_axis=0, tiled=True)]
    ppermute x0 -> x3, waiting for transfers between devices: none -> 7.89 us  [local(): lax.ppermute(pair, 'yhi', [(h, h ^ j) for h in range(4)])]
    all_to_all x3 -> x2, starting transfers between devices: 34 us -> 29.6 us  [exchange(): return lax.all_to_all(pieces, axes, split_axis=0, concat_axis=0, tiled=True)]
    ppermute x6, starting transfers between devices: 29 us -> 25.1 us  [trade(): return lax.ppermute(block, axis, [(0, 1), (1, 0)])]
  transfers between devices with their start and end apart: 19 -> 21, of which waited for: 8 -> 9; matrix products, arithmetic and copies ran while one was open for 9% -> 9% of each run, Pallas kernels for 4% -> 4%
where the time goes in v8:
time: 158 us; the launch traced here: 156 us
  starting transfers between devices  94.5 us (60%)
  waiting for transfers between devices  33.9 us (21%)
  matrix products  10.6 us (7%)
  Pallas kernels  6.33 us (4%)
  other arithmetic  4.77 us (3%)
  local copies, waits for them, and re-layouts  4.51 us (3%)
    all_to_all x2, starting transfers between devices, exchange(): return lax.all_to_all(pieces, axes, split_axis=0, concat_axis=0, tiled=True)  29.6 us
    ppermute x6, starting transfers between devices, trade(): return lax.ppermute(block, axis, [(0, 1), (1, 0)])  25.1 us
    ppermute x4, waiting for transfers between devices, local(): arrived = [lax.ppermute(later, ('ylo', 'yhi'), SPREAD[j]) for j in range(4)]  14.6 us
    ppermute x4, starting transfers between devices, local(): lax.ppermute(lax.dynamic_index_in_dim(frozen, high ^ j ^ ylo, 0, keepdims...  13.6 us
    ppermute x4, starting transfers between devices, local(): arrived = [lax.ppermute(later, ('ylo', 'yhi'), SPREAD[j]) for j in range(4)]  12.5 us
    ppermute x3, starting transfers between devices, local(): lax.ppermute(pair, 'yhi', [(h, h ^ j) for h in range(4)])  11.4 us
    dot_general x13, matrix products, dot(): lax.dot_general(left, right, ((contract[0], contract[1]), ((), ())), pref...  10.6 us
    ppermute x4, waiting for transfers between devices, local(): lax.ppermute(lax.dynamic_index_in_dim(frozen, high ^ j ^ ylo, 0, keepdims...  8.9 us
  transfers between devices with their start and end apart: 21, of which 9 were waited for; matrix products, arithmetic and copies ran while one was open for 9% of the time, Pallas kernels for 4%

profile of v8, /device:TPU:1, one launch (start us, length us, event | category | flops | bytes accessed | tf_op | source)
XLA Modules:
  0.0 155.9 jit_solution(15957792344362912531)
XLA Ops:
  7.0 20.4 %all-to-all-start = ((bf16[32,176,128]{2,1,0:T(8,128)(2,1)}), bf16[32,176,128]{2,1,0:T(8,128)(2,1)S(1)}, u32[]{:S(2)}, u32[]{:S(2)}) async-start(bf16[32,176,128]{2,1,0:T(8,128)(2,1)} %pad_maximum_fusion), calls=%async_computation | async-start | bytes 2883584 | tf_op jit(solution)/shard_map/all_to_all | solution.py:37
  27.4 2.3 %collective-permute-start.1 = (bf16[1024,512]{1,0:T(8,128)(2,1)S(1)}, bf16[1024,512]{1,0:T(8,128)(2,1)}, u32[]{:S(2)}, u32[]{:S(2)}) collective-permute-start(bf16[1024,512]{1,0:T(8,128)(2,1)S(1)} %copy-done.2), channel_id=1, source_target_pairs={{0,64},{64,0},{1,65},{65,1},{2,66},{66,2},{3,67},{67,3},{4,68},{68... | collective-permute-start | bytes 3145736 | tf_op jit(solution)/shard_map/ppermute | solution.py:49
  29.7 4.3 %collective-permute-start.5 = (bf16[128,512]{1,0:T(8,128)(2,1)S(1)}, bf16[128,512]{1,0:T(8,128)(2,1)S(1)}, u32[]{:S(2)}, u32[]{:S(2)}) collective-permute-start(bf16[128,512]{1,0:T(8,128)(2,1)S(1)} %copy-done.8), channel_id=1, source_target_pairs={{0,6},{2,70},{4,2},{6,66},{64,4},{66,68},{68,0},{70,64},{1,7},{3,7... | collective-permute-start | bytes 393224 | tf_op jit(solution)/shard_map/ppermute | solution.py:126
  34.0 5.7 %collective-permute-start.4 = (bf16[128,512]{1,0:T(8,128)(2,1)S(1)}, bf16[128,512]{1,0:T(8,128)(2,1)S(1)}, u32[]{:S(2)}, u32[]{:S(2)}) collective-permute-start(bf16[128,512]{1,0:T(8,128)(2,1)S(1)} %copy-done.8), channel_id=1, source_target_pairs={{0,4},{2,68},{4,0},{6,64},{64,6},{66,70},{68,2},{70,66},{1,5},{3,6... | collective-permute-start | bytes 393224 | tf_op jit(solution)/shard_map/ppermute | solution.py:126
  39.7 1.9 %collective-permute-start.3 = (bf16[128,512]{1,0:T(8,128)(2,1)S(1)}, bf16[128,512]{1,0:T(8,128)(2,1)S(1)}, u32[]{:S(2)}, u32[]{:S(2)}) collective-permute-start(bf16[128,512]{1,0:T(8,128)(2,1)S(1)} %copy-done.8), channel_id=1, source_target_pairs={{0,2},{2,66},{4,6},{6,70},{64,0},{66,64},{68,4},{70,68},{1,3},{3,6... | collective-permute-start | bytes 393224 | tf_op jit(solution)/shard_map/ppermute | solution.py:126
  42.3 4.9 %collective-permute-start.6 = (bf16[1024,512]{1,0:T(8,128)(2,1)S(1)}, bf16[1024,512]{1,0:T(8,128)(2,1)}, u32[]{:S(2)}, u32[]{:S(2)}) collective-permute-start(bf16[1024,512]{1,0:T(8,128)(2,1)S(1)} %copy-done.2), channel_id=1, source_target_pairs={{0,1},{1,0},{2,3},{3,2},{4,5},{5,4},{6,7},{7,6},{8,9},{9,8},{10,11... | collective-permute-start | bytes 3145736 | tf_op jit(solution)/shard_map/ppermute | solution.py:49
  47.2 12.1 %collective-permute-done.4 = bf16[128,512]{1,0:T(8,128)(2,1)S(1)} collective-permute-done((bf16[128,512]{1,0:T(8,128)(2,1)S(1)}, bf16[128,512]{1,0:T(8,128)(2,1)S(1)}, u32[]{:S(2)}, u32[]{:S(2)}) %collective-permute-start.4) | collective-permute-done | bytes 131104 | tf_op jit(solution)/shard_map/ppermute | solution.py:126
  59.3 2.5 %collective-permute-done.3 = bf16[128,512]{1,0:T(8,128)(2,1)S(1)} collective-permute-done((bf16[128,512]{1,0:T(8,128)(2,1)S(1)}, bf16[128,512]{1,0:T(8,128)(2,1)S(1)}, u32[]{:S(2)}, u32[]{:S(2)}) %collective-permute-start.3) | collective-permute-done | bytes 131104 | tf_op jit(solution)/shard_map/ppermute | solution.py:126
  61.8 6.2 %collective-permute-start.7 = (bf16[1024,512]{1,0:T(8,128)(2,1)}, bf16[1024,512]{1,0:T(8,128)(2,1)}, u32[]{:S(2)}, u32[]{:S(2)}) collective-permute-start(bf16[1024,512]{1,0:T(8,128)(2,1)} %collective-permute-done.1.far_ref), channel_id=1, source_target_pairs={{0,1},{1,0},{2,3},{3,2},{4,5},{5,4},{6,7},{7,6},{8,9},{9,8},{10,11... | collective-permute-start | bytes 3145736 | tf_op jit(solution)/shard_map/ppermute | solution.py:49
  70.7 3.7 %collective-permute-start.8 = (f32[48,128]{1,0:T(8,128)S(1)}, f32[48,128]{1,0:T(8,128)S(1)}, u32[]{:S(2)}, u32[]{:S(2)}) collective-permute-start(f32[48,128]{1,0:T(8,128)S(1)} %convert_reduce_fusion.1), channel_id=1, source_target_pairs={{0,64},{64,0},{1,65},{65,1},{2,66},{66,2},{3,67},{67,3},{4,68},{68... | collective-permute-start | bytes 73736 | tf_op jit(solution)/shard_map/ppermute | solution.py:49
  74.4 6.3 %shard_map.93 = bf16[2,2,8,176,128]{4,3,2,1,0:T(8,128)(2,1)} custom-call(s32[2]{0:T(128)} %pad_add_fusion.where_ref, bf16[1024,512]{1,0:T(8,128)(2,1)} %near_ref, bf16[1024,512]{1,0:T(8,128)(2,1)} %collective-permute-done.1.far_ref, bf16[1024,512]{1,0:T(8,128)(2,1)} %collective-permute-done.6.near_beside_ref, ...), custom_call_target="tpu_custom_call" | custom-call | flops 1073741824 | bytes 4194304 | tf_op jit(solution)/shard_map/pallas_call | solution.py:84
  81.6 9.2 %all-to-all-start.1 = ((bf16[32,176,128]{2,1,0:T(8,128)(2,1)}), bf16[32,176,128]{2,1,0:T(8,128)(2,1)S(1)}, u32[]{:S(2)}, u32[]{:S(2)}) async-start(bf16[32,176,128]{2,1,0:T(8,128)(2,1)} %broadcast_dynamic-update-slice_fusion), calls=%async_computation.1 | async-start | bytes 2883584 | tf_op jit(solution)/shard_map/all_to_all | solution.py:37
  92.1 1.9 %collective-permute-start.9 = (bf16[256,512]{1,0:T(8,128)(2,1)S(1)}, bf16[256,512]{1,0:T(8,128)(2,1)S(1)}, u32[]{:S(2)}, u32[]{:S(2)}) collective-permute-start(bf16[256,512]{1,0:T(8,128)(2,1)S(1)} %pad_maximum_fusion.7), channel_id=1, source_target_pairs={{0,64},{64,0},{1,65},{65,1},{2,66},{66,2},{3,67},{67,3},{4,68},{68... | collective-permute-start | bytes 786440 | tf_op jit(solution)/shard_map/ppermute | solution.py:49
  97.8 1.7 %fusion.1 = bf16[256,512]{1,0:T(8,128)(2,1)S(1)} fusion(f32[256,512]{1,0:T(8,128)S(1)} %fusion.8, bf16[1024,512]{1,0:T(8,128)(2,1)} %collective-permute-done.1.far_ref, bf16[32,8,8,128]{3,2,1,0:T(8,128)(2,1)S(1)} %bitcast.93), kind=kOutput, calls=%fused_computation.5 | convolution fusion | flops 268697600 | bytes 2359296 | tf_op jit(solution)/shard_map/dot_general | solution.py:33
  102.6 5.6 %collective-permute-start.13 = (bf16[128,512]{1,0:T(8,128)(2,1)S(1)}, bf16[128,512]{1,0:T(8,128)(2,1)S(1)}, u32[]{:S(2)}, u32[]{:S(2)}) collective-permute-start(bf16[128,512]{1,0:T(8,128)(2,1)S(1)} %get-tuple-element.71), channel_id=1, source_target_pairs={{0,68},{2,4},{4,64},{6,0},{64,70},{66,6},{68,66},{70,2},{1,69},{3,... | collective-permute-start | bytes 393224 | tf_op jit(solution)/shard_map/ppermute | solution.py:150
  108.2 5.4 %collective-permute-start.12 = (bf16[128,512]{1,0:T(8,128)(2,1)S(1)}, bf16[128,512]{1,0:T(8,128)(2,1)S(1)}, u32[]{:S(2)}, u32[]{:S(2)}) collective-permute-start(bf16[128,512]{1,0:T(8,128)(2,1)S(1)} %get-tuple-element.72), channel_id=1, source_target_pairs={{0,4},{2,68},{4,0},{6,64},{64,6},{66,70},{68,2},{70,66},{1,5},{3,6... | collective-permute-start | bytes 393224 | tf_op jit(solution)/shard_map/ppermute | solution.py:150
  113.6 1.9 %collective-permute-start.11 = (bf16[128,512]{1,0:T(8,128)(2,1)S(1)}, bf16[128,512]{1,0:T(8,128)(2,1)S(1)}, u32[]{:S(2)}, u32[]{:S(2)}) collective-permute-start(bf16[128,512]{1,0:T(8,128)(2,1)S(1)} %get-tuple-element.73), channel_id=1, source_target_pairs={{0,64},{2,0},{4,68},{6,4},{64,66},{66,2},{68,70},{70,6},{1,65},{3,... | collective-permute-start | bytes 393224 | tf_op jit(solution)/shard_map/ppermute | solution.py:150
  115.5 8.1 %collective-permute-done.12 = bf16[128,512]{1,0:T(8,128)(2,1)S(1)} collective-permute-done((bf16[128,512]{1,0:T(8,128)(2,1)S(1)}, bf16[128,512]{1,0:T(8,128)(2,1)S(1)}, u32[]{:S(2)}, u32[]{:S(2)}) %collective-permute-start.12) | collective-permute-done | bytes 131104 | tf_op jit(solution)/shard_map/ppermute | solution.py:150
  125.8 3.0 %collective-permute-start.17 = (bf16[512,128]{1,0:T(8,128)(2,1)S(1)}, bf16[512,128]{1,0:T(8,128)(2,1)S(1)}, u32[]{:S(2)}, u32[]{:S(2)}) collective-permute-start(bf16[512,128]{1,0:T(8,128)(2,1)S(1)} %pad_maximum_fusion.8), channel_id=1, source_target_pairs={{0,6},{2,4},{4,2},{6,0},{1,7},{3,5},{5,3},{7,1},{8,14},{10,12},{12... | collective-permute-start | bytes 393224 | tf_op jit(solution)/shard_map/ppermute | solution.py:175
  128.8 5.5 %collective-permute-start.16 = (bf16[512,128]{1,0:T(8,128)(2,1)S(1)}, bf16[512,128]{1,0:T(8,128)(2,1)S(1)}, u32[]{:S(2)}, u32[]{:S(2)}) collective-permute-start(bf16[512,128]{1,0:T(8,128)(2,1)S(1)} %pad_maximum_fusion.8), channel_id=1, source_target_pairs={{0,4},{2,6},{4,0},{6,2},{1,5},{3,7},{5,1},{7,3},{8,12},{10,14},{12... | collective-permute-start | bytes 393224 | tf_op jit(solution)/shard_map/ppermute | solution.py:175
  134.3 2.8 %collective-permute-start.15 = (bf16[512,128]{1,0:T(8,128)(2,1)S(1)}, bf16[512,128]{1,0:T(8,128)(2,1)S(1)}, u32[]{:S(2)}, u32[]{:S(2)}) collective-permute-start(bf16[512,128]{1,0:T(8,128)(2,1)S(1)} %pad_maximum_fusion.8), channel_id=1, source_target_pairs={{0,2},{2,0},{4,6},{6,4},{1,3},{3,1},{5,7},{7,5},{8,10},{10,8},{12,... | collective-permute-start | bytes 393224 | tf_op jit(solution)/shard_map/ppermute | solution.py:175
  138.2 2.2 %collective-permute-done.16 = bf16[512,128]{1,0:T(8,128)(2,1)S(1)} collective-permute-done((bf16[512,128]{1,0:T(8,128)(2,1)S(1)}, bf16[512,128]{1,0:T(8,128)(2,1)S(1)}, u32[]{:S(2)}, u32[]{:S(2)}) %collective-permute-start.16) | collective-permute-done | bytes 131104 | tf_op jit(solution)/shard_map/ppermute | solution.py:175
  140.4 5.7 %collective-permute-done.15 = bf16[512,128]{1,0:T(8,128)(2,1)S(1)} collective-permute-done((bf16[512,128]{1,0:T(8,128)(2,1)S(1)}, bf16[512,128]{1,0:T(8,128)(2,1)S(1)}, u32[]{:S(2)}, u32[]{:S(2)}) %collective-permute-start.15) | collective-permute-done | bytes 131104 | tf_op jit(solution)/shard_map/ppermute | solution.py:175
  146.5 6.1 %collective-permute-start.18 = (bf16[256,640]{1,0:T(8,128)(2,1)S(1)}, bf16[256,640]{1,0:T(8,128)(2,1)S(1)}, u32[]{:S(2)}, u32[]{:S(2)}) collective-permute-start(bf16[256,640]{1,0:T(8,128)(2,1)S(1)} %fusion.7), channel_id=1, source_target_pairs={{0,1},{1,0},{2,3},{3,2},{4,5},{5,4},{6,7},{7,6},{8,9},{9,8},{10,11... | collective-permute-start | bytes 983048 | tf_op jit(solution)/shard_map/ppermute | solution.py:49
  (85 shorter events, 25.0 us)
Async XLA Ops:
  0.6 4.9 %collective-permute-start = (bf16[128,128]{1,0:T(8,128)(2,1)}, bf16[128,128]{1,0:T(8,128)(2,1)S(1)}, u32[]{:S(2)}, u32[]{:S(2)}) collective-permute-start(bf16[128,128]{1,0:T(8,128)(2,1)} %param.6), channel_id=1, source_target_pairs={{0,0},{2,64},{4,256},{6,320},{64,128},{66,192},{68,384},{70,448},{... | collective-permute-start | bytes 98312 | tf_op jit(solution)/shard_map/ppermute | solution.py:110
  7.0 22.7 %copy-start.8 = (bf16[128,512]{1,0:T(8,128)(2,1)S(1)}, bf16[128,512]{1,0:T(8,128)(2,1)}, u32[]{:S(2)}) copy-start(bf16[128,512]{1,0:T(8,128)(2,1)} %param.10) | copy-start | bytes 393220
  7.0 63.6 %all-to-all-start = ((bf16[32,176,128]{2,1,0:T(8,128)(2,1)}), bf16[32,176,128]{2,1,0:T(8,128)(2,1)S(1)}, u32[]{:S(2)}, u32[]{:S(2)}) async-start(bf16[32,176,128]{2,1,0:T(8,128)(2,1)} %pad_maximum_fusion), calls=%async_computation | async-start | bytes 2883584 | tf_op jit(solution)/shard_map/all_to_all | solution.py:37
  27.4 34.4 %collective-permute-start.1 = (bf16[1024,512]{1,0:T(8,128)(2,1)S(1)}, bf16[1024,512]{1,0:T(8,128)(2,1)}, u32[]{:S(2)}, u32[]{:S(2)}) collective-permute-start(bf16[1024,512]{1,0:T(8,128)(2,1)S(1)} %copy-done.2), channel_id=1, source_target_pairs={{0,64},{64,0},{1,65},{65,1},{2,66},{66,2},{3,67},{67,3},{4,68},{68... | collective-permute-start | bytes 3145736 | tf_op jit(solution)/shard_map/ppermute | solution.py:49
  29.7 12.6 %collective-permute-start.5 = (bf16[128,512]{1,0:T(8,128)(2,1)S(1)}, bf16[128,512]{1,0:T(8,128)(2,1)S(1)}, u32[]{:S(2)}, u32[]{:S(2)}) collective-permute-start(bf16[128,512]{1,0:T(8,128)(2,1)S(1)} %copy-done.8), channel_id=1, source_target_pairs={{0,6},{2,70},{4,2},{6,66},{64,4},{66,68},{68,0},{70,64},{1,7},{3,7... | collective-permute-start | bytes 393224 | tf_op jit(solution)/shard_map/ppermute | solution.py:126
  34.0 25.3 %collective-permute-start.4 = (bf16[128,512]{1,0:T(8,128)(2,1)S(1)}, bf16[128,512]{1,0:T(8,128)(2,1)S(1)}, u32[]{:S(2)}, u32[]{:S(2)}) collective-permute-start(bf16[128,512]{1,0:T(8,128)(2,1)S(1)} %copy-done.8), channel_id=1, source_target_pairs={{0,4},{2,68},{4,0},{6,64},{64,6},{66,70},{68,2},{70,66},{1,5},{3,6... | collective-permute-start | bytes 393224 | tf_op jit(solution)/shard_map/ppermute | solution.py:126
  39.7 22.1 %collective-permute-start.3 = (bf16[128,512]{1,0:T(8,128)(2,1)S(1)}, bf16[128,512]{1,0:T(8,128)(2,1)S(1)}, u32[]{:S(2)}, u32[]{:S(2)}) collective-permute-start(bf16[128,512]{1,0:T(8,128)(2,1)S(1)} %copy-done.8), channel_id=1, source_target_pairs={{0,2},{2,66},{4,6},{6,70},{64,0},{66,64},{68,4},{70,68},{1,3},{3,6... | collective-permute-start | bytes 393224 | tf_op jit(solution)/shard_map/ppermute | solution.py:126
  41.6 20.2 %collective-permute-start.2 = (bf16[128,512]{1,0:T(8,128)(2,1)S(1)}, bf16[128,512]{1,0:T(8,128)(2,1)S(1)}, u32[]{:S(2)}, u32[]{:S(2)}) collective-permute-start(bf16[128,512]{1,0:T(8,128)(2,1)S(1)} %copy-done.8), channel_id=1, source_target_pairs={{0,0},{2,64},{4,4},{6,68},{64,2},{66,66},{68,6},{70,70},{1,1},{3,6... | collective-permute-start | bytes 393224 | tf_op jit(solution)/shard_map/ppermute | solution.py:126
  42.3 27.2 %collective-permute-start.6 = (bf16[1024,512]{1,0:T(8,128)(2,1)S(1)}, bf16[1024,512]{1,0:T(8,128)(2,1)}, u32[]{:S(2)}, u32[]{:S(2)}) collective-permute-start(bf16[1024,512]{1,0:T(8,128)(2,1)S(1)} %copy-done.2), channel_id=1, source_target_pairs={{0,1},{1,0},{2,3},{3,2},{4,5},{5,4},{6,7},{7,6},{8,9},{9,8},{10,11... | collective-permute-start | bytes 3145736 | tf_op jit(solution)/shard_map/ppermute | solution.py:49
  61.8 8.8 %collective-permute-start.7 = (bf16[1024,512]{1,0:T(8,128)(2,1)}, bf16[1024,512]{1,0:T(8,128)(2,1)}, u32[]{:S(2)}, u32[]{:S(2)}) collective-permute-start(bf16[1024,512]{1,0:T(8,128)(2,1)} %collective-permute-done.1.far_ref), channel_id=1, source_target_pairs={{0,1},{1,0},{2,3},{3,2},{4,5},{5,4},{6,7},{7,6},{8,9},{9,8},{10,11... | collective-permute-start | bytes 3145736 | tf_op jit(solution)/shard_map/ppermute | solution.py:49
  70.7 10.0 %collective-permute-start.8 = (f32[48,128]{1,0:T(8,128)S(1)}, f32[48,128]{1,0:T(8,128)S(1)}, u32[]{:S(2)}, u32[]{:S(2)}) collective-permute-start(f32[48,128]{1,0:T(8,128)S(1)} %convert_reduce_fusion.1), channel_id=1, source_target_pairs={{0,64},{64,0},{1,65},{65,1},{2,66},{66,2},{3,67},{67,3},{4,68},{68... | collective-permute-start | bytes 73736 | tf_op jit(solution)/shard_map/ppermute | solution.py:49
  81.6 43.3 %all-to-all-start.1 = ((bf16[32,176,128]{2,1,0:T(8,128)(2,1)}), bf16[32,176,128]{2,1,0:T(8,128)(2,1)S(1)}, u32[]{:S(2)}, u32[]{:S(2)}) async-start(bf16[32,176,128]{2,1,0:T(8,128)(2,1)} %broadcast_dynamic-update-slice_fusion), calls=%async_computation.1 | async-start | bytes 2883584 | tf_op jit(solution)/shard_map/all_to_all | solution.py:37
  92.1 8.8 %collective-permute-start.9 = (bf16[256,512]{1,0:T(8,128)(2,1)S(1)}, bf16[256,512]{1,0:T(8,128)(2,1)S(1)}, u32[]{:S(2)}, u32[]{:S(2)}) collective-permute-start(bf16[256,512]{1,0:T(8,128)(2,1)S(1)} %pad_maximum_fusion.7), channel_id=1, source_target_pairs={{0,64},{64,0},{1,65},{65,1},{2,66},{66,2},{3,67},{67,3},{4,68},{68... | collective-permute-start | bytes 786440 | tf_op jit(solution)/shard_map/ppermute | solution.py:49
  101.9 23.3 %copy-start.6 = (bf16[128,128]{1,0:T(8,128)(2,1)S(1)}, bf16[128,128]{1,0:T(8,128)(2,1)}, u32[]{:S(2)}) copy-start(bf16[128,128]{1,0:T(8,128)(2,1)} %param.6) | copy-start | bytes 98308
  101.9 13.6 %collective-permute-start.10 = (bf16[128,512]{1,0:T(8,128)(2,1)S(1)}, bf16[128,512]{1,0:T(8,128)(2,1)S(1)}, u32[]{:S(2)}, u32[]{:S(2)}) collective-permute-start(bf16[128,512]{1,0:T(8,128)(2,1)S(1)} %get-tuple-element.70), channel_id=1, source_target_pairs={{0,0},{2,64},{4,4},{6,68},{64,2},{66,66},{68,6},{70,70},{1,1},{3,6... | collective-permute-start | bytes 393224 | tf_op jit(solution)/shard_map/ppermute | solution.py:150
  102.6 12.9 %collective-permute-start.13 = (bf16[128,512]{1,0:T(8,128)(2,1)S(1)}, bf16[128,512]{1,0:T(8,128)(2,1)S(1)}, u32[]{:S(2)}, u32[]{:S(2)}) collective-permute-start(bf16[128,512]{1,0:T(8,128)(2,1)S(1)} %get-tuple-element.71), channel_id=1, source_target_pairs={{0,68},{2,4},{4,64},{6,0},{64,70},{66,6},{68,66},{70,2},{1,69},{3,... | collective-permute-start | bytes 393224 | tf_op jit(solution)/shard_map/ppermute | solution.py:150
  108.2 15.5 %collective-permute-start.12 = (bf16[128,512]{1,0:T(8,128)(2,1)S(1)}, bf16[128,512]{1,0:T(8,128)(2,1)S(1)}, u32[]{:S(2)}, u32[]{:S(2)}) collective-permute-start(bf16[128,512]{1,0:T(8,128)(2,1)S(1)} %get-tuple-element.72), channel_id=1, source_target_pairs={{0,4},{2,68},{4,0},{6,64},{64,6},{66,70},{68,2},{70,66},{1,5},{3,6... | collective-permute-start | bytes 393224 | tf_op jit(solution)/shard_map/ppermute | solution.py:150
  113.6 10.8 %collective-permute-start.11 = (bf16[128,512]{1,0:T(8,128)(2,1)S(1)}, bf16[128,512]{1,0:T(8,128)(2,1)S(1)}, u32[]{:S(2)}, u32[]{:S(2)}) collective-permute-start(bf16[128,512]{1,0:T(8,128)(2,1)S(1)} %get-tuple-element.73), channel_id=1, source_target_pairs={{0,64},{2,0},{4,68},{6,4},{64,66},{66,2},{68,70},{70,6},{1,65},{3,... | collective-permute-start | bytes 393224 | tf_op jit(solution)/shard_map/ppermute | solution.py:150
  125.1 21.0 %copy-start.5 = (bf16[512,512]{1,0:T(8,128)(2,1)S(1)}, bf16[512,512]{1,0:T(8,128)(2,1)}, u32[]{:S(2)}) copy-start(bf16[512,512]{1,0:T(8,128)(2,1)} %pad_maximum_fusion.5) | copy-start | bytes 1572868
  125.8 12.4 %collective-permute-start.17 = (bf16[512,128]{1,0:T(8,128)(2,1)S(1)}, bf16[512,128]{1,0:T(8,128)(2,1)S(1)}, u32[]{:S(2)}, u32[]{:S(2)}) collective-permute-start(bf16[512,128]{1,0:T(8,128)(2,1)S(1)} %pad_maximum_fusion.8), channel_id=1, source_target_pairs={{0,6},{2,4},{4,2},{6,0},{1,7},{3,5},{5,3},{7,1},{8,14},{10,12},{12... | collective-permute-start | bytes 393224 | tf_op jit(solution)/shard_map/ppermute | solution.py:175
  128.8 11.6 %collective-permute-start.16 = (bf16[512,128]{1,0:T(8,128)(2,1)S(1)}, bf16[512,128]{1,0:T(8,128)(2,1)S(1)}, u32[]{:S(2)}, u32[]{:S(2)}) collective-permute-start(bf16[512,128]{1,0:T(8,128)(2,1)S(1)} %pad_maximum_fusion.8), channel_id=1, source_target_pairs={{0,4},{2,6},{4,0},{6,2},{1,5},{3,7},{5,1},{7,3},{8,12},{10,14},{12... | collective-permute-start | bytes 393224 | tf_op jit(solution)/shard_map/ppermute | solution.py:175
  134.3 11.7 %collective-permute-start.15 = (bf16[512,128]{1,0:T(8,128)(2,1)S(1)}, bf16[512,128]{1,0:T(8,128)(2,1)S(1)}, u32[]{:S(2)}, u32[]{:S(2)}) collective-permute-start(bf16[512,128]{1,0:T(8,128)(2,1)S(1)} %pad_maximum_fusion.8), channel_id=1, source_target_pairs={{0,2},{2,0},{4,6},{6,4},{1,3},{3,1},{5,7},{7,5},{8,10},{10,8},{12,... | collective-permute-start | bytes 393224 | tf_op jit(solution)/shard_map/ppermute | solution.py:175
  137.3 16.1 %collective-permute-start.14 = (f32[128,128]{0,1:T(8,128)S(1)}, f32[128,128]{0,1:T(8,128)S(1)}, u32[]{:S(2)}, u32[]{:S(2)}) collective-permute-start(f32[128,128]{0,1:T(8,128)S(1)} %copy.26), channel_id=1, source_target_pairs={{0,0},{64,2},{256,4},{320,6},{128,64},{192,66},{384,68},{448,70},{... | collective-permute-start | bytes 196616 | tf_op jit(solution)/shard_map/ppermute | solution.py:163
  146.5 7.7 %collective-permute-start.18 = (bf16[256,640]{1,0:T(8,128)(2,1)S(1)}, bf16[256,640]{1,0:T(8,128)(2,1)S(1)}, u32[]{:S(2)}, u32[]{:S(2)}) collective-permute-start(bf16[256,640]{1,0:T(8,128)(2,1)S(1)} %fusion.7), channel_id=1, source_target_pairs={{0,1},{1,0},{2,3},{3,2},{4,5},{5,4},{6,7},{7,6},{8,9},{9,8},{10,11... | collective-permute-start | bytes 983048 | tf_op jit(solution)/shard_map/ppermute | solution.py:49
  (6 other events, 45.9 us)

commit v9 on v7

--- a/solution.py
+++ b/solution.py
@@ -124,7 +124,7 @@
     first = exchange(first, ("x", "z"))
 
     arrived = [lax.ppermute(later, ("ylo", "yhi"), SPREAD[j]) for j in range(4)]
-    far, arrived = lax.optimization_barrier((far, arrived))
+    far, arrived[0], arrived[1], arrived[3] = lax.optimization_barrier((far, arrived[0], arrived[1], arrived[3]))
     own_core, other_core = (weight, far), (trade(weight, "core"), trade(far, "core"))
     arrived = jnp.stack(arrived)
     first, own_core, other_core, arrived = lax.optimization_barrier((first, own_core, other_core, arrived))

time: 157 us -> 162 us (1.032)
  waiting for transfers between devices: 34.9 us -> 40.3 us
    ppermute x4, waiting for transfers between devices: 14.6 us -> 22 us  [local(): arrived = [lax.ppermute(later, ('ylo', 'yhi'), SPREAD[j]) for j in range(4)]]
  transfers between devices with their start and end apart: 19 -> 19, of which waited for: 8 -> 6; matrix products, arithmetic and copies ran while one was open for 9% -> 9% of each run, Pallas kernels for 4% -> 4%
where the time goes in v9:
time: 162 us; the launch traced here: 160 us
  starting transfers between devices  91.1 us (56%)
  waiting for transfers between devices  40.3 us (25%)
  matrix products  10.6 us (7%)
  Pallas kernels  6.35 us (4%)
  local copies, waits for them, and re-layouts  5.32 us (3%)
  other arithmetic  4.77 us (3%)
    all_to_all x3, starting transfers between devices, exchange(): return lax.all_to_all(pieces, axes, split_axis=0, concat_axis=0, tiled=True)  33.1 us
    ppermute x6, starting transfers between devices, trade(): return lax.ppermute(block, axis, [(0, 1), (1, 0)])  28.1 us
    ppermute x4, waiting for transfers between devices, local(): arrived = [lax.ppermute(later, ('ylo', 'yhi'), SPREAD[j]) for j in range(4)]  22 us
    ppermute x4, starting transfers between devices, local(): lax.ppermute(lax.dynamic_index_in_dim(frozen, high ^ j ^ ylo, 0, keepdims...  14.8 us
    ppermute x4, starting transfers between devices, local(): arrived = [lax.ppermute(later, ('ylo', 'yhi'), SPREAD[j]) for j in range(4)]  12.8 us
    dot_general x13, matrix products, dot(): lax.dot_general(left, right, ((contract[0], contract[1]), ((), ())), pref...  10.6 us
    all_to_all x3, waiting for transfers between devices, exchange(): return lax.all_to_all(pieces, axes, split_axis=0, concat_axis=0, tiled=True)  8.99 us
    ppermute x4, waiting for transfers between devices, local(): lax.ppermute(lax.dynamic_index_in_dim(frozen, high ^ j ^ ylo, 0, keepdims...  8.78 us
  transfers between devices with their start and end apart: 19, of which 6 were waited for; matrix products, arithmetic and copies ran while one was open for 9% of the time, Pallas kernels for 4%

profile of v9, /device:TPU:1, one launch (start us, length us, event | category | flops | bytes accessed | tf_op | source)
XLA Modules:
  0.0 159.7 jit_solution(17821334457629550324)
XLA Ops:
  7.0 20.4 %all-to-all-start = ((bf16[32,176,128]{2,1,0:T(8,128)(2,1)}), bf16[32,176,128]{2,1,0:T(8,128)(2,1)S(1)}, u32[]{:S(2)}, u32[]{:S(2)}) async-start(bf16[32,176,128]{2,1,0:T(8,128)(2,1)} %pad_maximum_fusion), calls=%async_computation | async-start | bytes 2883584 | tf_op jit(solution)/shard_map/all_to_all | solution.py:37
  27.4 2.3 %collective-permute-start.1 = (bf16[1024,512]{1,0:T(8,128)(2,1)S(1)}, bf16[1024,512]{1,0:T(8,128)(2,1)}, u32[]{:S(2)}, u32[]{:S(2)}) collective-permute-start(bf16[1024,512]{1,0:T(8,128)(2,1)S(1)} %copy-done.2), channel_id=1, source_target_pairs={{0,64},{64,0},{1,65},{65,1},{2,66},{66,2},{3,67},{67,3},{4,68},{68... | collective-permute-start | bytes 3145736 | tf_op jit(solution)/shard_map/ppermute | solution.py:49
  29.7 4.3 %collective-permute-start.4 = (bf16[128,512]{1,0:T(8,128)(2,1)S(1)}, bf16[128,512]{1,0:T(8,128)(2,1)S(1)}, u32[]{:S(2)}, u32[]{:S(2)}) collective-permute-start(bf16[128,512]{1,0:T(8,128)(2,1)S(1)} %copy-done.8), channel_id=1, source_target_pairs={{0,6},{2,70},{4,2},{6,66},{64,4},{66,68},{68,0},{70,64},{1,7},{3,7... | collective-permute-start | bytes 393224 | tf_op jit(solution)/shard_map/ppermute | solution.py:126
  34.0 3.0 %collective-permute-start.3 = (bf16[128,512]{1,0:T(8,128)(2,1)S(1)}, bf16[128,512]{1,0:T(8,128)(2,1)S(1)}, u32[]{:S(2)}, u32[]{:S(2)}) collective-permute-start(bf16[128,512]{1,0:T(8,128)(2,1)S(1)} %copy-done.8), channel_id=1, source_target_pairs={{0,2},{2,66},{4,6},{6,70},{64,0},{66,64},{68,4},{70,68},{1,3},{3,6... | collective-permute-start | bytes 393224 | tf_op jit(solution)/shard_map/ppermute | solution.py:126
  37.6 5.1 %collective-permute-start.5 = (bf16[1024,512]{1,0:T(8,128)(2,1)S(1)}, bf16[1024,512]{1,0:T(8,128)(2,1)}, u32[]{:S(2)}, u32[]{:S(2)}) collective-permute-start(bf16[1024,512]{1,0:T(8,128)(2,1)S(1)} %copy-done.2), channel_id=1, source_target_pairs={{0,1},{1,0},{2,3},{3,2},{4,5},{5,4},{6,7},{7,6},{8,9},{9,8},{10,11... | collective-permute-start | bytes 3145736 | tf_op jit(solution)/shard_map/ppermute | solution.py:49
  42.7 14.9 %collective-permute-done.3 = bf16[128,512]{1,0:T(8,128)(2,1)S(1)} collective-permute-done((bf16[128,512]{1,0:T(8,128)(2,1)S(1)}, bf16[128,512]{1,0:T(8,128)(2,1)S(1)}, u32[]{:S(2)}, u32[]{:S(2)}) %collective-permute-start.3) | collective-permute-done | bytes 131104 | tf_op jit(solution)/shard_map/ppermute | solution.py:126
  57.7 4.7 %collective-permute-start.6 = (bf16[1024,512]{1,0:T(8,128)(2,1)}, bf16[1024,512]{1,0:T(8,128)(2,1)}, u32[]{:S(2)}, u32[]{:S(2)}) collective-permute-start(bf16[1024,512]{1,0:T(8,128)(2,1)} %collective-permute-done.1.far_ref), channel_id=1, source_target_pairs={{0,1},{1,0},{2,3},{3,2},{4,5},{5,4},{6,7},{7,6},{8,9},{9,8},{10,11... | collective-permute-start | bytes 3145736 | tf_op jit(solution)/shard_map/ppermute | solution.py:49
  62.4 4.9 %collective-permute-start.7 = (bf16[128,512]{1,0:T(8,128)(2,1)S(1)}, bf16[128,512]{1,0:T(8,128)(2,1)S(1)}, u32[]{:S(2)}, u32[]{:S(2)}) collective-permute-start(bf16[128,512]{1,0:T(8,128)(2,1)S(1)} %copy-done.8), channel_id=1, source_target_pairs={{0,4},{2,68},{4,0},{6,64},{64,6},{66,70},{68,2},{70,66},{1,5},{3,6... | collective-permute-start | bytes 393224 | tf_op jit(solution)/shard_map/ppermute | solution.py:126
  67.9 7.1 %collective-permute-done.7 = bf16[128,512]{1,0:T(8,128)(2,1)S(1)} collective-permute-done((bf16[128,512]{1,0:T(8,128)(2,1)S(1)}, bf16[128,512]{1,0:T(8,128)(2,1)S(1)}, u32[]{:S(2)}, u32[]{:S(2)}) %collective-permute-start.7) | collective-permute-done | bytes 131104 | tf_op jit(solution)/shard_map/ppermute | solution.py:126
  75.9 4.0 %collective-permute-start.8 = (f32[48,128]{1,0:T(8,128)S(1)}, f32[48,128]{1,0:T(8,128)S(1)}, u32[]{:S(2)}, u32[]{:S(2)}) collective-permute-start(f32[48,128]{1,0:T(8,128)S(1)} %convert_reduce_fusion.1), channel_id=1, source_target_pairs={{0,64},{64,0},{1,65},{65,1},{2,66},{66,2},{3,67},{67,3},{4,68},{68... | collective-permute-start | bytes 73736 | tf_op jit(solution)/shard_map/ppermute | solution.py:49
  79.9 6.3 %shard_map.93 = bf16[2,2,8,176,128]{4,3,2,1,0:T(8,128)(2,1)} custom-call(s32[2]{0:T(128)} %pad_add_fusion.where_ref, bf16[1024,512]{1,0:T(8,128)(2,1)} %near_ref, bf16[1024,512]{1,0:T(8,128)(2,1)} %collective-permute-done.1.far_ref, bf16[1024,512]{1,0:T(8,128)(2,1)} %collective-permute-done.5.near_beside_ref, ...), custom_call_target="tpu_custom_call" | custom-call | flops 1073741824 | bytes 4194304 | tf_op jit(solution)/shard_map/pallas_call | solution.py:84
  87.1 9.2 %all-to-all-start.1 = ((bf16[32,176,128]{2,1,0:T(8,128)(2,1)}), bf16[32,176,128]{2,1,0:T(8,128)(2,1)S(1)}, u32[]{:S(2)}, u32[]{:S(2)}) async-start(bf16[32,176,128]{2,1,0:T(8,128)(2,1)} %broadcast_dynamic-update-slice_fusion), calls=%async_computation.1 | async-start | bytes 2883584 | tf_op jit(solution)/shard_map/all_to_all | solution.py:37
  97.7 1.9 %collective-permute-start.9 = (bf16[256,512]{1,0:T(8,128)(2,1)S(1)}, bf16[256,512]{1,0:T(8,128)(2,1)S(1)}, u32[]{:S(2)}, u32[]{:S(2)}) collective-permute-start(bf16[256,512]{1,0:T(8,128)(2,1)S(1)} %pad_maximum_fusion.6), channel_id=1, source_target_pairs={{0,64},{64,0},{1,65},{65,1},{2,66},{66,2},{3,67},{67,3},{4,68},{68... | collective-permute-start | bytes 786440 | tf_op jit(solution)/shard_map/ppermute | solution.py:49
  99.9 1.7 %fusion.8 = f32[256,512]{1,0:T(8,128)S(1)} fusion(bf16[1024,512]{1,0:T(8,128)(2,1)} %collective-permute-done.6.far_beside_ref, bf16[32,8,8,128]{3,2,1,0:T(8,128)(2,1)S(1)} %bitcast.95), kind=kOutput, calls=%fused_computation.21 | convolution fusion | flops 268435456 | bytes 2097152 | tf_op jit(solution)/shard_map/dot_general | solution.py:33
  101.6 1.7 %fusion.10 = f32[256,512]{1,0:T(8,128)S(1)} fusion(bf16[1024,512]{1,0:T(8,128)(2,1)} %collective-permute-done.5.near_beside_ref, bf16[32,8,8,128]{3,2,1,0:T(8,128)(2,1)S(1)} %bitcast.96), kind=kOutput, calls=%fused_computation.23 | convolution fusion | flops 268435456 | bytes 2097152 | tf_op jit(solution)/shard_map/dot_general | solution.py:33
  103.3 1.7 %fusion.1 = bf16[256,512]{1,0:T(8,128)(2,1)S(1)} fusion(f32[256,512]{1,0:T(8,128)S(1)} %fusion.8, bf16[1024,512]{1,0:T(8,128)(2,1)} %collective-permute-done.1.far_ref, bf16[32,8,8,128]{3,2,1,0:T(8,128)(2,1)S(1)} %bitcast.93), kind=kOutput, calls=%fused_computation.5 | convolution fusion | flops 268697600 | bytes 2359296 | tf_op jit(solution)/shard_map/dot_general | solution.py:33
  107.6 6.1 %collective-permute-start.13 = (bf16[128,512]{1,0:T(8,128)(2,1)S(1)}, bf16[128,512]{1,0:T(8,128)(2,1)S(1)}, u32[]{:S(2)}, u32[]{:S(2)}) collective-permute-start(bf16[128,512]{1,0:T(8,128)(2,1)S(1)} %get-tuple-element.73), channel_id=1, source_target_pairs={{0,68},{2,4},{4,64},{6,0},{64,70},{66,6},{68,66},{70,2},{1,69},{3,... | collective-permute-start | bytes 393224 | tf_op jit(solution)/shard_map/ppermute | solution.py:147
  113.7 6.2 %collective-permute-start.12 = (bf16[128,512]{1,0:T(8,128)(2,1)S(1)}, bf16[128,512]{1,0:T(8,128)(2,1)S(1)}, u32[]{:S(2)}, u32[]{:S(2)}) collective-permute-start(bf16[128,512]{1,0:T(8,128)(2,1)S(1)} %get-tuple-element.74), channel_id=1, source_target_pairs={{0,4},{2,68},{4,0},{6,64},{64,6},{66,70},{68,2},{70,66},{1,5},{3,6... | collective-permute-start | bytes 393224 | tf_op jit(solution)/shard_map/ppermute | solution.py:147
  119.9 1.9 %collective-permute-start.11 = (bf16[128,512]{1,0:T(8,128)(2,1)S(1)}, bf16[128,512]{1,0:T(8,128)(2,1)S(1)}, u32[]{:S(2)}, u32[]{:S(2)}) collective-permute-start(bf16[128,512]{1,0:T(8,128)(2,1)S(1)} %get-tuple-element.75), channel_id=1, source_target_pairs={{0,64},{2,0},{4,68},{6,4},{64,66},{66,2},{68,70},{70,6},{1,65},{3,... | collective-permute-start | bytes 393224 | tf_op jit(solution)/shard_map/ppermute | solution.py:147
  121.8 7.0 %collective-permute-done.12 = bf16[128,512]{1,0:T(8,128)(2,1)S(1)} collective-permute-done((bf16[128,512]{1,0:T(8,128)(2,1)S(1)}, bf16[128,512]{1,0:T(8,128)(2,1)S(1)}, u32[]{:S(2)}, u32[]{:S(2)}) %collective-permute-start.12) | collective-permute-done | bytes 131104 | tf_op jit(solution)/shard_map/ppermute | solution.py:147
  128.9 1.7 %collective-permute-done.11 = bf16[128,512]{1,0:T(8,128)(2,1)S(1)} collective-permute-done((bf16[128,512]{1,0:T(8,128)(2,1)S(1)}, bf16[128,512]{1,0:T(8,128)(2,1)S(1)}, u32[]{:S(2)}, u32[]{:S(2)}) %collective-permute-start.11) | collective-permute-done | bytes 131104 | tf_op jit(solution)/shard_map/ppermute | solution.py:147
  132.2 3.5 %all-to-all-start.2 = ((bf16[4,512,128]{2,1,0:T(8,128)(2,1)}), bf16[4,512,128]{2,1,0:T(8,128)(2,1)S(1)}, u32[]{:S(2)}, u32[]{:S(2)}) async-start(bf16[4,512,128]{2,1,0:T(8,128)(2,1)} %broadcast_in_dim.8), calls=%async_computation.2 | async-start | bytes 1048576 | tf_op jit(solution)/shard_map/all_to_all | solution.py:37
  137.0 9.0 %all-to-all-done.2 = bf16[4,512,128]{2,1,0:T(8,128)(2,1)S(1)} async-done(((bf16[4,512,128]{2,1,0:T(8,128)(2,1)}), bf16[4,512,128]{2,1,0:T(8,128)(2,1)S(1)}, u32[]{:S(2)}, u32[]{:S(2)}) %all-to-all-start.2) | async-done | bytes 524320 | tf_op jit(solution)/shard_map/all_to_all | solution.py:37
  146.4 10.0 %collective-permute-start.15 = (bf16[256,640]{1,0:T(8,128)(2,1)S(1)}, bf16[256,640]{1,0:T(8,128)(2,1)S(1)}, u32[]{:S(2)}, u32[]{:S(2)}) collective-permute-start(bf16[256,640]{1,0:T(8,128)(2,1)S(1)} %fusion.7), channel_id=1, source_target_pairs={{0,1},{1,0},{2,3},{3,2},{4,5},{5,4},{6,7},{7,6},{8,9},{9,8},{10,11... | collective-permute-start | bytes 983048 | tf_op jit(solution)/shard_map/ppermute | solution.py:49
  (79 shorter events, 19.9 us)
Async XLA Ops:
  0.6 4.9 %collective-permute-start = (bf16[128,128]{1,0:T(8,128)(2,1)}, bf16[128,128]{1,0:T(8,128)(2,1)S(1)}, u32[]{:S(2)}, u32[]{:S(2)}) collective-permute-start(bf16[128,128]{1,0:T(8,128)(2,1)} %param.6), channel_id=1, source_target_pairs={{0,0},{2,64},{4,256},{6,320},{64,128},{66,192},{68,384},{70,448},{... | collective-permute-start | bytes 98312 | tf_op jit(solution)/shard_map/ppermute | solution.py:110
  7.0 20.4 %copy-start.2 = (bf16[1024,512]{1,0:T(8,128)(2,1)S(1)}, bf16[1024,512]{1,0:T(8,128)(2,1)}, u32[]{:S(2)}) copy-start(bf16[1024,512]{1,0:T(8,128)(2,1)} %near_ref) | copy-start | bytes 3145732
  7.0 22.7 %copy-start.8 = (bf16[128,512]{1,0:T(8,128)(2,1)S(1)}, bf16[128,512]{1,0:T(8,128)(2,1)}, u32[]{:S(2)}) copy-start(bf16[128,512]{1,0:T(8,128)(2,1)} %param.10) | copy-start | bytes 393220
  7.0 68.8 %all-to-all-start = ((bf16[32,176,128]{2,1,0:T(8,128)(2,1)}), bf16[32,176,128]{2,1,0:T(8,128)(2,1)S(1)}, u32[]{:S(2)}, u32[]{:S(2)}) async-start(bf16[32,176,128]{2,1,0:T(8,128)(2,1)} %pad_maximum_fusion), calls=%async_computation | async-start | bytes 2883584 | tf_op jit(solution)/shard_map/all_to_all | solution.py:37
  27.4 30.3 %collective-permute-start.1 = (bf16[1024,512]{1,0:T(8,128)(2,1)S(1)}, bf16[1024,512]{1,0:T(8,128)(2,1)}, u32[]{:S(2)}, u32[]{:S(2)}) collective-permute-start(bf16[1024,512]{1,0:T(8,128)(2,1)S(1)} %copy-done.2), channel_id=1, source_target_pairs={{0,64},{64,0},{1,65},{65,1},{2,66},{66,2},{3,67},{67,3},{4,68},{68... | collective-permute-start | bytes 3145736 | tf_op jit(solution)/shard_map/ppermute | solution.py:49
  29.7 13.0 %collective-permute-start.4 = (bf16[128,512]{1,0:T(8,128)(2,1)S(1)}, bf16[128,512]{1,0:T(8,128)(2,1)S(1)}, u32[]{:S(2)}, u32[]{:S(2)}) collective-permute-start(bf16[128,512]{1,0:T(8,128)(2,1)S(1)} %copy-done.8), channel_id=1, source_target_pairs={{0,6},{2,70},{4,2},{6,66},{64,4},{66,68},{68,0},{70,64},{1,7},{3,7... | collective-permute-start | bytes 393224 | tf_op jit(solution)/shard_map/ppermute | solution.py:126
  34.0 23.7 %collective-permute-start.3 = (bf16[128,512]{1,0:T(8,128)(2,1)S(1)}, bf16[128,512]{1,0:T(8,128)(2,1)S(1)}, u32[]{:S(2)}, u32[]{:S(2)}) collective-permute-start(bf16[128,512]{1,0:T(8,128)(2,1)S(1)} %copy-done.8), channel_id=1, source_target_pairs={{0,2},{2,66},{4,6},{6,70},{64,0},{66,64},{68,4},{70,68},{1,3},{3,6... | collective-permute-start | bytes 393224 | tf_op jit(solution)/shard_map/ppermute | solution.py:126
  37.0 20.7 %collective-permute-start.2 = (bf16[128,512]{1,0:T(8,128)(2,1)S(1)}, bf16[128,512]{1,0:T(8,128)(2,1)S(1)}, u32[]{:S(2)}, u32[]{:S(2)}) collective-permute-start(bf16[128,512]{1,0:T(8,128)(2,1)S(1)} %copy-done.8), channel_id=1, source_target_pairs={{0,0},{2,64},{4,4},{6,68},{64,2},{66,66},{68,6},{70,70},{1,1},{3,6... | collective-permute-start | bytes 393224 | tf_op jit(solution)/shard_map/ppermute | solution.py:126
  37.6 38.2 %collective-permute-start.5 = (bf16[1024,512]{1,0:T(8,128)(2,1)S(1)}, bf16[1024,512]{1,0:T(8,128)(2,1)}, u32[]{:S(2)}, u32[]{:S(2)}) collective-permute-start(bf16[1024,512]{1,0:T(8,128)(2,1)S(1)} %copy-done.2), channel_id=1, source_target_pairs={{0,1},{1,0},{2,3},{3,2},{4,5},{5,4},{6,7},{7,6},{8,9},{9,8},{10,11... | collective-permute-start | bytes 3145736 | tf_op jit(solution)/shard_map/ppermute | solution.py:49
  57.7 18.1 %collective-permute-start.6 = (bf16[1024,512]{1,0:T(8,128)(2,1)}, bf16[1024,512]{1,0:T(8,128)(2,1)}, u32[]{:S(2)}, u32[]{:S(2)}) collective-permute-start(bf16[1024,512]{1,0:T(8,128)(2,1)} %collective-permute-done.1.far_ref), channel_id=1, source_target_pairs={{0,1},{1,0},{2,3},{3,2},{4,5},{5,4},{6,7},{7,6},{8,9},{9,8},{10,11... | collective-permute-start | bytes 3145736 | tf_op jit(solution)/shard_map/ppermute | solution.py:49
  62.4 12.6 %collective-permute-start.7 = (bf16[128,512]{1,0:T(8,128)(2,1)S(1)}, bf16[128,512]{1,0:T(8,128)(2,1)S(1)}, u32[]{:S(2)}, u32[]{:S(2)}) collective-permute-start(bf16[128,512]{1,0:T(8,128)(2,1)S(1)} %copy-done.8), channel_id=1, source_target_pairs={{0,4},{2,68},{4,0},{6,64},{64,6},{66,70},{68,2},{70,66},{1,5},{3,6... | collective-permute-start | bytes 393224 | tf_op jit(solution)/shard_map/ppermute | solution.py:126
  75.9 10.4 %collective-permute-start.8 = (f32[48,128]{1,0:T(8,128)S(1)}, f32[48,128]{1,0:T(8,128)S(1)}, u32[]{:S(2)}, u32[]{:S(2)}) collective-permute-start(f32[48,128]{1,0:T(8,128)S(1)} %convert_reduce_fusion.1), channel_id=1, source_target_pairs={{0,64},{64,0},{1,65},{65,1},{2,66},{66,2},{3,67},{67,3},{4,68},{68... | collective-permute-start | bytes 73736 | tf_op jit(solution)/shard_map/ppermute | solution.py:49
  87.1 43.5 %all-to-all-start.1 = ((bf16[32,176,128]{2,1,0:T(8,128)(2,1)}), bf16[32,176,128]{2,1,0:T(8,128)(2,1)S(1)}, u32[]{:S(2)}, u32[]{:S(2)}) async-start(bf16[32,176,128]{2,1,0:T(8,128)(2,1)} %broadcast_dynamic-update-slice_fusion), calls=%async_computation.1 | async-start | bytes 2883584 | tf_op jit(solution)/shard_map/all_to_all | solution.py:37
  97.7 8.4 %collective-permute-start.9 = (bf16[256,512]{1,0:T(8,128)(2,1)S(1)}, bf16[256,512]{1,0:T(8,128)(2,1)S(1)}, u32[]{:S(2)}, u32[]{:S(2)}) collective-permute-start(bf16[256,512]{1,0:T(8,128)(2,1)S(1)} %pad_maximum_fusion.6), channel_id=1, source_target_pairs={{0,64},{64,0},{1,65},{65,1},{2,66},{66,2},{3,67},{67,3},{4,68},{68... | collective-permute-start | bytes 786440 | tf_op jit(solution)/shard_map/ppermute | solution.py:49
  106.9 23.8 %copy-start.6 = (bf16[128,128]{1,0:T(8,128)(2,1)S(1)}, bf16[128,128]{1,0:T(8,128)(2,1)}, u32[]{:S(2)}) copy-start(bf16[128,128]{1,0:T(8,128)(2,1)} %param.6) | copy-start | bytes 98308
  107.0 14.8 %collective-permute-start.10 = (bf16[128,512]{1,0:T(8,128)(2,1)S(1)}, bf16[128,512]{1,0:T(8,128)(2,1)S(1)}, u32[]{:S(2)}, u32[]{:S(2)}) collective-permute-start(bf16[128,512]{1,0:T(8,128)(2,1)S(1)} %get-tuple-element.72), channel_id=1, source_target_pairs={{0,0},{2,64},{4,4},{6,68},{64,2},{66,66},{68,6},{70,70},{1,1},{3,6... | collective-permute-start | bytes 393224 | tf_op jit(solution)/shard_map/ppermute | solution.py:147
  107.6 14.2 %collective-permute-start.13 = (bf16[128,512]{1,0:T(8,128)(2,1)S(1)}, bf16[128,512]{1,0:T(8,128)(2,1)S(1)}, u32[]{:S(2)}, u32[]{:S(2)}) collective-permute-start(bf16[128,512]{1,0:T(8,128)(2,1)S(1)} %get-tuple-element.73), channel_id=1, source_target_pairs={{0,68},{2,4},{4,64},{6,0},{64,70},{66,6},{68,66},{70,2},{1,69},{3,... | collective-permute-start | bytes 393224 | tf_op jit(solution)/shard_map/ppermute | solution.py:147
  113.7 15.2 %collective-permute-start.12 = (bf16[128,512]{1,0:T(8,128)(2,1)S(1)}, bf16[128,512]{1,0:T(8,128)(2,1)S(1)}, u32[]{:S(2)}, u32[]{:S(2)}) collective-permute-start(bf16[128,512]{1,0:T(8,128)(2,1)S(1)} %get-tuple-element.74), channel_id=1, source_target_pairs={{0,4},{2,68},{4,0},{6,64},{64,6},{66,70},{68,2},{70,66},{1,5},{3,6... | collective-permute-start | bytes 393224 | tf_op jit(solution)/shard_map/ppermute | solution.py:147
  119.9 10.7 %collective-permute-start.11 = (bf16[128,512]{1,0:T(8,128)(2,1)S(1)}, bf16[128,512]{1,0:T(8,128)(2,1)S(1)}, u32[]{:S(2)}, u32[]{:S(2)}) collective-permute-start(bf16[128,512]{1,0:T(8,128)(2,1)S(1)} %get-tuple-element.75), channel_id=1, source_target_pairs={{0,64},{2,0},{4,68},{6,4},{64,66},{66,2},{68,70},{70,6},{1,65},{3,... | collective-permute-start | bytes 393224 | tf_op jit(solution)/shard_map/ppermute | solution.py:147
  132.2 13.8 %all-to-all-start.2 = ((bf16[4,512,128]{2,1,0:T(8,128)(2,1)}), bf16[4,512,128]{2,1,0:T(8,128)(2,1)S(1)}, u32[]{:S(2)}, u32[]{:S(2)}) async-start(bf16[4,512,128]{2,1,0:T(8,128)(2,1)} %broadcast_in_dim.8), calls=%async_computation.2 | async-start | bytes 1048576 | tf_op jit(solution)/shard_map/all_to_all | solution.py:37
  135.8 10.2 %copy-start.5 = (bf16[512,512]{1,0:T(8,128)(2,1)S(1)}, bf16[512,512]{1,0:T(8,128)(2,1)}, u32[]{:S(2)}) copy-start(bf16[512,512]{1,0:T(8,128)(2,1)} %pad_maximum_fusion.4) | copy-start | bytes 1572868
  135.9 21.2 %collective-permute-start.14 = (f32[128,128]{0,1:T(8,128)S(1)}, f32[128,128]{0,1:T(8,128)S(1)}, u32[]{:S(2)}, u32[]{:S(2)}) collective-permute-start(f32[128,128]{0,1:T(8,128)S(1)} %copy.32), channel_id=1, source_target_pairs={{0,0},{64,2},{256,4},{320,6},{128,64},{192,66},{384,68},{448,70},{... | collective-permute-start | bytes 196616 | tf_op jit(solution)/shard_map/ppermute | solution.py:160
  146.0 11.2 %copy-start.7 = (bf16[128,256]{1,0:T(8,128)(2,1)S(1)}, bf16[128,256]{1,0:T(8,128)(2,1)}, u32[]{:S(2)}) copy-start(bf16[128,256]{1,0:T(8,128)(2,1)} %param.8) | copy-start | bytes 196612
  146.4 11.6 %collective-permute-start.15 = (bf16[256,640]{1,0:T(8,128)(2,1)S(1)}, bf16[256,640]{1,0:T(8,128)(2,1)S(1)}, u32[]{:S(2)}, u32[]{:S(2)}) collective-permute-start(bf16[256,640]{1,0:T(8,128)(2,1)S(1)} %fusion.7), channel_id=1, source_target_pairs={{0,1},{1,0},{2,3},{3,2},{4,5},{5,4},{6,7},{7,6},{8,9},{9,8},{10,11... | collective-permute-start | bytes 983048 | tf_op jit(solution)/shard_map/ppermute | solution.py:49
  (4 other events, 10.8 us)

commit v10 on v7

--- a/solution.py
+++ b/solution.py
@@ -142,7 +142,6 @@
     frozen = jnp.stack([f.reshape(2, batch, hidden) for f in frozen], axis=1).reshape(4, batch, hidden)
     kept = [lax.dynamic_index_in_dim(arrived, high ^ ylo ^ p, 0, keepdims=False) for p in (0, 2, 1, 3)]
     column = jnp.concatenate([*kept[:2], trade(jnp.concatenate(kept[2:]), "ylo")])
-    frozen, column = lax.optimization_barrier((frozen, column))
     frozen = sum(
         lax.ppermute(
             lax.dynamic_index_in_dim(frozen, high ^ j ^ ylo, 0, keepdims=False), ("ylo", "yhi"), HOME[j]
@@ -169,6 +168,7 @@
     kept_rest = (kept - kept_high.astype(F32)).astype(BF16)
     down_part = dot(back_low, kept_high, ((1,), (1,))) + dot(back_low, kept_rest, ((1,), (1,)))
     pair = exchange(to_all(jnp.concatenate([low, down_part.astype(BF16)], axis=0), "yhi"), "yhi")
+    pair, column = lax.optimization_barrier((pair, column))
     lows = pair[:, :rank].reshape(2, 2, rank, batch)
     lows = [lax.dynamic_index_in_dim(lows, l, 1, keepdims=False) for l in (ylo, 1 - ylo)]
     up_part = dot(jnp.concatenate([*lows[0], *lows[1]], axis=1), column, ((1,), (0,)))

time: 157 us -> 158 us (level)
  waiting for transfers between devices: 34.9 us -> 32.6 us
  other arithmetic: 4.77 us -> 6.42 us
    ppermute x4, waiting for transfers between devices: 8.86 us -> 4.9 us  [local(): lax.ppermute(lax.dynamic_index_in_dim(frozen, high ^ j ^ ylo, 0, keepdims...]
    all_to_all x3, waiting for transfers between devices: 9.36 us -> 11.9 us  [exchange(): return lax.all_to_all(pieces, axes, split_axis=0, concat_axis=0, tiled=True)]
  transfers between devices with their start and end apart: 19 -> 19, of which waited for: 8 -> 7; matrix products, arithmetic and copies ran while one was open for 9% -> 11% of each run, Pallas kernels for 4% -> 4%
where the time goes in v10:
time: 158 us; the launch traced here: 155 us
  starting transfers between devices  92.7 us (59%)
  waiting for transfers between devices  32.6 us (21%)
  matrix products  10.6 us (7%)
  other arithmetic  6.42 us (4%)
  Pallas kernels  6.35 us (4%)
  local copies, waits for them, and re-layouts  4.78 us (3%)
    all_to_all x3, starting transfers between devices, exchange(): return lax.all_to_all(pieces, axes, split_axis=0, concat_axis=0, tiled=True)  34.1 us
    ppermute x6, starting transfers between devices, trade(): return lax.ppermute(block, axis, [(0, 1), (1, 0)])  30.2 us
    ppermute x4, waiting for transfers between devices, local(): arrived = [lax.ppermute(later, ('ylo', 'yhi'), SPREAD[j]) for j in range(4)]  14.6 us
    ppermute x4, starting transfers between devices, local(): lax.ppermute(lax.dynamic_index_in_dim(frozen, high ^ j ^ ylo, 0, keepdims...  13.7 us
    ppermute x4, starting transfers between devices, local(): arrived = [lax.ppermute(later, ('ylo', 'yhi'), SPREAD[j]) for j in range(4)]  12.5 us
    all_to_all x3, waiting for transfers between devices, exchange(): return lax.all_to_all(pieces, axes, split_axis=0, concat_axis=0, tiled=True)  11.9 us
    dot_general x13, matrix products, dot(): lax.dot_general(left, right, ((contract[0], contract[1]), ((), ())), pref...  10.6 us
    pallas_call x1, Pallas kernels, slabs_of(): pl.pallas_call(slab_kernel, grid_spec=pltpu.PrefetchScalarGridSpec(num_sc...  6.35 us
  transfers between devices with their start and end apart: 19, of which 7 were waited for; matrix products, arithmetic and copies ran while one was open for 11% of the time, Pallas kernels for 4%

profile of v10, /device:TPU:1, one launch (start us, length us, event | category | flops | bytes accessed | tf_op | source)
XLA Modules:
  0.0 154.7 jit_solution(18218037834031126727)
XLA Ops:
  7.0 20.4 %all-to-all-start = ((bf16[32,176,128]{2,1,0:T(8,128)(2,1)}), bf16[32,176,128]{2,1,0:T(8,128)(2,1)S(1)}, u32[]{:S(2)}, u32[]{:S(2)}) async-start(bf16[32,176,128]{2,1,0:T(8,128)(2,1)} %pad_maximum_fusion), calls=%async_computation | async-start | bytes 2883584 | tf_op jit(solution)/shard_map/all_to_all | solution.py:37
  27.4 2.3 %collective-permute-start.1 = (bf16[1024,512]{1,0:T(8,128)(2,1)S(1)}, bf16[1024,512]{1,0:T(8,128)(2,1)}, u32[]{:S(2)}, u32[]{:S(2)}) collective-permute-start(bf16[1024,512]{1,0:T(8,128)(2,1)S(1)} %copy-done.2), channel_id=1, source_target_pairs={{0,64},{64,0},{1,65},{65,1},{2,66},{66,2},{3,67},{67,3},{4,68},{68... | collective-permute-start | bytes 3145736 | tf_op jit(solution)/shard_map/ppermute | solution.py:49
  29.7 4.3 %collective-permute-start.5 = (bf16[128,512]{1,0:T(8,128)(2,1)S(1)}, bf16[128,512]{1,0:T(8,128)(2,1)S(1)}, u32[]{:S(2)}, u32[]{:S(2)}) collective-permute-start(bf16[128,512]{1,0:T(8,128)(2,1)S(1)} %copy-done.8), channel_id=1, source_target_pairs={{0,6},{2,70},{4,2},{6,66},{64,4},{66,68},{68,0},{70,64},{1,7},{3,7... | collective-permute-start | bytes 393224 | tf_op jit(solution)/shard_map/ppermute | solution.py:126
  34.0 5.7 %collective-permute-start.4 = (bf16[128,512]{1,0:T(8,128)(2,1)S(1)}, bf16[128,512]{1,0:T(8,128)(2,1)S(1)}, u32[]{:S(2)}, u32[]{:S(2)}) collective-permute-start(bf16[128,512]{1,0:T(8,128)(2,1)S(1)} %copy-done.8), channel_id=1, source_target_pairs={{0,4},{2,68},{4,0},{6,64},{64,6},{66,70},{68,2},{70,66},{1,5},{3,6... | collective-permute-start | bytes 393224 | tf_op jit(solution)/shard_map/ppermute | solution.py:126
  39.7 1.9 %collective-permute-start.3 = (bf16[128,512]{1,0:T(8,128)(2,1)S(1)}, bf16[128,512]{1,0:T(8,128)(2,1)S(1)}, u32[]{:S(2)}, u32[]{:S(2)}) collective-permute-start(bf16[128,512]{1,0:T(8,128)(2,1)S(1)} %copy-done.8), channel_id=1, source_target_pairs={{0,2},{2,66},{4,6},{6,70},{64,0},{66,64},{68,4},{70,68},{1,3},{3,6... | collective-permute-start | bytes 393224 | tf_op jit(solution)/shard_map/ppermute | solution.py:126
  42.3 4.9 %collective-permute-start.6 = (bf16[1024,512]{1,0:T(8,128)(2,1)S(1)}, bf16[1024,512]{1,0:T(8,128)(2,1)}, u32[]{:S(2)}, u32[]{:S(2)}) collective-permute-start(bf16[1024,512]{1,0:T(8,128)(2,1)S(1)} %copy-done.2), channel_id=1, source_target_pairs={{0,1},{1,0},{2,3},{3,2},{4,5},{5,4},{6,7},{7,6},{8,9},{9,8},{10,11... | collective-permute-start | bytes 3145736 | tf_op jit(solution)/shard_map/ppermute | solution.py:49
  47.2 12.1 %collective-permute-done.4 = bf16[128,512]{1,0:T(8,128)(2,1)S(1)} collective-permute-done((bf16[128,512]{1,0:T(8,128)(2,1)S(1)}, bf16[128,512]{1,0:T(8,128)(2,1)S(1)}, u32[]{:S(2)}, u32[]{:S(2)}) %collective-permute-start.4) | collective-permute-done | bytes 131104 | tf_op jit(solution)/shard_map/ppermute | solution.py:126
  59.3 2.5 %collective-permute-done.3 = bf16[128,512]{1,0:T(8,128)(2,1)S(1)} collective-permute-done((bf16[128,512]{1,0:T(8,128)(2,1)S(1)}, bf16[128,512]{1,0:T(8,128)(2,1)S(1)}, u32[]{:S(2)}, u32[]{:S(2)}) %collective-permute-start.3) | collective-permute-done | bytes 131104 | tf_op jit(solution)/shard_map/ppermute | solution.py:126
  61.8 6.2 %collective-permute-start.7 = (bf16[1024,512]{1,0:T(8,128)(2,1)}, bf16[1024,512]{1,0:T(8,128)(2,1)}, u32[]{:S(2)}, u32[]{:S(2)}) collective-permute-start(bf16[1024,512]{1,0:T(8,128)(2,1)} %collective-permute-done.1.far_ref), channel_id=1, source_target_pairs={{0,1},{1,0},{2,3},{3,2},{4,5},{5,4},{6,7},{7,6},{8,9},{9,8},{10,11... | collective-permute-start | bytes 3145736 | tf_op jit(solution)/shard_map/ppermute | solution.py:49
  70.7 3.7 %collective-permute-start.8 = (f32[48,128]{1,0:T(8,128)S(1)}, f32[48,128]{1,0:T(8,128)S(1)}, u32[]{:S(2)}, u32[]{:S(2)}) collective-permute-start(f32[48,128]{1,0:T(8,128)S(1)} %convert_reduce_fusion.1), channel_id=1, source_target_pairs={{0,64},{64,0},{1,65},{65,1},{2,66},{66,2},{3,67},{67,3},{4,68},{68... | collective-permute-start | bytes 73736 | tf_op jit(solution)/shard_map/ppermute | solution.py:49
  74.4 6.4 %shard_map.93 = bf16[2,2,8,176,128]{4,3,2,1,0:T(8,128)(2,1)} custom-call(s32[2]{0:T(128)} %pad_add_fusion.where_ref, bf16[1024,512]{1,0:T(8,128)(2,1)} %near_ref, bf16[1024,512]{1,0:T(8,128)(2,1)} %collective-permute-done.1.far_ref, bf16[1024,512]{1,0:T(8,128)(2,1)} %collective-permute-done.6.near_beside_ref, ...), custom_call_target="tpu_custom_call" | custom-call | flops 1073741824 | bytes 4194304 | tf_op jit(solution)/shard_map/pallas_call | solution.py:84
  81.6 9.2 %all-to-all-start.1 = ((bf16[32,176,128]{2,1,0:T(8,128)(2,1)}), bf16[32,176,128]{2,1,0:T(8,128)(2,1)S(1)}, u32[]{:S(2)}, u32[]{:S(2)}) async-start(bf16[32,176,128]{2,1,0:T(8,128)(2,1)} %broadcast_dynamic-update-slice_fusion), calls=%async_computation.1 | async-start | bytes 2883584 | tf_op jit(solution)/shard_map/all_to_all | solution.py:37
  93.5 1.7 %fusion.10 = f32[256,512]{1,0:T(8,128)S(1)} fusion(bf16[1024,512]{1,0:T(8,128)(2,1)} %collective-permute-done.6.near_beside_ref, bf16[32,8,8,128]{3,2,1,0:T(8,128)(2,1)S(1)} %bitcast.96), kind=kOutput, calls=%fused_computation.23 | convolution fusion | flops 268435456 | bytes 2097152 | tf_op jit(solution)/shard_map/dot_general | solution.py:33
  95.1 1.7 %fusion.1 = bf16[256,512]{1,0:T(8,128)(2,1)S(1)} fusion(f32[256,512]{1,0:T(8,128)S(1)} %fusion.8, bf16[1024,512]{1,0:T(8,128)(2,1)} %collective-permute-done.1.far_ref, bf16[32,8,8,128]{3,2,1,0:T(8,128)(2,1)S(1)} %bitcast.93), kind=kOutput, calls=%fused_computation.5 | convolution fusion | flops 268697600 | bytes 2359296 | tf_op jit(solution)/shard_map/dot_general | solution.py:33
  98.3 5.3 %collective-permute-start.12 = (bf16[128,512]{1,0:T(8,128)(2,1)S(1)}, bf16[128,512]{1,0:T(8,128)(2,1)S(1)}, u32[]{:S(2)}, u32[]{:S(2)}) collective-permute-start(bf16[128,512]{1,0:T(8,128)(2,1)S(1)} %get-tuple-element.79), channel_id=1, source_target_pairs={{0,68},{2,4},{4,64},{6,0},{64,70},{66,6},{68,66},{70,2},{1,69},{3,... | collective-permute-start | bytes 393224 | tf_op jit(solution)/shard_map/ppermute | solution.py:146
  103.6 5.7 %collective-permute-start.11 = (bf16[128,512]{1,0:T(8,128)(2,1)S(1)}, bf16[128,512]{1,0:T(8,128)(2,1)S(1)}, u32[]{:S(2)}, u32[]{:S(2)}) collective-permute-start(bf16[128,512]{1,0:T(8,128)(2,1)S(1)} %get-tuple-element.80), channel_id=1, source_target_pairs={{0,4},{2,68},{4,0},{6,64},{64,6},{66,70},{68,2},{70,66},{1,5},{3,6... | collective-permute-start | bytes 393224 | tf_op jit(solution)/shard_map/ppermute | solution.py:146
  109.3 1.9 %collective-permute-start.10 = (bf16[128,512]{1,0:T(8,128)(2,1)S(1)}, bf16[128,512]{1,0:T(8,128)(2,1)S(1)}, u32[]{:S(2)}, u32[]{:S(2)}) collective-permute-start(bf16[128,512]{1,0:T(8,128)(2,1)S(1)} %get-tuple-element.81), channel_id=1, source_target_pairs={{0,64},{2,0},{4,68},{6,4},{64,66},{66,2},{68,70},{70,6},{1,65},{3,... | collective-permute-start | bytes 393224 | tf_op jit(solution)/shard_map/ppermute | solution.py:146
  112.0 3.1 %collective-permute-start.14 = (bf16[256,512]{1,0:T(8,128)(2,1)}, bf16[256,512]{1,0:T(8,128)(2,1)}, u32[]{:S(2)}, u32[]{:S(2)}) collective-permute-start(bf16[256,512]{1,0:T(8,128)(2,1)} %pad_maximum_fusion.6), channel_id=1, source_target_pairs={{0,64},{64,0},{1,65},{65,1},{2,66},{66,2},{3,67},{67,3},{4,68},{68... | collective-permute-start | bytes 786440 | tf_op jit(solution)/shard_map/ppermute | solution.py:49
  115.1 3.8 %collective-permute-done.11 = bf16[128,512]{1,0:T(8,128)(2,1)S(1)} collective-permute-done((bf16[128,512]{1,0:T(8,128)(2,1)S(1)}, bf16[128,512]{1,0:T(8,128)(2,1)S(1)}, u32[]{:S(2)}, u32[]{:S(2)}) %collective-permute-start.11) | collective-permute-done | bytes 131104 | tf_op jit(solution)/shard_map/ppermute | solution.py:146
  120.1 4.8 %all-to-all-done.1 = bf16[32,176,128]{2,1,0:T(8,128)(2,1)S(1)} async-done(((bf16[32,176,128]{2,1,0:T(8,128)(2,1)}), bf16[32,176,128]{2,1,0:T(8,128)(2,1)S(1)}, u32[]{:S(2)}, u32[]{:S(2)}) %all-to-all-start.1) | async-done | bytes 1441824 | tf_op jit(solution)/shard_map/all_to_all | solution.py:37
  126.4 4.5 %all-to-all-start.2 = ((bf16[4,512,128]{2,1,0:T(8,128)(2,1)}), bf16[4,512,128]{2,1,0:T(8,128)(2,1)S(1)}, u32[]{:S(2)}, u32[]{:S(2)}) async-start(bf16[4,512,128]{2,1,0:T(8,128)(2,1)} %broadcast_in_dim.8), calls=%async_computation.2 | async-start | bytes 1048576 | tf_op jit(solution)/shard_map/all_to_all | solution.py:37
  130.9 1.8 %pad_maximum_fusion.4 = bf16[512,512]{1,0:T(8,128)(2,1)} fusion(bf16[256,512]{1,0:T(8,128)(2,1)} %collective-permute-done.14, bf16[128,512]{1,0:T(8,128)(2,1)S(1)} %get-tuple-element.77, bf16[128,512]{1,0:T(8,128)(2,1)S(1)} %get-tuple-element.74), kind=kLoop, calls=%fused_computation.29 | loop fusion | flops 1572864 | bytes 1048576 | tf_op jit(solution)/shard_map/concatenate | solution.py:144
  133.9 7.1 %all-to-all-done.2 = bf16[4,512,128]{2,1,0:T(8,128)(2,1)S(1)} async-done(((bf16[4,512,128]{2,1,0:T(8,128)(2,1)}), bf16[4,512,128]{2,1,0:T(8,128)(2,1)S(1)}, u32[]{:S(2)}, u32[]{:S(2)}) %all-to-all-start.2) | async-done | bytes 524320 | tf_op jit(solution)/shard_map/all_to_all | solution.py:37
  141.4 10.0 %collective-permute-start.15 = (bf16[256,640]{1,0:T(8,128)(2,1)S(1)}, bf16[256,640]{1,0:T(8,128)(2,1)S(1)}, u32[]{:S(2)}, u32[]{:S(2)}) collective-permute-start(bf16[256,640]{1,0:T(8,128)(2,1)S(1)} %fusion.7), channel_id=1, source_target_pairs={{0,1},{1,0},{2,3},{3,2},{4,5},{5,4},{6,7},{7,6},{8,9},{9,8},{10,11... | collective-permute-start | bytes 983048 | tf_op jit(solution)/shard_map/ppermute | solution.py:49
  (79 shorter events, 22.6 us)
Async XLA Ops:
  0.6 4.9 %collective-permute-start = (bf16[128,128]{1,0:T(8,128)(2,1)}, bf16[128,128]{1,0:T(8,128)(2,1)S(1)}, u32[]{:S(2)}, u32[]{:S(2)}) collective-permute-start(bf16[128,128]{1,0:T(8,128)(2,1)} %param.6), channel_id=1, source_target_pairs={{0,0},{2,64},{4,256},{6,320},{64,128},{66,192},{68,384},{70,448},{... | collective-permute-start | bytes 98312 | tf_op jit(solution)/shard_map/ppermute | solution.py:110
  7.0 20.4 %copy-start.2 = (bf16[1024,512]{1,0:T(8,128)(2,1)S(1)}, bf16[1024,512]{1,0:T(8,128)(2,1)}, u32[]{:S(2)}) copy-start(bf16[1024,512]{1,0:T(8,128)(2,1)} %near_ref) | copy-start | bytes 3145732
  7.0 22.7 %copy-start.8 = (bf16[128,512]{1,0:T(8,128)(2,1)S(1)}, bf16[128,512]{1,0:T(8,128)(2,1)}, u32[]{:S(2)}) copy-start(bf16[128,512]{1,0:T(8,128)(2,1)} %param.10) | copy-start | bytes 393220
  7.0 63.6 %all-to-all-start = ((bf16[32,176,128]{2,1,0:T(8,128)(2,1)}), bf16[32,176,128]{2,1,0:T(8,128)(2,1)S(1)}, u32[]{:S(2)}, u32[]{:S(2)}) async-start(bf16[32,176,128]{2,1,0:T(8,128)(2,1)} %pad_maximum_fusion), calls=%async_computation | async-start | bytes 2883584 | tf_op jit(solution)/shard_map/all_to_all | solution.py:37
  27.4 34.4 %collective-permute-start.1 = (bf16[1024,512]{1,0:T(8,128)(2,1)S(1)}, bf16[1024,512]{1,0:T(8,128)(2,1)}, u32[]{:S(2)}, u32[]{:S(2)}) collective-permute-start(bf16[1024,512]{1,0:T(8,128)(2,1)S(1)} %copy-done.2), channel_id=1, source_target_pairs={{0,64},{64,0},{1,65},{65,1},{2,66},{66,2},{3,67},{67,3},{4,68},{68... | collective-permute-start | bytes 3145736 | tf_op jit(solution)/shard_map/ppermute | solution.py:49
  29.7 12.6 %collective-permute-start.5 = (bf16[128,512]{1,0:T(8,128)(2,1)S(1)}, bf16[128,512]{1,0:T(8,128)(2,1)S(1)}, u32[]{:S(2)}, u32[]{:S(2)}) collective-permute-start(bf16[128,512]{1,0:T(8,128)(2,1)S(1)} %copy-done.8), channel_id=1, source_target_pairs={{0,6},{2,70},{4,2},{6,66},{64,4},{66,68},{68,0},{70,64},{1,7},{3,7... | collective-permute-start | bytes 393224 | tf_op jit(solution)/shard_map/ppermute | solution.py:126
  34.0 25.3 %collective-permute-start.4 = (bf16[128,512]{1,0:T(8,128)(2,1)S(1)}, bf16[128,512]{1,0:T(8,128)(2,1)S(1)}, u32[]{:S(2)}, u32[]{:S(2)}) collective-permute-start(bf16[128,512]{1,0:T(8,128)(2,1)S(1)} %copy-done.8), channel_id=1, source_target_pairs={{0,4},{2,68},{4,0},{6,64},{64,6},{66,70},{68,2},{70,66},{1,5},{3,6... | collective-permute-start | bytes 393224 | tf_op jit(solution)/shard_map/ppermute | solution.py:126
  39.7 22.1 %collective-permute-start.3 = (bf16[128,512]{1,0:T(8,128)(2,1)S(1)}, bf16[128,512]{1,0:T(8,128)(2,1)S(1)}, u32[]{:S(2)}, u32[]{:S(2)}) collective-permute-start(bf16[128,512]{1,0:T(8,128)(2,1)S(1)} %copy-done.8), channel_id=1, source_target_pairs={{0,2},{2,66},{4,6},{6,70},{64,0},{66,64},{68,4},{70,68},{1,3},{3,6... | collective-permute-start | bytes 393224 | tf_op jit(solution)/shard_map/ppermute | solution.py:126
  41.6 20.2 %collective-permute-start.2 = (bf16[128,512]{1,0:T(8,128)(2,1)S(1)}, bf16[128,512]{1,0:T(8,128)(2,1)S(1)}, u32[]{:S(2)}, u32[]{:S(2)}) collective-permute-start(bf16[128,512]{1,0:T(8,128)(2,1)S(1)} %copy-done.8), channel_id=1, source_target_pairs={{0,0},{2,64},{4,4},{6,68},{64,2},{66,66},{68,6},{70,70},{1,1},{3,6... | collective-permute-start | bytes 393224 | tf_op jit(solution)/shard_map/ppermute | solution.py:126
  42.3 27.2 %collective-permute-start.6 = (bf16[1024,512]{1,0:T(8,128)(2,1)S(1)}, bf16[1024,512]{1,0:T(8,128)(2,1)}, u32[]{:S(2)}, u32[]{:S(2)}) collective-permute-start(bf16[1024,512]{1,0:T(8,128)(2,1)S(1)} %copy-done.2), channel_id=1, source_target_pairs={{0,1},{1,0},{2,3},{3,2},{4,5},{5,4},{6,7},{7,6},{8,9},{9,8},{10,11... | collective-permute-start | bytes 3145736 | tf_op jit(solution)/shard_map/ppermute | solution.py:49
  61.8 8.8 %collective-permute-start.7 = (bf16[1024,512]{1,0:T(8,128)(2,1)}, bf16[1024,512]{1,0:T(8,128)(2,1)}, u32[]{:S(2)}, u32[]{:S(2)}) collective-permute-start(bf16[1024,512]{1,0:T(8,128)(2,1)} %collective-permute-done.1.far_ref), channel_id=1, source_target_pairs={{0,1},{1,0},{2,3},{3,2},{4,5},{5,4},{6,7},{7,6},{8,9},{9,8},{10,11... | collective-permute-start | bytes 3145736 | tf_op jit(solution)/shard_map/ppermute | solution.py:49
  70.7 10.0 %collective-permute-start.8 = (f32[48,128]{1,0:T(8,128)S(1)}, f32[48,128]{1,0:T(8,128)S(1)}, u32[]{:S(2)}, u32[]{:S(2)}) collective-permute-start(f32[48,128]{1,0:T(8,128)S(1)} %convert_reduce_fusion.1), channel_id=1, source_target_pairs={{0,64},{64,0},{1,65},{65,1},{2,66},{66,2},{3,67},{67,3},{4,68},{68... | collective-permute-start | bytes 73736 | tf_op jit(solution)/shard_map/ppermute | solution.py:49
  81.6 43.3 %all-to-all-start.1 = ((bf16[32,176,128]{2,1,0:T(8,128)(2,1)}), bf16[32,176,128]{2,1,0:T(8,128)(2,1)S(1)}, u32[]{:S(2)}, u32[]{:S(2)}) async-start(bf16[32,176,128]{2,1,0:T(8,128)(2,1)} %broadcast_dynamic-update-slice_fusion), calls=%async_computation.1 | async-start | bytes 2883584 | tf_op jit(solution)/shard_map/all_to_all | solution.py:37
  97.4 13.9 %copy-start.1 = (bf16[4,128,512]{2,1,0:T(8,128)(2,1)S(1)}, bf16[4,128,512]{2,1,0:T(8,128)(2,1)}, u32[]{:S(2)}) copy-start(bf16[4,128,512]{2,1,0:T(8,128)(2,1)} %pad_maximum_fusion.2.arrived_ref) | copy-start | bytes 1572868
  97.5 17.6 %collective-permute-start.9 = (bf16[128,512]{1,0:T(8,128)(2,1)S(1)}, bf16[128,512]{1,0:T(8,128)(2,1)S(1)}, u32[]{:S(2)}, u32[]{:S(2)}) collective-permute-start(bf16[128,512]{1,0:T(8,128)(2,1)S(1)} %get-tuple-element.78), channel_id=1, source_target_pairs={{0,0},{2,64},{4,4},{6,68},{64,2},{66,66},{68,6},{70,70},{1,1},{3,6... | collective-permute-start | bytes 393224 | tf_op jit(solution)/shard_map/ppermute | solution.py:146
  98.3 16.9 %collective-permute-start.12 = (bf16[128,512]{1,0:T(8,128)(2,1)S(1)}, bf16[128,512]{1,0:T(8,128)(2,1)S(1)}, u32[]{:S(2)}, u32[]{:S(2)}) collective-permute-start(bf16[128,512]{1,0:T(8,128)(2,1)S(1)} %get-tuple-element.79), channel_id=1, source_target_pairs={{0,68},{2,4},{4,64},{6,0},{64,70},{66,6},{68,66},{70,2},{1,69},{3,... | collective-permute-start | bytes 393224 | tf_op jit(solution)/shard_map/ppermute | solution.py:146
  103.6 15.4 %collective-permute-start.11 = (bf16[128,512]{1,0:T(8,128)(2,1)S(1)}, bf16[128,512]{1,0:T(8,128)(2,1)S(1)}, u32[]{:S(2)}, u32[]{:S(2)}) collective-permute-start(bf16[128,512]{1,0:T(8,128)(2,1)S(1)} %get-tuple-element.80), channel_id=1, source_target_pairs={{0,4},{2,68},{4,0},{6,64},{64,6},{66,70},{68,2},{70,66},{1,5},{3,6... | collective-permute-start | bytes 393224 | tf_op jit(solution)/shard_map/ppermute | solution.py:146
  109.3 15.7 %copy-start.6 = (bf16[128,128]{1,0:T(8,128)(2,1)S(1)}, bf16[128,128]{1,0:T(8,128)(2,1)}, u32[]{:S(2)}) copy-start(bf16[128,128]{1,0:T(8,128)(2,1)} %param.6) | copy-start | bytes 98308
  109.3 10.7 %collective-permute-start.10 = (bf16[128,512]{1,0:T(8,128)(2,1)S(1)}, bf16[128,512]{1,0:T(8,128)(2,1)S(1)}, u32[]{:S(2)}, u32[]{:S(2)}) collective-permute-start(bf16[128,512]{1,0:T(8,128)(2,1)S(1)} %get-tuple-element.81), channel_id=1, source_target_pairs={{0,64},{2,0},{4,68},{6,4},{64,66},{66,2},{68,70},{70,6},{1,65},{3,... | collective-permute-start | bytes 393224 | tf_op jit(solution)/shard_map/ppermute | solution.py:146
  112.0 18.9 %collective-permute-start.14 = (bf16[256,512]{1,0:T(8,128)(2,1)}, bf16[256,512]{1,0:T(8,128)(2,1)}, u32[]{:S(2)}, u32[]{:S(2)}) collective-permute-start(bf16[256,512]{1,0:T(8,128)(2,1)} %pad_maximum_fusion.6), channel_id=1, source_target_pairs={{0,64},{64,0},{1,65},{65,1},{2,66},{66,2},{3,67},{67,3},{4,68},{68... | collective-permute-start | bytes 786440 | tf_op jit(solution)/shard_map/ppermute | solution.py:49
  126.4 14.5 %all-to-all-start.2 = ((bf16[4,512,128]{2,1,0:T(8,128)(2,1)}), bf16[4,512,128]{2,1,0:T(8,128)(2,1)S(1)}, u32[]{:S(2)}, u32[]{:S(2)}) async-start(bf16[4,512,128]{2,1,0:T(8,128)(2,1)} %broadcast_in_dim.8), calls=%async_computation.2 | async-start | bytes 1048576 | tf_op jit(solution)/shard_map/all_to_all | solution.py:37
  133.0 19.2 %collective-permute-start.13 = (f32[128,128]{0,1:T(8,128)S(1)}, f32[128,128]{0,1:T(8,128)S(1)}, u32[]{:S(2)}, u32[]{:S(2)}) collective-permute-start(f32[128,128]{0,1:T(8,128)S(1)} %copy.32), channel_id=1, source_target_pairs={{0,0},{64,2},{256,4},{320,6},{128,64},{192,66},{384,68},{448,70},{... | collective-permute-start | bytes 196616 | tf_op jit(solution)/shard_map/ppermute | solution.py:159
  141.1 11.1 %copy-start.7 = (bf16[128,256]{1,0:T(8,128)(2,1)S(1)}, bf16[128,256]{1,0:T(8,128)(2,1)}, u32[]{:S(2)}) copy-start(bf16[128,256]{1,0:T(8,128)(2,1)} %param.8) | copy-start | bytes 196612
  141.4 11.5 %collective-permute-start.15 = (bf16[256,640]{1,0:T(8,128)(2,1)S(1)}, bf16[256,640]{1,0:T(8,128)(2,1)S(1)}, u32[]{:S(2)}, u32[]{:S(2)}) collective-permute-start(bf16[256,640]{1,0:T(8,128)(2,1)S(1)} %fusion.7), channel_id=1, source_target_pairs={{0,1},{1,0},{2,3},{3,2},{4,5},{5,4},{6,7},{7,6},{8,9},{9,8},{10,11... | collective-permute-start | bytes 983048 | tf_op jit(solution)/shard_map/ppermute | solution.py:49
  (4 other events, 18.8 us)

commit v11 on v7

--- a/solution.py
+++ b/solution.py
@@ -75,7 +75,7 @@
 
 def slabs_of(core, first, own_core, other_core, arrived, extra):
     batch = arrived.shape[1]
-    block, take = batch, 4
+    block, take = batch, 8
     depth, hidden = own_core[0].shape
     steps = depth // (take * block)
     early = pl.BlockSpec((take * block, hidden), lambda s, r, _: (jnp.where(s == 0, r, steps - 1), 0))

time: 157 us -> 156 us (level)
  no operation moved by 1% of the time
where the time goes in v11:
time: 156 us; the launch traced here: 154 us
  starting transfers between devices  91.4 us (59%)
  waiting for transfers between devices  34.9 us (22%)
  matrix products  10.6 us (7%)
  Pallas kernels  5.41 us (3%)
  local copies, waits for them, and re-layouts  5.32 us (3%)
  other arithmetic  4.77 us (3%)
    all_to_all x3, starting transfers between devices, exchange(): return lax.all_to_all(pieces, axes, split_axis=0, concat_axis=0, tiled=True)  34 us
    ppermute x6, starting transfers between devices, trade(): return lax.ppermute(block, axis, [(0, 1), (1, 0)])  29 us
    ppermute x4, waiting for transfers between devices, local(): arrived = [lax.ppermute(later, ('ylo', 'yhi'), SPREAD[j]) for j in range(4)]  14.6 us
    ppermute x4, starting transfers between devices, local(): lax.ppermute(lax.dynamic_index_in_dim(frozen, high ^ j ^ ylo, 0, keepdims...  13.6 us
    ppermute x4, starting transfers between devices, local(): arrived = [lax.ppermute(later, ('ylo', 'yhi'), SPREAD[j]) for j in range(4)]  12.5 us
    dot_general x13, matrix products, dot(): lax.dot_general(left, right, ((contract[0], contract[1]), ((), ())), pref...  10.6 us
    all_to_all x3, waiting for transfers between devices, exchange(): return lax.all_to_all(pieces, axes, split_axis=0, concat_axis=0, tiled=True)  9.31 us
    ppermute x4, waiting for transfers between devices, local(): lax.ppermute(lax.dynamic_index_in_dim(frozen, high ^ j ^ ylo, 0, keepdims...  8.88 us
  transfers between devices with their start and end apart: 19, of which 8 were waited for; matrix products, arithmetic and copies ran while one was open for 9% of the time, Pallas kernels for 4%

profile of v11, /device:TPU:1, one launch (start us, length us, event | category | flops | bytes accessed | tf_op | source)
XLA Modules:
  0.0 153.6 jit_solution(3489514297496017247)
XLA Ops:
  0.6 1.5 %collective-permute-start = (bf16[128,128]{1,0:T(8,128)(2,1)}, bf16[128,128]{1,0:T(8,128)(2,1)S(1)}, u32[]{:S(2)}, u32[]{:S(2)}) collective-permute-start(bf16[128,128]{1,0:T(8,128)(2,1)} %param.6), channel_id=1, source_target_pairs={{0,0},{2,64},{4,256},{6,320},{64,128},{66,192},{68,384},{70,448},{... | collective-permute-start | bytes 98312 | tf_op jit(solution)/shard_map/ppermute | solution.py:110
  7.0 20.4 %all-to-all-start = ((bf16[32,176,128]{2,1,0:T(8,128)(2,1)}), bf16[32,176,128]{2,1,0:T(8,128)(2,1)S(1)}, u32[]{:S(2)}, u32[]{:S(2)}) async-start(bf16[32,176,128]{2,1,0:T(8,128)(2,1)} %pad_maximum_fusion), calls=%async_computation | async-start | bytes 2883584 | tf_op jit(solution)/shard_map/all_to_all | solution.py:37
  27.4 2.3 %collective-permute-start.1 = (bf16[1024,512]{1,0:T(8,128)(2,1)S(1)}, bf16[1024,512]{1,0:T(8,128)(2,1)}, u32[]{:S(2)}, u32[]{:S(2)}) collective-permute-start(bf16[1024,512]{1,0:T(8,128)(2,1)S(1)} %copy-done.2), channel_id=1, source_target_pairs={{0,64},{64,0},{1,65},{65,1},{2,66},{66,2},{3,67},{67,3},{4,68},{68... | collective-permute-start | bytes 3145736 | tf_op jit(solution)/shard_map/ppermute | solution.py:49
  29.7 4.3 %collective-permute-start.5 = (bf16[128,512]{1,0:T(8,128)(2,1)S(1)}, bf16[128,512]{1,0:T(8,128)(2,1)S(1)}, u32[]{:S(2)}, u32[]{:S(2)}) collective-permute-start(bf16[128,512]{1,0:T(8,128)(2,1)S(1)} %copy-done.8), channel_id=1, source_target_pairs={{0,6},{2,70},{4,2},{6,66},{64,4},{66,68},{68,0},{70,64},{1,7},{3,7... | collective-permute-start | bytes 393224 | tf_op jit(solution)/shard_map/ppermute | solution.py:126
  34.0 5.7 %collective-permute-start.4 = (bf16[128,512]{1,0:T(8,128)(2,1)S(1)}, bf16[128,512]{1,0:T(8,128)(2,1)S(1)}, u32[]{:S(2)}, u32[]{:S(2)}) collective-permute-start(bf16[128,512]{1,0:T(8,128)(2,1)S(1)} %copy-done.8), channel_id=1, source_target_pairs={{0,4},{2,68},{4,0},{6,64},{64,6},{66,70},{68,2},{70,66},{1,5},{3,6... | collective-permute-start | bytes 393224 | tf_op jit(solution)/shard_map/ppermute | solution.py:126
  39.7 1.9 %collective-permute-start.3 = (bf16[128,512]{1,0:T(8,128)(2,1)S(1)}, bf16[128,512]{1,0:T(8,128)(2,1)S(1)}, u32[]{:S(2)}, u32[]{:S(2)}) collective-permute-start(bf16[128,512]{1,0:T(8,128)(2,1)S(1)} %copy-done.8), channel_id=1, source_target_pairs={{0,2},{2,66},{4,6},{6,70},{64,0},{66,64},{68,4},{70,68},{1,3},{3,6... | collective-permute-start | bytes 393224 | tf_op jit(solution)/shard_map/ppermute | solution.py:126
  42.3 4.9 %collective-permute-start.6 = (bf16[1024,512]{1,0:T(8,128)(2,1)S(1)}, bf16[1024,512]{1,0:T(8,128)(2,1)}, u32[]{:S(2)}, u32[]{:S(2)}) collective-permute-start(bf16[1024,512]{1,0:T(8,128)(2,1)S(1)} %copy-done.2), channel_id=1, source_target_pairs={{0,1},{1,0},{2,3},{3,2},{4,5},{5,4},{6,7},{7,6},{8,9},{9,8},{10,11... | collective-permute-start | bytes 3145736 | tf_op jit(solution)/shard_map/ppermute | solution.py:49
  47.2 12.1 %collective-permute-done.4 = bf16[128,512]{1,0:T(8,128)(2,1)S(1)} collective-permute-done((bf16[128,512]{1,0:T(8,128)(2,1)S(1)}, bf16[128,512]{1,0:T(8,128)(2,1)S(1)}, u32[]{:S(2)}, u32[]{:S(2)}) %collective-permute-start.4) | collective-permute-done | bytes 131104 | tf_op jit(solution)/shard_map/ppermute | solution.py:126
  59.3 2.5 %collective-permute-done.3 = bf16[128,512]{1,0:T(8,128)(2,1)S(1)} collective-permute-done((bf16[128,512]{1,0:T(8,128)(2,1)S(1)}, bf16[128,512]{1,0:T(8,128)(2,1)S(1)}, u32[]{:S(2)}, u32[]{:S(2)}) %collective-permute-start.3) | collective-permute-done | bytes 131104 | tf_op jit(solution)/shard_map/ppermute | solution.py:126
  61.8 6.2 %collective-permute-start.7 = (bf16[1024,512]{1,0:T(8,128)(2,1)}, bf16[1024,512]{1,0:T(8,128)(2,1)}, u32[]{:S(2)}, u32[]{:S(2)}) collective-permute-start(bf16[1024,512]{1,0:T(8,128)(2,1)} %collective-permute-done.1.far_ref), channel_id=1, source_target_pairs={{0,1},{1,0},{2,3},{3,2},{4,5},{5,4},{6,7},{7,6},{8,9},{9,8},{10,11... | collective-permute-start | bytes 3145736 | tf_op jit(solution)/shard_map/ppermute | solution.py:49
  70.7 3.7 %collective-permute-start.8 = (f32[48,128]{1,0:T(8,128)S(1)}, f32[48,128]{1,0:T(8,128)S(1)}, u32[]{:S(2)}, u32[]{:S(2)}) collective-permute-start(f32[48,128]{1,0:T(8,128)S(1)} %convert_reduce_fusion.1), channel_id=1, source_target_pairs={{0,64},{64,0},{1,65},{65,1},{2,66},{66,2},{3,67},{67,3},{4,68},{68... | collective-permute-start | bytes 73736 | tf_op jit(solution)/shard_map/ppermute | solution.py:49
  74.4 5.4 %shard_map.93 = bf16[2,2,8,176,128]{4,3,2,1,0:T(8,128)(2,1)} custom-call(s32[2]{0:T(128)} %pad_add_fusion.where_ref, bf16[1024,512]{1,0:T(8,128)(2,1)} %near_ref, bf16[1024,512]{1,0:T(8,128)(2,1)} %collective-permute-done.1.far_ref, bf16[1024,512]{1,0:T(8,128)(2,1)} %collective-permute-done.6.near_beside_ref, ...), custom_call_target="tpu_custom_call" | custom-call | flops 1073741824 | bytes 4194304 | tf_op jit(solution)/shard_map/pallas_call | solution.py:84
  80.6 9.2 %all-to-all-start.1 = ((bf16[32,176,128]{2,1,0:T(8,128)(2,1)}), bf16[32,176,128]{2,1,0:T(8,128)(2,1)S(1)}, u32[]{:S(2)}, u32[]{:S(2)}) async-start(bf16[32,176,128]{2,1,0:T(8,128)(2,1)} %broadcast_dynamic-update-slice_fusion), calls=%async_computation.1 | async-start | bytes 2883584 | tf_op jit(solution)/shard_map/all_to_all | solution.py:37
  91.2 1.9 %collective-permute-start.9 = (bf16[256,512]{1,0:T(8,128)(2,1)S(1)}, bf16[256,512]{1,0:T(8,128)(2,1)S(1)}, u32[]{:S(2)}, u32[]{:S(2)}) collective-permute-start(bf16[256,512]{1,0:T(8,128)(2,1)S(1)} %pad_maximum_fusion.6), channel_id=1, source_target_pairs={{0,64},{64,0},{1,65},{65,1},{2,66},{66,2},{3,67},{67,3},{4,68},{68... | collective-permute-start | bytes 786440 | tf_op jit(solution)/shard_map/ppermute | solution.py:49
  93.5 1.7 %fusion.8 = f32[256,512]{1,0:T(8,128)S(1)} fusion(bf16[1024,512]{1,0:T(8,128)(2,1)} %collective-permute-done.7.far_beside_ref, bf16[32,8,8,128]{3,2,1,0:T(8,128)(2,1)S(1)} %bitcast.95), kind=kOutput, calls=%fused_computation.21 | convolution fusion | flops 268435456 | bytes 2097152 | tf_op jit(solution)/shard_map/dot_general | solution.py:33
  95.1 1.7 %fusion.10 = f32[256,512]{1,0:T(8,128)S(1)} fusion(bf16[1024,512]{1,0:T(8,128)(2,1)} %collective-permute-done.6.near_beside_ref, bf16[32,8,8,128]{3,2,1,0:T(8,128)(2,1)S(1)} %bitcast.96), kind=kOutput, calls=%fused_computation.23 | convolution fusion | flops 268435456 | bytes 2097152 | tf_op jit(solution)/shard_map/dot_general | solution.py:33
  96.8 1.7 %fusion.1 = bf16[256,512]{1,0:T(8,128)(2,1)S(1)} fusion(f32[256,512]{1,0:T(8,128)S(1)} %fusion.8, bf16[1024,512]{1,0:T(8,128)(2,1)} %collective-permute-done.1.far_ref, bf16[32,8,8,128]{3,2,1,0:T(8,128)(2,1)S(1)} %bitcast.93), kind=kOutput, calls=%fused_computation.5 | convolution fusion | flops 268697600 | bytes 2359296 | tf_op jit(solution)/shard_map/dot_general | solution.py:33
  101.5 5.6 %collective-permute-start.13 = (bf16[128,512]{1,0:T(8,128)(2,1)S(1)}, bf16[128,512]{1,0:T(8,128)(2,1)S(1)}, u32[]{:S(2)}, u32[]{:S(2)}) collective-permute-start(bf16[128,512]{1,0:T(8,128)(2,1)S(1)} %get-tuple-element.75), channel_id=1, source_target_pairs={{0,68},{2,4},{4,64},{6,0},{64,70},{66,6},{68,66},{70,2},{1,69},{3,... | collective-permute-start | bytes 393224 | tf_op jit(solution)/shard_map/ppermute | solution.py:147
  107.1 5.4 %collective-permute-start.12 = (bf16[128,512]{1,0:T(8,128)(2,1)S(1)}, bf16[128,512]{1,0:T(8,128)(2,1)S(1)}, u32[]{:S(2)}, u32[]{:S(2)}) collective-permute-start(bf16[128,512]{1,0:T(8,128)(2,1)S(1)} %get-tuple-element.76), channel_id=1, source_target_pairs={{0,4},{2,68},{4,0},{6,64},{64,6},{66,70},{68,2},{70,66},{1,5},{3,6... | collective-permute-start | bytes 393224 | tf_op jit(solution)/shard_map/ppermute | solution.py:147
  112.5 1.9 %collective-permute-start.11 = (bf16[128,512]{1,0:T(8,128)(2,1)S(1)}, bf16[128,512]{1,0:T(8,128)(2,1)S(1)}, u32[]{:S(2)}, u32[]{:S(2)}) collective-permute-start(bf16[128,512]{1,0:T(8,128)(2,1)S(1)} %get-tuple-element.77), channel_id=1, source_target_pairs={{0,64},{2,0},{4,68},{6,4},{64,66},{66,2},{68,70},{70,6},{1,65},{3,... | collective-permute-start | bytes 393224 | tf_op jit(solution)/shard_map/ppermute | solution.py:147
  114.5 8.1 %collective-permute-done.12 = bf16[128,512]{1,0:T(8,128)(2,1)S(1)} collective-permute-done((bf16[128,512]{1,0:T(8,128)(2,1)S(1)}, bf16[128,512]{1,0:T(8,128)(2,1)S(1)}, u32[]{:S(2)}, u32[]{:S(2)}) %collective-permute-start.12) | collective-permute-done | bytes 131104 | tf_op jit(solution)/shard_map/ppermute | solution.py:147
  125.5 4.3 %all-to-all-start.2 = ((bf16[4,512,128]{2,1,0:T(8,128)(2,1)}), bf16[4,512,128]{2,1,0:T(8,128)(2,1)S(1)}, u32[]{:S(2)}, u32[]{:S(2)}) async-start(bf16[4,512,128]{2,1,0:T(8,128)(2,1)} %broadcast_in_dim.8), calls=%async_computation.2 | async-start | bytes 1048576 | tf_op jit(solution)/shard_map/all_to_all | solution.py:37
  131.1 8.8 %all-to-all-done.2 = bf16[4,512,128]{2,1,0:T(8,128)(2,1)S(1)} async-done(((bf16[4,512,128]{2,1,0:T(8,128)(2,1)}), bf16[4,512,128]{2,1,0:T(8,128)(2,1)S(1)}, u32[]{:S(2)}, u32[]{:S(2)}) %all-to-all-start.2) | async-done | bytes 524320 | tf_op jit(solution)/shard_map/all_to_all | solution.py:37
  140.4 10.0 %collective-permute-start.15 = (bf16[256,640]{1,0:T(8,128)(2,1)S(1)}, bf16[256,640]{1,0:T(8,128)(2,1)S(1)}, u32[]{:S(2)}, u32[]{:S(2)}) collective-permute-start(bf16[256,640]{1,0:T(8,128)(2,1)S(1)} %fusion.7), channel_id=1, source_target_pairs={{0,1},{1,0},{2,3},{3,2},{4,5},{5,4},{6,7},{7,6},{8,9},{9,8},{10,11... | collective-permute-start | bytes 983048 | tf_op jit(solution)/shard_map/ppermute | solution.py:49
  (79 shorter events, 21.2 us)
Async XLA Ops:
  0.6 4.9 %collective-permute-start = (bf16[128,128]{1,0:T(8,128)(2,1)}, bf16[128,128]{1,0:T(8,128)(2,1)S(1)}, u32[]{:S(2)}, u32[]{:S(2)}) collective-permute-start(bf16[128,128]{1,0:T(8,128)(2,1)} %param.6), channel_id=1, source_target_pairs={{0,0},{2,64},{4,256},{6,320},{64,128},{66,192},{68,384},{70,448},{... | collective-permute-start | bytes 98312 | tf_op jit(solution)/shard_map/ppermute | solution.py:110
  7.0 20.4 %copy-start.2 = (bf16[1024,512]{1,0:T(8,128)(2,1)S(1)}, bf16[1024,512]{1,0:T(8,128)(2,1)}, u32[]{:S(2)}) copy-start(bf16[1024,512]{1,0:T(8,128)(2,1)} %near_ref) | copy-start | bytes 3145732
  7.0 22.7 %copy-start.8 = (bf16[128,512]{1,0:T(8,128)(2,1)S(1)}, bf16[128,512]{1,0:T(8,128)(2,1)}, u32[]{:S(2)}) copy-start(bf16[128,512]{1,0:T(8,128)(2,1)} %param.10) | copy-start | bytes 393220
  7.0 63.6 %all-to-all-start = ((bf16[32,176,128]{2,1,0:T(8,128)(2,1)}), bf16[32,176,128]{2,1,0:T(8,128)(2,1)S(1)}, u32[]{:S(2)}, u32[]{:S(2)}) async-start(bf16[32,176,128]{2,1,0:T(8,128)(2,1)} %pad_maximum_fusion), calls=%async_computation | async-start | bytes 2883584 | tf_op jit(solution)/shard_map/all_to_all | solution.py:37
  27.4 34.4 %collective-permute-start.1 = (bf16[1024,512]{1,0:T(8,128)(2,1)S(1)}, bf16[1024,512]{1,0:T(8,128)(2,1)}, u32[]{:S(2)}, u32[]{:S(2)}) collective-permute-start(bf16[1024,512]{1,0:T(8,128)(2,1)S(1)} %copy-done.2), channel_id=1, source_target_pairs={{0,64},{64,0},{1,65},{65,1},{2,66},{66,2},{3,67},{67,3},{4,68},{68... | collective-permute-start | bytes 3145736 | tf_op jit(solution)/shard_map/ppermute | solution.py:49
  29.7 12.6 %collective-permute-start.5 = (bf16[128,512]{1,0:T(8,128)(2,1)S(1)}, bf16[128,512]{1,0:T(8,128)(2,1)S(1)}, u32[]{:S(2)}, u32[]{:S(2)}) collective-permute-start(bf16[128,512]{1,0:T(8,128)(2,1)S(1)} %copy-done.8), channel_id=1, source_target_pairs={{0,6},{2,70},{4,2},{6,66},{64,4},{66,68},{68,0},{70,64},{1,7},{3,7... | collective-permute-start | bytes 393224 | tf_op jit(solution)/shard_map/ppermute | solution.py:126
  34.0 25.3 %collective-permute-start.4 = (bf16[128,512]{1,0:T(8,128)(2,1)S(1)}, bf16[128,512]{1,0:T(8,128)(2,1)S(1)}, u32[]{:S(2)}, u32[]{:S(2)}) collective-permute-start(bf16[128,512]{1,0:T(8,128)(2,1)S(1)} %copy-done.8), channel_id=1, source_target_pairs={{0,4},{2,68},{4,0},{6,64},{64,6},{66,70},{68,2},{70,66},{1,5},{3,6... | collective-permute-start | bytes 393224 | tf_op jit(solution)/shard_map/ppermute | solution.py:126
  39.7 22.1 %collective-permute-start.3 = (bf16[128,512]{1,0:T(8,128)(2,1)S(1)}, bf16[128,512]{1,0:T(8,128)(2,1)S(1)}, u32[]{:S(2)}, u32[]{:S(2)}) collective-permute-start(bf16[128,512]{1,0:T(8,128)(2,1)S(1)} %copy-done.8), channel_id=1, source_target_pairs={{0,2},{2,66},{4,6},{6,70},{64,0},{66,64},{68,4},{70,68},{1,3},{3,6... | collective-permute-start | bytes 393224 | tf_op jit(solution)/shard_map/ppermute | solution.py:126
  41.6 20.2 %collective-permute-start.2 = (bf16[128,512]{1,0:T(8,128)(2,1)S(1)}, bf16[128,512]{1,0:T(8,128)(2,1)S(1)}, u32[]{:S(2)}, u32[]{:S(2)}) collective-permute-start(bf16[128,512]{1,0:T(8,128)(2,1)S(1)} %copy-done.8), channel_id=1, source_target_pairs={{0,0},{2,64},{4,4},{6,68},{64,2},{66,66},{68,6},{70,70},{1,1},{3,6... | collective-permute-start | bytes 393224 | tf_op jit(solution)/shard_map/ppermute | solution.py:126
  42.3 27.2 %collective-permute-start.6 = (bf16[1024,512]{1,0:T(8,128)(2,1)S(1)}, bf16[1024,512]{1,0:T(8,128)(2,1)}, u32[]{:S(2)}, u32[]{:S(2)}) collective-permute-start(bf16[1024,512]{1,0:T(8,128)(2,1)S(1)} %copy-done.2), channel_id=1, source_target_pairs={{0,1},{1,0},{2,3},{3,2},{4,5},{5,4},{6,7},{7,6},{8,9},{9,8},{10,11... | collective-permute-start | bytes 3145736 | tf_op jit(solution)/shard_map/ppermute | solution.py:49
  61.8 8.8 %collective-permute-start.7 = (bf16[1024,512]{1,0:T(8,128)(2,1)}, bf16[1024,512]{1,0:T(8,128)(2,1)}, u32[]{:S(2)}, u32[]{:S(2)}) collective-permute-start(bf16[1024,512]{1,0:T(8,128)(2,1)} %collective-permute-done.1.far_ref), channel_id=1, source_target_pairs={{0,1},{1,0},{2,3},{3,2},{4,5},{5,4},{6,7},{7,6},{8,9},{9,8},{10,11... | collective-permute-start | bytes 3145736 | tf_op jit(solution)/shard_map/ppermute | solution.py:49
  70.7 9.1 %collective-permute-start.8 = (f32[48,128]{1,0:T(8,128)S(1)}, f32[48,128]{1,0:T(8,128)S(1)}, u32[]{:S(2)}, u32[]{:S(2)}) collective-permute-start(f32[48,128]{1,0:T(8,128)S(1)} %convert_reduce_fusion.1), channel_id=1, source_target_pairs={{0,64},{64,0},{1,65},{65,1},{2,66},{66,2},{3,67},{67,3},{4,68},{68... | collective-permute-start | bytes 73736 | tf_op jit(solution)/shard_map/ppermute | solution.py:49
  80.6 43.3 %all-to-all-start.1 = ((bf16[32,176,128]{2,1,0:T(8,128)(2,1)}), bf16[32,176,128]{2,1,0:T(8,128)(2,1)S(1)}, u32[]{:S(2)}, u32[]{:S(2)}) async-start(bf16[32,176,128]{2,1,0:T(8,128)(2,1)} %broadcast_dynamic-update-slice_fusion), calls=%async_computation.1 | async-start | bytes 2883584 | tf_op jit(solution)/shard_map/all_to_all | solution.py:37
  91.2 8.8 %collective-permute-start.9 = (bf16[256,512]{1,0:T(8,128)(2,1)S(1)}, bf16[256,512]{1,0:T(8,128)(2,1)S(1)}, u32[]{:S(2)}, u32[]{:S(2)}) collective-permute-start(bf16[256,512]{1,0:T(8,128)(2,1)S(1)} %pad_maximum_fusion.6), channel_id=1, source_target_pairs={{0,64},{64,0},{1,65},{65,1},{2,66},{66,2},{3,67},{67,3},{4,68},{68... | collective-permute-start | bytes 786440 | tf_op jit(solution)/shard_map/ppermute | solution.py:49
  100.8 23.2 %copy-start.6 = (bf16[128,128]{1,0:T(8,128)(2,1)S(1)}, bf16[128,128]{1,0:T(8,128)(2,1)}, u32[]{:S(2)}) copy-start(bf16[128,128]{1,0:T(8,128)(2,1)} %param.6) | copy-start | bytes 98308
  100.9 13.6 %collective-permute-start.10 = (bf16[128,512]{1,0:T(8,128)(2,1)S(1)}, bf16[128,512]{1,0:T(8,128)(2,1)S(1)}, u32[]{:S(2)}, u32[]{:S(2)}) collective-permute-start(bf16[128,512]{1,0:T(8,128)(2,1)S(1)} %get-tuple-element.74), channel_id=1, source_target_pairs={{0,0},{2,64},{4,4},{6,68},{64,2},{66,66},{68,6},{70,70},{1,1},{3,6... | collective-permute-start | bytes 393224 | tf_op jit(solution)/shard_map/ppermute | solution.py:147
  101.5 12.9 %collective-permute-start.13 = (bf16[128,512]{1,0:T(8,128)(2,1)S(1)}, bf16[128,512]{1,0:T(8,128)(2,1)S(1)}, u32[]{:S(2)}, u32[]{:S(2)}) collective-permute-start(bf16[128,512]{1,0:T(8,128)(2,1)S(1)} %get-tuple-element.75), channel_id=1, source_target_pairs={{0,68},{2,4},{4,64},{6,0},{64,70},{66,6},{68,66},{70,2},{1,69},{3,... | collective-permute-start | bytes 393224 | tf_op jit(solution)/shard_map/ppermute | solution.py:147
  107.1 15.5 %collective-permute-start.12 = (bf16[128,512]{1,0:T(8,128)(2,1)S(1)}, bf16[128,512]{1,0:T(8,128)(2,1)S(1)}, u32[]{:S(2)}, u32[]{:S(2)}) collective-permute-start(bf16[128,512]{1,0:T(8,128)(2,1)S(1)} %get-tuple-element.76), channel_id=1, source_target_pairs={{0,4},{2,68},{4,0},{6,64},{64,6},{66,70},{68,2},{70,66},{1,5},{3,6... | collective-permute-start | bytes 393224 | tf_op jit(solution)/shard_map/ppermute | solution.py:147
  112.5 10.8 %collective-permute-start.11 = (bf16[128,512]{1,0:T(8,128)(2,1)S(1)}, bf16[128,512]{1,0:T(8,128)(2,1)S(1)}, u32[]{:S(2)}, u32[]{:S(2)}) collective-permute-start(bf16[128,512]{1,0:T(8,128)(2,1)S(1)} %get-tuple-element.77), channel_id=1, source_target_pairs={{0,64},{2,0},{4,68},{6,4},{64,66},{66,2},{68,70},{70,6},{1,65},{3,... | collective-permute-start | bytes 393224 | tf_op jit(solution)/shard_map/ppermute | solution.py:147
  125.5 14.4 %all-to-all-start.2 = ((bf16[4,512,128]{2,1,0:T(8,128)(2,1)}), bf16[4,512,128]{2,1,0:T(8,128)(2,1)S(1)}, u32[]{:S(2)}, u32[]{:S(2)}) async-start(bf16[4,512,128]{2,1,0:T(8,128)(2,1)} %broadcast_in_dim.8), calls=%async_computation.2 | async-start | bytes 1048576 | tf_op jit(solution)/shard_map/all_to_all | solution.py:37
  130.0 9.9 %copy-start.5 = (bf16[512,512]{1,0:T(8,128)(2,1)S(1)}, bf16[512,512]{1,0:T(8,128)(2,1)}, u32[]{:S(2)}) copy-start(bf16[512,512]{1,0:T(8,128)(2,1)} %pad_maximum_fusion.4) | copy-start | bytes 1572868
  130.1 21.0 %collective-permute-start.14 = (f32[128,128]{0,1:T(8,128)S(1)}, f32[128,128]{0,1:T(8,128)S(1)}, u32[]{:S(2)}, u32[]{:S(2)}) collective-permute-start(f32[128,128]{0,1:T(8,128)S(1)} %copy.32), channel_id=1, source_target_pairs={{0,0},{64,2},{256,4},{320,6},{128,64},{192,66},{384,68},{448,70},{... | collective-permute-start | bytes 196616 | tf_op jit(solution)/shard_map/ppermute | solution.py:160
  140.0 11.1 %copy-start.7 = (bf16[128,256]{1,0:T(8,128)(2,1)S(1)}, bf16[128,256]{1,0:T(8,128)(2,1)}, u32[]{:S(2)}) copy-start(bf16[128,256]{1,0:T(8,128)(2,1)} %param.8) | copy-start | bytes 196612
  140.4 11.5 %collective-permute-start.15 = (bf16[256,640]{1,0:T(8,128)(2,1)S(1)}, bf16[256,640]{1,0:T(8,128)(2,1)S(1)}, u32[]{:S(2)}, u32[]{:S(2)}) collective-permute-start(bf16[256,640]{1,0:T(8,128)(2,1)S(1)} %fusion.7), channel_id=1, source_target_pairs={{0,1},{1,0},{2,3},{3,2},{4,5},{5,4},{6,7},{7,6},{8,9},{9,8},{10,11... | collective-permute-start | bytes 983048 | tf_op jit(solution)/shard_map/ppermute | solution.py:49
  (4 other events, 11.7 us)
